TPU v7x, 128 devices: a whole 4x4x4 slice. The times are simulated.
128 devices in a mesh: prow: 8 (over y, core), pcol: 16 (over z, x).
Axes of the slice: x: 4, y: 4, z: 4, core: 2. Of those that a mesh axis runs over, the one named last changes fastest.
Arguments:
- right_side: float32 [120, 262144], P(None, ('prow', 'pcol')), may hold values from -6 to 6
- part_count: int32 [128], P(('prow', 'pcol')), may hold values from 1024 to 2048, as said below
- elem_class: int32 [262144], P(('prow', 'pcol')), may hold values from 0 to 255
- face_link: int32 [1048576], P(('prow', 'pcol')), may hold values from -1 to 11263, as said below
- face_orient: int32 [1048576], P(('prow', 'pcol')), may hold values from 0 to 5
- face_normal: float32 [3, 1048576], P(None, ('prow', 'pcol')), may hold values from -1 to 1, as said below
- boundary_metric_quotient: float32 [1048576], P(('prow', 'pcol')), may hold values from 0.5 to 2
- bound_face: int32 [128, 8, 384], P(('prow', 'pcol')), may hold values from -1 to 8191, as said below
- lift: float32 [4, 20, 10], replicated, may hold values from -2.5 to 2.5
- inverse_table: bfloat16 [256, 120, 120], replicated
Outputs:
- basis: float32 [3, 120, 262144], P(None, None, ('prow', 'pcol'))
- hess: float32 [3, 2], replicated
Inputs may be any that keep to these rules, and one draw needn't show every extreme that they name: Partition p's live elements take its first part_count[p] slots; one partition is full. `bound_face`: slots of list k of a partition hold faces s * 2048 + e of its live elements (repeats possible); -1 marks an empty slot and empty slots follow the filled ones; lists toward directions outside the grid are empty, every other list fills at least half of its 384 slots, and one partition fills all slots of those lists. `face_link`: a code q in 0 to 3071 names filled slot q % 384 of list 7 - q // 384 of the partition at the offset of direction q // 384, which exists; each filled slot of a list toward a partition is named by exactly one face of that partition; q >= 3072 names a face of a live element of the same partition; -1 is the physical boundary; all faces of empty element slots are -1. `face_normal`: unit vectors.
All inputs are finite; a program needn't handle non-finite values.
Results may differ from a plain program's by a relative error of at most 0.003.
Values sent between devices are 32-bit elements; how exact they have to be, the bound alone decides.
A program may use at most 128 MiB of HBM per device.

v0:
```python
import jax
import jax.numpy as jnp
import numpy as np
from jax import lax
from jax.sharding import PartitionSpec as P

EPSILON = 1e-06
PERMUTATIONS = ((0, 1, 2), (0, 2, 1), (1, 0, 2), (1, 2, 0), (2, 0, 1), (2, 1, 0))
OFFSETS = tuple(((direction // 3 - 1, direction % 3 - 1) for direction in (0, 1, 2, 3, 5, 6, 7, 8)))


def passed_along(value, axis, steps):
    count = lax.axis_size(axis)
    leading, last = (max(0, -steps), min(count, count - steps))
    return lax.ppermute(value, axis, [(source, source + steps) for source in range(leading, last)])


def trace_tables():
    element_points = [
        (coord_a, coord_b, coord_c, 3 - coord_a - coord_b - coord_c)
        for coord_a in range(4)
        for coord_b in range(4 - coord_a)
        for coord_c in range(4 - coord_a - coord_b)
    ]
    face_points = [
        (coord_a, coord_b, 3 - coord_a - coord_b)
        for coord_a in range(4)
        for coord_b in range(4 - coord_a)
    ]
    select_rows = []
    for opposite in range(4):
        corners = [vertex for vertex in range(4) if vertex != opposite]
        members = []
        for triple in face_points:
            coords = [0, 0, 0, 0]
            for position in range(3):
                coords[corners[position]] = triple[position]
            members.append(element_points.index(tuple(coords)))
        select_rows.append(
            [component * 20 + members[position] for component in range(6) for position in range(10)]
        )
    turn_rows = [
        [
            face_points.index((triple[sigma_row[0]], triple[sigma_row[1]], triple[sigma_row[2]]))
            for triple in face_points
        ]
        for sigma_row in PERMUTATIONS
    ]
    return (np.array(select_rows, np.int32), np.array(turn_rows, np.int32))


def turn_matrices(turn_rows):
    tables = np.zeros((6, 10, 10), np.float32)
    for option in range(6):
        for position in range(10):
            tables[option, position, turn_rows[option][position]] = 1.0
    return tables


def cross_with(normal, field_part):
    return jnp.stack(
        [
            normal[1] * field_part[2] - normal[2] * field_part[1],
            normal[2] * field_part[0] - normal[0] * field_part[2],
            normal[0] * field_part[1] - normal[1] * field_part[0],
        ]
    )


def upwind_flux(neighbour, normal, scaling):
    fields = neighbour.reshape(6, 10, -1)
    electric = fields[:3]
    magnetic = fields[3:]
    outward = normal[:, None, :]
    along_electric = jnp.sum(outward * electric, axis=0)
    along_magnetic = jnp.sum(outward * magnetic, axis=0)
    flux_electric = electric - outward * along_electric - cross_with(outward, magnetic)
    flux_magnetic = magnetic - outward * along_magnetic + cross_with(outward, electric)
    return 0.5 * scaling * jnp.concatenate([flux_electric, flux_magnetic], axis=0)


def neighbour_traces(own_traces, incoming_boundary_values, links, turns, turn_tables):
    extended = jnp.concatenate([incoming_boundary_values, own_traces], axis=1)
    picked = jnp.take(extended, jnp.maximum(links, 0), axis=1)
    mirror = jnp.concatenate([-own_traces[:30], own_traces[30:]], axis=0)
    picked = jnp.where(links[None, :] < 0, mirror, picked)
    shaped = picked.reshape(6, 10, -1)
    turned = jnp.zeros_like(shaped)
    for option in range(6):
        rotated = jnp.einsum(
            "jk,ckf->cjf", turn_tables[option], shaped, precision=lax.Precision.HIGHEST
        )
        turned = turned + jnp.where(turns[None, None, :] == option, rotated, 0.0)
    return turned.reshape(60, -1)


def lift_faces(flux, lift):
    grouped = flux.reshape(6, 10, 4, -1)
    return jnp.einsum("fij,cjfe->cie", lift, grouped, precision=lax.Precision.HIGHEST).reshape(
        120, -1
    )


def precondition(coupled, cell_categories, inverse_table):
    unknowns, elements = coupled.shape
    block_size = min(256, elements)
    block_count = elements // block_size

    def one_block(block_index, result):
        first_col = block_index * block_size
        block_class = lax.dynamic_slice_in_dim(cell_categories, first_col, block_size)
        columns = lax.dynamic_slice_in_dim(coupled, first_col, block_size, 1)
        gathered = jnp.take(inverse_table, block_class, axis=0)
        product = jnp.einsum("eij,je->ie", gathered, columns, preferred_element_type=jnp.float32)
        return lax.dynamic_update_slice_in_dim(result, product, first_col, 1)

    empty = jnp.zeros((unknowns, elements), jnp.float32)
    return lax.fori_loop(0, block_count, one_block, empty)


def route_lists(outgoing):
    arrived = [None] * 8
    for index in range(8):
        row_step, col_step = OFFSETS[index]
        value = outgoing[:, 7 - index]
        if row_step != 0:
            value = passed_along(value, "prow", -row_step)
        if col_step != 0:
            value = passed_along(value, "pcol", -col_step)
        arrived[index] = value
    return jnp.stack(arrived, axis=1)


def shards(
    right_side,
    part_count,
    elem_class,
    face_link,
    face_orient,
    face_normal,
    boundary_metric_quotient,
    bound_face,
    lift,
    inverse_table,
):
    unknowns, elements = right_side.shape
    all_subdomains = lax.axis_size("prow") * lax.axis_size("pcol")
    weight = 1.0 / (unknowns * elements * all_subdomains)
    select_rows, turn_rows = trace_tables()
    trace_index = select_rows.T.reshape(-1)
    turn_tables = turn_matrices(turn_rows)
    live_cell_flags = (jnp.arange(elements) < part_count[0]).astype(jnp.float32)[None, :]
    lists = bound_face[0]
    list_slots = lists.shape[1]
    flat_lists = lists.reshape(-1)
    list_mask = (flat_lists >= 0)[None, :].astype(jnp.float32)

    def local_inner(left_vec, right_vec):
        return jnp.sum(left_vec * right_vec) * weight

    first_vec = right_side * live_cell_flags
    scale_now = jnp.sqrt(lax.psum(local_inner(first_vec, first_vec), ("prow", "pcol")) + EPSILON)
    pending = first_vec
    basis_list = []
    columns = []
    for step_index in range(2):
        current = pending / scale_now
        own_traces = current[trace_index].reshape(60, 4 * elements)
        outgoing = (jnp.take(own_traces, jnp.maximum(flat_lists, 0), axis=1) * list_mask).reshape(
            60, 8, list_slots
        )
        incoming_boundary_values = route_lists(outgoing).reshape(60, 8 * list_slots)
        neighbour = neighbour_traces(
            own_traces, incoming_boundary_values, face_link, face_orient, turn_tables
        )
        coupled = lift_faces(upwind_flux(neighbour, face_normal, boundary_metric_quotient), lift)
        basis_list.append(current)
        applied = precondition(coupled.astype(jnp.bfloat16), elem_class, inverse_table)
        image_vec = current + live_cell_flags * applied
        local_dots = jnp.stack([local_inner(earlier, image_vec) for earlier in basis_list])
        coefficients = lax.psum(local_dots, ("prow", "pcol"))
        remainder = image_vec
        for earlier_index in range(len(basis_list)):
            remainder = remainder - coefficients[earlier_index] * basis_list[earlier_index]
        scale_now = jnp.sqrt(
            lax.psum(local_inner(remainder, remainder), ("prow", "pcol")) + EPSILON
        )
        columns.append((coefficients, scale_now))
        pending = remainder
    basis_list.append(pending / scale_now)
    first_col, second_col = columns
    zero_entry = jnp.zeros((), jnp.float32)
    hess = jnp.stack(
        [
            jnp.stack([first_col[0][0], second_col[0][0]]),
            jnp.stack([first_col[1], second_col[0][1]]),
            jnp.stack([zero_entry, second_col[1]]),
        ]
    )
    return (jnp.stack(basis_list), hess)


def solution(mesh):
    in_specs = (
        P(None, ("prow", "pcol")),
        P(("prow", "pcol")),
        P(("prow", "pcol")),
        P(("prow", "pcol")),
        P(("prow", "pcol")),
        P(None, ("prow", "pcol")),
        P(("prow", "pcol")),
        P(("prow", "pcol"), None, None),
        P(),
        P(),
    )
    out_specs = (P(None, None, ("prow", "pcol")), P())
    return jax.shard_map(shards, mesh=mesh, in_specs=in_specs, out_specs=out_specs, check_vma=False)
```

profile of v0, /device:TPU:1, one launch (start us, length us, event | category | flops | bytes accessed | tf_op | source)
XLA Modules:
  0.0 1041.2 jit_solution(17453391662893369224)
XLA Ops:
  5.5 68.7 %psum.35 = f32[]{:T(128)} all-reduce(f32[]{:T(128)S(6)} %mul.189), channel_id=1, replica_groups=mesh['prow'=8,'pcol'=16] {'prow','pcol'}, use_global_device_ids=true, to_apply=%region_1.0 | all-reduce | flops 1 | bytes 8 | tf_op jit(solution)/shard_map/psum | solution.py:162
  84.4 13.1 %gather_fusion.4 = f32[3072,60]{1,0:T(8,128)} fusion(f32[60,8192]{0,1:T(8,128)} %copy.75, s32[3072]{0:T(1024)S(1)} %fusion.38), kind=kCustom, calls=%fused_computation.clone | custom fusion | bytes 1486848 | tf_op jit(solution)/shard_map/jit(_take)/gather | solution.py:169
  147.7 10.7 %copy.91 = bf16[256,120,120]{2,1,0:T(8,128)(2,1)} copy(bf16[256,120,120]{0,2,1:T(8,128)(2,1)} %param.44) | data formatting | bytes 14745600 | tf_op jit(solution)/shard_map/while | solution.py:118
  167.2 30.5 %gather_fusion.5 = f32[8192,60]{1,0:T(8,128)} fusion(f32[60,11264]{0,1:T(8,128)} %pad_maximum_fusion, s32[8192]{0:T(1024)S(1)} %maximum_clamp_fusion), kind=kCustom, calls=%fused_computation.1.clone | custom fusion | bytes 3964928 | tf_op jit(solution)/shard_map/jit(_take)/gather | solution.py:84
  197.8 7.5 maximum_select_fusion
  242.0 167.4 %while.26 = (s32[]{:T(128)}, f32[120,2048]{1,0:T(8,128)S(1)}, bf16[120,2048]{1,0:T(8,128)(2,1)S(1)}, s32[2048]{0:T(1024)}, bf16[256,120,120]{2,1,0:T(8,128)(2,1)...) while((s32[]{:T(128)}, f32[120,2048]{1,0:T(8,128)S(1)}, bf16[120,2048]{1,0:T(8,128)(2,1)S(1)}, ...), condition=%wide.region_5.9_spmd, body=%wide.region_4.8_spmd.sunk | while | flops 14748166 | bytes 23294616 | solution.py:118
  242.9 11.9 %gather_fusion = bf16[256,120,120]{2,1,0:T(8,128)(2,1)} fusion(bf16[256,120,120]{2,1,0:T(8,128)(2,1)} %get-tuple-element.404, s32[1024]{0:T(1024)S(1)} %pad_clamp_fusion.5), kind=kCustom, calls=%fused_computation.2.clone.clone.1 | custom fusion | bytes 14746624 | tf_op jit(solution)/shard_map/while/body/eval_jaxpr/jit(_take)/gather | solution.py:113
  254.9 7.9 multiply_reduce_fusion.14
  263.8 11.9 %gather_fusion = bf16[256,120,120]{2,1,0:T(8,128)(2,1)} fusion(bf16[256,120,120]{2,1,0:T(8,128)(2,1)} %get-tuple-element.404, s32[1024]{0:T(1024)S(1)} %pad_clamp_fusion.5), kind=kCustom, calls=%fused_computation.2.clone.clone.1 | custom fusion | bytes 14746624 | tf_op jit(solution)/shard_map/while/body/eval_jaxpr/jit(_take)/gather | solution.py:113
  275.8 7.9 multiply_reduce_fusion.14
  284.7 12.0 %gather_fusion = bf16[256,120,120]{2,1,0:T(8,128)(2,1)} fusion(bf16[256,120,120]{2,1,0:T(8,128)(2,1)} %get-tuple-element.404, s32[1024]{0:T(1024)S(1)} %pad_clamp_fusion.5), kind=kCustom, calls=%fused_computation.2.clone.clone.1 | custom fusion | bytes 14746624 | tf_op jit(solution)/shard_map/while/body/eval_jaxpr/jit(_take)/gather | solution.py:113
  296.7 7.9 multiply_reduce_fusion.14
  305.6 12.0 %gather_fusion = bf16[256,120,120]{2,1,0:T(8,128)(2,1)} fusion(bf16[256,120,120]{2,1,0:T(8,128)(2,1)} %get-tuple-element.404, s32[1024]{0:T(1024)S(1)} %pad_clamp_fusion.5), kind=kCustom, calls=%fused_computation.2.clone.clone.1 | custom fusion | bytes 14746624 | tf_op jit(solution)/shard_map/while/body/eval_jaxpr/jit(_take)/gather | solution.py:113
  317.6 7.9 multiply_reduce_fusion.14
  326.5 11.9 %gather_fusion = bf16[256,120,120]{2,1,0:T(8,128)(2,1)} fusion(bf16[256,120,120]{2,1,0:T(8,128)(2,1)} %get-tuple-element.404, s32[1024]{0:T(1024)S(1)} %pad_clamp_fusion.5), kind=kCustom, calls=%fused_computation.2.clone.clone.1 | custom fusion | bytes 14746624 | tf_op jit(solution)/shard_map/while/body/eval_jaxpr/jit(_take)/gather | solution.py:113
  338.5 7.9 multiply_reduce_fusion.14
  347.4 12.0 %gather_fusion = bf16[256,120,120]{2,1,0:T(8,128)(2,1)} fusion(bf16[256,120,120]{2,1,0:T(8,128)(2,1)} %get-tuple-element.404, s32[1024]{0:T(1024)S(1)} %pad_clamp_fusion.5), kind=kCustom, calls=%fused_computation.2.clone.clone.1 | custom fusion | bytes 14746624 | tf_op jit(solution)/shard_map/while/body/eval_jaxpr/jit(_take)/gather | solution.py:113
  359.5 7.9 multiply_reduce_fusion.14
  368.3 12.0 %gather_fusion = bf16[256,120,120]{2,1,0:T(8,128)(2,1)} fusion(bf16[256,120,120]{2,1,0:T(8,128)(2,1)} %get-tuple-element.404, s32[1024]{0:T(1024)S(1)} %pad_clamp_fusion.5), kind=kCustom, calls=%fused_computation.2.clone.clone.1 | custom fusion | bytes 14746624 | tf_op jit(solution)/shard_map/while/body/eval_jaxpr/jit(_take)/gather | solution.py:113
  380.4 7.9 multiply_reduce_fusion.14
  389.2 11.9 %gather_fusion = bf16[256,120,120]{2,1,0:T(8,128)(2,1)} fusion(bf16[256,120,120]{2,1,0:T(8,128)(2,1)} %get-tuple-element.404, s32[1024]{0:T(1024)S(1)} %pad_clamp_fusion.5), kind=kCustom, calls=%fused_computation.2.clone.clone.1 | custom fusion | bytes 14746624 | tf_op jit(solution)/shard_map/while/body/eval_jaxpr/jit(_take)/gather | solution.py:113
  401.3 7.9 multiply_reduce_fusion.14
  410.9 71.9 %psum.36 = f32[1]{0:T(128)} all-reduce(f32[1]{0:T(128)} %bitcast.34), channel_id=1, replica_groups=mesh['prow'=8,'pcol'=16] {'prow','pcol'}, use_global_device_ids=true, to_apply=%region_7.11 | all-reduce | flops 1 | bytes 8 | tf_op jit(solution)/shard_map/psum | solution.py:181
  484.9 63.2 %psum.37 = f32[]{:T(128)} all-reduce(f32[]{:T(128)S(6)} %mul.415), channel_id=1, replica_groups=mesh['prow'=8,'pcol'=16] {'prow','pcol'}, use_global_device_ids=true, to_apply=%region_9.13 | all-reduce | flops 1 | bytes 8 | tf_op jit(solution)/shard_map/psum | solution.py:186
  559.5 11.8 %gather_fusion.6 = f32[3072,60]{1,0:T(8,128)S(1)} fusion(f32[60,8192]{0,1:T(8,128)} %copy.94, s32[3072]{0:T(1024)} %copy-done.17), kind=kCustom, calls=%fused_computation.3.clone | custom fusion | bytes 1486848 | tf_op jit(solution)/shard_map/jit(_take)/gather | solution.py:169
  600.9 4.6 collective-permute-start.20
  630.2 33.2 %gather_fusion.7 = f32[8192,60]{1,0:T(8,128)} fusion(f32[60,11264]{0,1:T(8,128)} %pad_maximum_fusion.1, s32[8192]{0:T(1024)} %copy-done.6), kind=kCustom, calls=%fused_computation.4.clone | custom fusion | bytes 3964928 | tf_op jit(solution)/shard_map/jit(_take)/gather | solution.py:84
  663.4 7.5 maximum_select_fusion.1
  678.3 5.1 convolution_select_fusion.5
  716.4 173.9 %while.27 = (s32[]{:T(128)}, f32[120,2048]{1,0:T(8,128)S(1)}, bf16[120,2048]{1,0:T(8,128)(2,1)}, s32[2048]{0:T(1024)}, bf16[256,120,120]{2,1,0:T(8,128)(2,1)}, /*index=5*/s32[]{:T(128)}, s32[]{:T(128)}, s32[]{:T(128)}, s32[]{:T(128)}) while((s32[]{:T(128)}, f32[120,2048]{1,0:T(8,128)S(1)}, bf16[120,2048]{1,0:T(8,128)(2,1)}, ...), condition=%wide.region_13.17_spmd, body=%wide.region_12.16_spmd.sunk | while | flops 14748166 | bytes 23294616 | solution.py:118
  717.2 11.9 %gather_fusion.1 = bf16[256,120,120]{2,1,0:T(8,128)(2,1)} fusion(bf16[256,120,120]{2,1,0:T(8,128)(2,1)} %get-tuple-element.431, s32[1024]{0:T(1024)S(1)} %pad_clamp_fusion.6), kind=kCustom, calls=%fused_computation.5.clone.clone.1 | custom fusion | bytes 14746624 | tf_op jit(solution)/shard_map/while/body/eval_jaxpr/jit(_take)/gather | solution.py:113
  730.1 7.9 multiply_reduce_fusion.15
  738.9 11.9 %gather_fusion.1 = bf16[256,120,120]{2,1,0:T(8,128)(2,1)} fusion(bf16[256,120,120]{2,1,0:T(8,128)(2,1)} %get-tuple-element.431, s32[1024]{0:T(1024)S(1)} %pad_clamp_fusion.6), kind=kCustom, calls=%fused_computation.5.clone.clone.1 | custom fusion | bytes 14746624 | tf_op jit(solution)/shard_map/while/body/eval_jaxpr/jit(_take)/gather | solution.py:113
  751.8 7.9 multiply_reduce_fusion.15
  760.7 12.0 %gather_fusion.1 = bf16[256,120,120]{2,1,0:T(8,128)(2,1)} fusion(bf16[256,120,120]{2,1,0:T(8,128)(2,1)} %get-tuple-element.431, s32[1024]{0:T(1024)S(1)} %pad_clamp_fusion.6), kind=kCustom, calls=%fused_computation.5.clone.clone.1 | custom fusion | bytes 14746624 | tf_op jit(solution)/shard_map/while/body/eval_jaxpr/jit(_take)/gather | solution.py:113
  773.5 7.9 multiply_reduce_fusion.15
  782.4 12.0 %gather_fusion.1 = bf16[256,120,120]{2,1,0:T(8,128)(2,1)} fusion(bf16[256,120,120]{2,1,0:T(8,128)(2,1)} %get-tuple-element.431, s32[1024]{0:T(1024)S(1)} %pad_clamp_fusion.6), kind=kCustom, calls=%fused_computation.5.clone.clone.1 | custom fusion | bytes 14746624 | tf_op jit(solution)/shard_map/while/body/eval_jaxpr/jit(_take)/gather | solution.py:113
  795.3 7.9 multiply_reduce_fusion.15
  804.1 11.9 %gather_fusion.1 = bf16[256,120,120]{2,1,0:T(8,128)(2,1)} fusion(bf16[256,120,120]{2,1,0:T(8,128)(2,1)} %get-tuple-element.431, s32[1024]{0:T(1024)S(1)} %pad_clamp_fusion.6), kind=kCustom, calls=%fused_computation.5.clone.clone.1 | custom fusion | bytes 14746624 | tf_op jit(solution)/shard_map/while/body/eval_jaxpr/jit(_take)/gather | solution.py:113
  817.0 7.9 multiply_reduce_fusion.15
  825.9 12.0 %gather_fusion.1 = bf16[256,120,120]{2,1,0:T(8,128)(2,1)} fusion(bf16[256,120,120]{2,1,0:T(8,128)(2,1)} %get-tuple-element.431, s32[1024]{0:T(1024)S(1)} %pad_clamp_fusion.6), kind=kCustom, calls=%fused_computation.5.clone.clone.1 | custom fusion | bytes 14746624 | tf_op jit(solution)/shard_map/while/body/eval_jaxpr/jit(_take)/gather | solution.py:113
  838.8 7.9 multiply_reduce_fusion.15
  847.6 12.0 %gather_fusion.1 = bf16[256,120,120]{2,1,0:T(8,128)(2,1)} fusion(bf16[256,120,120]{2,1,0:T(8,128)(2,1)} %get-tuple-element.431, s32[1024]{0:T(1024)S(1)} %pad_clamp_fusion.6), kind=kCustom, calls=%fused_computation.5.clone.clone.1 | custom fusion | bytes 14746624 | tf_op jit(solution)/shard_map/while/body/eval_jaxpr/jit(_take)/gather | solution.py:113
  860.5 7.9 multiply_reduce_fusion.15
  869.4 11.9 %gather_fusion.1 = bf16[256,120,120]{2,1,0:T(8,128)(2,1)} fusion(bf16[256,120,120]{2,1,0:T(8,128)(2,1)} %get-tuple-element.431, s32[1024]{0:T(1024)S(1)} %pad_clamp_fusion.6), kind=kCustom, calls=%fused_computation.5.clone.clone.1 | custom fusion | bytes 14746624 | tf_op jit(solution)/shard_map/while/body/eval_jaxpr/jit(_take)/gather | solution.py:113
  882.2 7.9 multiply_reduce_fusion.15
  893.8 71.9 %psum.38 = f32[2]{0:T(128)S(1)} all-reduce(f32[2]{0:T(128)S(1)} %pad_maximum_fusion.6), channel_id=1, replica_groups=mesh['prow'=8,'pcol'=16] {'prow','pcol'}, use_global_device_ids=true, to_apply=%region_16.20 | all-reduce | flops 2 | bytes 16 | tf_op jit(solution)/shard_map/psum | solution.py:181
  972.1 63.1 %psum.39 = f32[]{:T(128)} all-reduce(f32[]{:T(128)S(6)} %mul.446), channel_id=1, replica_groups=mesh['prow'=8,'pcol'=16] {'prow','pcol'}, use_global_device_ids=true, to_apply=%region_18.22 | all-reduce | flops 1 | bytes 8 | tf_op jit(solution)/shard_map/psum | solution.py:186
  (364 shorter events, 250.8 us)
Async XLA Ops:
  2.7 81.6 %copy-start.17 = (s32[3072]{0:T(1024)}, s32[3072]{0:T(1024)S(1)}, u32[]{:S(2)}) copy-start(s32[3072]{0:T(1024)S(1)} %fusion.38) | copy-start | bytes 36868
  5.5 92.0 %copy-start.47 = (pred[3072]{0:T(1024)(128)(4,1)}, pred[3072]{0:T(1024)(128)(4,1)S(1)}, u32[]{:S(2)}) copy-start(pred[3072]{0:T(1024)(128)(4,1)S(1)} %compare_and_fusion.2) | copy-start | bytes 9220
  84.4 13.1 %copy-start.16 = (f32[3072]{0:T(1024)}, f32[3072]{0:T(1024)S(1)}, u32[]{:S(2)}) copy-start(f32[3072]{0:T(1024)S(1)} %reshape.258) | copy-start | bytes 36868
  101.0 18.1 %copy-start.46 = (s32[8192]{0:T(1024)S(1)}, s32[8192]{0:T(1024)}, u32[]{:S(2)}) copy-start(s32[8192]{0:T(1024)} %param.39) | copy-start | bytes 98308
  101.0 18.7 %copy-start.4 = (f32[3,8192]{1,0:T(4,128)S(1)}, f32[3,8192]{1,0:T(4,128)}, u32[]{:S(2)}) copy-start(f32[3,8192]{1,0:T(4,128)} %param.40) | copy-start | bytes 294916
  102.8 18.7 %collective-permute-start = (f32[60,384]{1,0:T(8,128)}, f32[60,384]{1,0:T(8,128)}, u32[]{:S(2)}, u32[]{:S(2)}) collective-permute-start(f32[60,384]{1,0:T(8,128)} %bitcast.151), channel_id=1, source_target_pairs={{0,16},{16,32},{32,48},{48,64},{64,80},{80,96},{96,112},{1,17},{17... | collective-permute-start | bytes 276488 | tf_op jit(solution)/shard_map/ppermute | solution.py:15
  106.0 33.4 %copy-start.15 = (s32[8192]{0:T(1024)S(1)}, s32[8192]{0:T(1024)}, u32[]{:S(2)}) copy-start(s32[8192]{0:T(1024)} %param.38) | copy-start | bytes 98308
  106.0 17.5 %collective-permute-start.3 = (f32[60,384]{1,0:T(8,128)}, f32[60,384]{1,0:T(8,128)}, u32[]{:S(2)}, u32[]{:S(2)}) collective-permute-start(f32[60,384]{1,0:T(8,128)} %bitcast.150), channel_id=1, source_target_pairs={{0,16},{16,32},{32,48},{48,64},{64,80},{80,96},{96,112},{1,17},{17... | collective-permute-start | bytes 276488 | tf_op jit(solution)/shard_map/ppermute | solution.py:15
  108.9 16.9 %collective-permute-start.7 = (f32[60,384]{1,0:T(8,128)}, f32[60,384]{1,0:T(8,128)}, u32[]{:S(2)}, u32[]{:S(2)}) collective-permute-start(f32[60,384]{1,0:T(8,128)} %bitcast.15), channel_id=1, source_target_pairs={{16,0},{32,16},{48,32},{64,48},{80,64},{96,80},{112,96},{17,1},{33... | collective-permute-start | bytes 276488 | tf_op jit(solution)/shard_map/ppermute | solution.py:15
  112.0 15.7 %collective-permute-start.10 = (f32[60,384]{1,0:T(8,128)S(1)}, f32[60,384]{1,0:T(8,128)}, u32[]{:S(2)}, u32[]{:S(2)}) collective-permute-start(f32[60,384]{1,0:T(8,128)S(1)} %bitcast.147), channel_id=1, source_target_pairs={{16,0},{32,16},{48,32},{64,48},{80,64},{96,80},{112,96},{17,1},{33... | collective-permute-start | bytes 276488 | tf_op jit(solution)/shard_map/ppermute | solution.py:15
  114.1 17.6 %collective-permute-start.2 = (f32[60,384]{1,0:T(8,128)S(1)}, f32[60,384]{1,0:T(8,128)S(1)}, u32[]{:S(2)}, u32[]{:S(2)}) collective-permute-start(f32[60,384]{1,0:T(8,128)S(1)} %bitcast.146), channel_id=1, source_target_pairs={{0,16},{16,32},{32,48},{48,64},{64,80},{80,96},{96,112},{1,17},{17... | collective-permute-start | bytes 276488 | tf_op jit(solution)/shard_map/ppermute | solution.py:15
  120.4 111.5 %copy-start.7 = (f32[1,8192]{1,0:T(1,128)}, f32[1,8192]{1,0:T(1,128)S(1)}, u32[]{:S(2)}) copy-start(f32[1,8192]{1,0:T(1,128)S(1)} %get-tuple-element.297) | copy-start | bytes 98308
  120.5 111.5 %copy-start.9 = (f32[1,8192]{1,0:T(1,128)}, f32[1,8192]{1,0:T(1,128)S(1)}, u32[]{:S(2)}) copy-start(f32[1,8192]{1,0:T(1,128)S(1)} %get-tuple-element.298) | copy-start | bytes 98308
  121.2 46.0 %copy-start.6 = (s32[8192]{0:T(1024)}, s32[8192]{0:T(1024)S(1)}, u32[]{:S(2)}) copy-start(s32[8192]{0:T(1024)S(1)} %maximum_clamp_fusion) | copy-start | bytes 98308
  121.5 11.5 %collective-permute-start.5 = (f32[60,384]{1,0:T(8,128)S(1)}, f32[60,384]{1,0:T(8,128)S(1)}, u32[]{:S(2)}, u32[]{:S(2)}) collective-permute-start(f32[60,384]{1,0:T(8,128)S(1)} %bitcast.152), channel_id=1, source_target_pairs={{0,1},{1,2},{2,3},{3,4},{4,5},{5,6},{6,7},{7,8},{8,9},{9,10},{10,1... | collective-permute-start | bytes 276488 | tf_op jit(solution)/shard_map/ppermute | solution.py:15
  123.6 14.1 %collective-permute-start.6 = (f32[60,384]{1,0:T(8,128)S(1)}, f32[60,384]{1,0:T(8,128)S(1)}, u32[]{:S(2)}, u32[]{:S(2)}) collective-permute-start(f32[60,384]{1,0:T(8,128)S(1)} %bitcast.148), channel_id=1, source_target_pairs={{1,0},{2,1},{3,2},{4,3},{5,4},{6,5},{7,6},{8,7},{9,8},{10,9},{11,1... | collective-permute-start | bytes 276488 | tf_op jit(solution)/shard_map/ppermute | solution.py:15
  125.8 32.9 %collective-permute-start.9 = (f32[60,384]{1,0:T(8,128)S(1)}, f32[60,384]{1,0:T(8,128)S(1)}, u32[]{:S(2)}, u32[]{:S(2)}) collective-permute-start(f32[60,384]{1,0:T(8,128)S(1)} %bitcast.145), channel_id=1, source_target_pairs={{16,0},{32,16},{48,32},{64,48},{80,64},{96,80},{112,96},{17,1},{33... | collective-permute-start | bytes 276488 | tf_op jit(solution)/shard_map/ppermute | solution.py:15
  127.7 31.1 %collective-permute-start.1 = (f32[60,384]{1,0:T(8,128)}, f32[60,384]{1,0:T(8,128)S(1)}, u32[]{:S(2)}, u32[]{:S(2)}) collective-permute-start(f32[60,384]{1,0:T(8,128)} %collective-permute-done), channel_id=1, source_target_pairs={{0,1},{1,2},{2,3},{3,4},{4,5},{5,6},{6,7},{7,8},{8,9},{9,10},{10,1... | collective-permute-start | bytes 276488 | tf_op jit(solution)/shard_map/ppermute | solution.py:15
  131.7 12.2 %copy-start.18 = (f32[60,384]{1,0:T(8,128)}, f32[60,384]{1,0:T(8,128)S(1)}, u32[]{:S(2)}) copy-start(f32[60,384]{1,0:T(8,128)S(1)} %collective-permute-done.2) | copy-start | bytes 276484
  131.7 27.1 %collective-permute-start.4 = (f32[60,384]{1,0:T(8,128)}, f32[60,384]{1,0:T(8,128)S(1)}, u32[]{:S(2)}, u32[]{:S(2)}) collective-permute-start(f32[60,384]{1,0:T(8,128)} %collective-permute-done.3), channel_id=1, source_target_pairs={{1,0},{2,1},{3,2},{4,3},{5,4},{6,5},{7,6},{8,7},{9,8},{10,9},{11,1... | collective-permute-start | bytes 276488 | tf_op jit(solution)/shard_map/ppermute | solution.py:15
  133.0 25.9 %collective-permute-start.8 = (f32[60,384]{1,0:T(8,128)}, f32[60,384]{1,0:T(8,128)}, u32[]{:S(2)}, u32[]{:S(2)}) collective-permute-start(f32[60,384]{1,0:T(8,128)} %collective-permute-done.7), channel_id=1, source_target_pairs={{0,1},{1,2},{2,3},{3,4},{4,5},{5,6},{6,7},{7,8},{8,9},{9,10},{10,1... | collective-permute-start | bytes 276488 | tf_op jit(solution)/shard_map/ppermute | solution.py:15
  137.7 22.2 %collective-permute-start.11 = (f32[60,384]{1,0:T(8,128)}, f32[60,384]{1,0:T(8,128)}, u32[]{:S(2)}, u32[]{:S(2)}) collective-permute-start(f32[60,384]{1,0:T(8,128)} %collective-permute-done.10), channel_id=1, source_target_pairs={{1,0},{2,1},{3,2},{4,3},{5,4},{6,5},{7,6},{8,7},{9,8},{10,9},{11,1... | collective-permute-start | bytes 276488 | tf_op jit(solution)/shard_map/ppermute | solution.py:15
  139.4 58.3 %copy-start.20 = (pred[8192]{0:T(1024)(128)(4,1)}, pred[8192]{0:T(1024)(128)(4,1)S(1)}, u32[]{:S(2)}) copy-start(pred[8192]{0:T(1024)(128)(4,1)S(1)} %get-tuple-element.307) | copy-start | bytes 24580
  139.5 4.5 copy-start.2
  147.7 10.7 %copy-start.19 = (f32[60,384]{1,0:T(8,128)S(1)}, f32[60,384]{1,0:T(8,128)}, u32[]{:S(2)}) copy-start(f32[60,384]{1,0:T(8,128)} %copy-done.18) | copy-start | bytes 276484
  221.1 3.7 copy-start.24
  221.1 3.7 copy-start.36
  242.0 167.4 %copy-start.1 = (f32[120,2048]{1,0:T(8,128)S(1)}, f32[120,2048]{1,0:T(8,128)}, u32[]{:S(2)}) copy-start(f32[120,2048]{1,0:T(8,128)} %param.35) | copy-start | bytes 2949124
  575.1 14.6 %collective-permute-start.12 = (f32[60,384]{1,0:T(8,128)}, f32[60,384]{1,0:T(8,128)}, u32[]{:S(2)}, u32[]{:S(2)}) collective-permute-start(f32[60,384]{1,0:T(8,128)} %bitcast.157), channel_id=1, source_target_pairs={{0,16},{16,32},{32,48},{48,64},{64,80},{80,96},{96,112},{1,17},{17... | collective-permute-start | bytes 276488 | tf_op jit(solution)/shard_map/ppermute | solution.py:15
  579.1 11.8 %collective-permute-start.15 = (f32[60,384]{1,0:T(8,128)}, f32[60,384]{1,0:T(8,128)S(1)}, u32[]{:S(2)}, u32[]{:S(2)}) collective-permute-start(f32[60,384]{1,0:T(8,128)} %bitcast.41), channel_id=1, source_target_pairs={{0,16},{16,32},{32,48},{48,64},{64,80},{80,96},{96,112},{1,17},{17... | collective-permute-start | bytes 276488 | tf_op jit(solution)/shard_map/ppermute | solution.py:15
  581.1 12.5 %collective-permute-start.19 = (f32[60,384]{1,0:T(8,128)S(1)}, f32[60,384]{1,0:T(8,128)}, u32[]{:S(2)}, u32[]{:S(2)}) collective-permute-start(f32[60,384]{1,0:T(8,128)S(1)} %bitcast.156), channel_id=1, source_target_pairs={{16,0},{32,16},{48,32},{64,48},{80,64},{96,80},{112,96},{17,1},{33... | collective-permute-start | bytes 276488 | tf_op jit(solution)/shard_map/ppermute | solution.py:15
  583.7 11.9 %collective-permute-start.22 = (f32[60,384]{1,0:T(8,128)S(1)}, f32[60,384]{1,0:T(8,128)}, u32[]{:S(2)}, u32[]{:S(2)}) collective-permute-start(f32[60,384]{1,0:T(8,128)S(1)} %bitcast.155), channel_id=1, source_target_pairs={{16,0},{32,16},{48,32},{64,48},{80,64},{96,80},{112,96},{17,1},{33... | collective-permute-start | bytes 276488 | tf_op jit(solution)/shard_map/ppermute | solution.py:15
  585.7 13.8 %collective-permute-start.14 = (f32[60,384]{1,0:T(8,128)S(1)}, f32[60,384]{1,0:T(8,128)S(1)}, u32[]{:S(2)}, u32[]{:S(2)}) collective-permute-start(f32[60,384]{1,0:T(8,128)S(1)} %bitcast.154), channel_id=1, source_target_pairs={{0,16},{16,32},{32,48},{48,64},{64,80},{80,96},{96,112},{1,17},{17... | collective-permute-start | bytes 276488 | tf_op jit(solution)/shard_map/ppermute | solution.py:15
  589.6 11.2 %collective-permute-start.17 = (f32[60,384]{1,0:T(8,128)S(1)}, f32[60,384]{1,0:T(8,128)S(1)}, u32[]{:S(2)}, u32[]{:S(2)}) collective-permute-start(f32[60,384]{1,0:T(8,128)S(1)} %bitcast.153), channel_id=1, source_target_pairs={{0,1},{1,2},{2,3},{3,4},{4,5},{5,6},{6,7},{7,8},{8,9},{9,10},{10,1... | collective-permute-start | bytes 276488 | tf_op jit(solution)/shard_map/ppermute | solution.py:15
  591.6 13.9 %collective-permute-start.18 = (f32[60,384]{1,0:T(8,128)S(1)}, f32[60,384]{1,0:T(8,128)S(1)}, u32[]{:S(2)}, u32[]{:S(2)}) collective-permute-start(f32[60,384]{1,0:T(8,128)S(1)} %bitcast.149), channel_id=1, source_target_pairs={{1,0},{2,1},{3,2},{4,3},{5,4},{6,5},{7,6},{8,7},{9,8},{10,9},{11,1... | collective-permute-start | bytes 276488 | tf_op jit(solution)/shard_map/ppermute | solution.py:15
  593.6 25.1 %collective-permute-start.21 = (f32[60,384]{1,0:T(8,128)}, f32[60,384]{1,0:T(8,128)S(1)}, u32[]{:S(2)}, u32[]{:S(2)}) collective-permute-start(f32[60,384]{1,0:T(8,128)} %bitcast.45), channel_id=1, source_target_pairs={{16,0},{32,16},{48,32},{64,48},{80,64},{96,80},{112,96},{17,1},{33... | collective-permute-start | bytes 276488 | tf_op jit(solution)/shard_map/ppermute | solution.py:15
  595.6 23.3 %collective-permute-start.13 = (f32[60,384]{1,0:T(8,128)}, f32[60,384]{1,0:T(8,128)S(1)}, u32[]{:S(2)}, u32[]{:S(2)}) collective-permute-start(f32[60,384]{1,0:T(8,128)} %collective-permute-done.12), channel_id=1, source_target_pairs={{0,1},{1,2},{2,3},{3,4},{4,5},{5,6},{6,7},{7,8},{8,9},{9,10},{10,1... | collective-permute-start | bytes 276488 | tf_op jit(solution)/shard_map/ppermute | solution.py:15
  599.6 19.4 %collective-permute-start.16 = (f32[60,384]{1,0:T(8,128)}, f32[60,384]{1,0:T(8,128)}, u32[]{:S(2)}, u32[]{:S(2)}) collective-permute-start(f32[60,384]{1,0:T(8,128)} %copy-done.49), channel_id=1, source_target_pairs={{1,0},{2,1},{3,2},{4,3},{5,4},{6,5},{7,6},{8,7},{9,8},{10,9},{11,1... | collective-permute-start | bytes 276488 | tf_op jit(solution)/shard_map/ppermute | solution.py:15
  600.9 19.0 %collective-permute-start.20 = (f32[60,384]{1,0:T(8,128)}, f32[60,384]{1,0:T(8,128)}, u32[]{:S(2)}, u32[]{:S(2)}) collective-permute-start(f32[60,384]{1,0:T(8,128)} %collective-permute-done.19), channel_id=1, source_target_pairs={{0,1},{1,2},{2,3},{3,4},{4,5},{5,6},{6,7},{7,8},{8,9},{9,10},{10,1... | collective-permute-start | bytes 276488 | tf_op jit(solution)/shard_map/ppermute | solution.py:15
  605.5 15.3 %collective-permute-start.23 = (f32[60,384]{1,0:T(8,128)}, f32[60,384]{1,0:T(8,128)}, u32[]{:S(2)}, u32[]{:S(2)}) collective-permute-start(f32[60,384]{1,0:T(8,128)} %collective-permute-done.22), channel_id=1, source_target_pairs={{1,0},{2,1},{3,2},{4,3},{5,4},{6,5},{7,6},{8,7},{9,8},{10,9},{11,1... | collective-permute-start | bytes 276488 | tf_op jit(solution)/shard_map/ppermute | solution.py:15
  630.2 33.2 %copy-start.21 = (pred[8192]{0:T(1024)(128)(4,1)S(1)}, pred[8192]{0:T(1024)(128)(4,1)}, u32[]{:S(2)}) copy-start(pred[8192]{0:T(1024)(128)(4,1)} %copy-done.20) | copy-start | bytes 24580
  678.2 5.2 copy-start
  678.2 5.2 copy-start.31
  678.3 5.2 copy-start.43
  687.0 3.5 copy-start.27
  687.0 3.5 copy-start.39
  690.6 4.0 copy-start.25
  690.6 4.0 copy-start.37
  (26 other events, 70.6 us)
where the time goes:
time: 1050 us; the launch traced here: 1040 us
  local copies, waits for them, and re-layouts  372 us (35%)
  blocking collectives  339 us (32%)
  other arithmetic  210 us (20%)
  starting transfers between devices  58.9 us (6%)
  matrix products  52 us (5%)
    gather x16, local copies, waits for them, and re-layouts, one_block(): gathered = jnp.take(inverse_table, block_class, axis=0)  191 us
    psum x2, blocking collectives, shards(): coefficients = lax.psum(local_dots, ('prow', 'pcol'))  144 us
    while x32, other arithmetic  134 us
    psum x2, blocking collectives, shards(): lax.psum(local_inner(remainder, remainder), ('prow', 'pcol')) + EPSILON  126 us
    psum x1, blocking collectives, shards(): lax.psum(local_inner(first_vec, first_vec), ('prow', 'pcol')) + EPSILON  68.7 us
    gather x2, local copies, waits for them, and re-layouts, neighbour_traces(): picked = jnp.take(extended, jnp.maximum(links, 0), axis=1)  63.7 us
    ppermute x24, starting transfers between devices, passed_along(): lax.ppermute(value, axis, [(source, source + steps) for source in range(l...  58.9 us
    dot_general x12, matrix products, neighbour_traces(): jnp.einsum('jk,ckf->cjf', turn_tables[option], shaped, precision=lax.Prec...  43.5 us
  transfers between devices with their start and end apart: 24, of which 0 were waited for; matrix products, arithmetic and copies ran while one was open for 4% of the time, Pallas kernels for 0%

commit v1 on v0

--- a/solution.py
+++ b/solution.py
@@ -155,17 +155,8 @@
     flat_lists = lists.reshape(-1)
     list_mask = (flat_lists >= 0)[None, :].astype(jnp.float32)
 
-    def local_inner(left_vec, right_vec):
-        return jnp.sum(left_vec * right_vec) * weight
-
-    first_vec = right_side * live_cell_flags
-    scale_now = jnp.sqrt(lax.psum(local_inner(first_vec, first_vec), ("prow", "pcol")) + EPSILON)
-    pending = first_vec
-    basis_list = []
-    columns = []
-    for step_index in range(2):
-        current = pending / scale_now
-        own_traces = current[trace_index].reshape(60, 4 * elements)
+    def coupled_image(vector):
+        own_traces = vector[trace_index].reshape(60, 4 * elements)
         outgoing = (jnp.take(own_traces, jnp.maximum(flat_lists, 0), axis=1) * list_mask).reshape(
             60, 8, list_slots
         )
@@ -174,30 +165,53 @@
             own_traces, incoming_boundary_values, face_link, face_orient, turn_tables
         )
         coupled = lift_faces(upwind_flux(neighbour, face_normal, boundary_metric_quotient), lift)
-        basis_list.append(current)
-        applied = precondition(coupled.astype(jnp.bfloat16), elem_class, inverse_table)
-        image_vec = current + live_cell_flags * applied
-        local_dots = jnp.stack([local_inner(earlier, image_vec) for earlier in basis_list])
-        coefficients = lax.psum(local_dots, ("prow", "pcol"))
-        remainder = image_vec
-        for earlier_index in range(len(basis_list)):
-            remainder = remainder - coefficients[earlier_index] * basis_list[earlier_index]
-        scale_now = jnp.sqrt(
-            lax.psum(local_inner(remainder, remainder), ("prow", "pcol")) + EPSILON
-        )
-        columns.append((coefficients, scale_now))
-        pending = remainder
-    basis_list.append(pending / scale_now)
-    first_col, second_col = columns
+        return live_cell_flags * precondition(coupled.astype(jnp.bfloat16), elem_class, inverse_table)
+
+    def local_inner(left_vec, right_vec):
+        return jnp.sum(left_vec * right_vec) * weight
+
+    first = right_side * live_cell_flags
+    second = coupled_image(first)
+    third = coupled_image(second)
+    gram = lax.psum(
+        jnp.stack(
+            [
+                local_inner(first, first),
+                local_inner(first, second),
+                local_inner(second, second),
+                local_inner(first, third),
+                local_inner(second, third),
+                local_inner(third, third),
+            ]
+        ),
+        ("prow", "pcol"),
+    )
+    ff, ft, tt, fu, tu, uu = (gram[index] for index in range(6))
+    beta = jnp.sqrt(ff + EPSILON)
+    h00 = (ff + ft) / (beta * beta)
+    p = (EPSILON - ft) / (beta * beta)
+    h10 = jnp.sqrt((tt + 2 * p * ft + p * p * ff) / (beta * beta) + EPSILON)
+    k1 = 1.0 / (beta * h10)
+    h01 = k1 / beta * (fu + (1 + p) * ft + p * ff)
+    h11 = k1 * k1 * (tu + (1 + p) * tt + p * ft + p * fu + p * (1 + p) * ft + p * p * ff)
+    q = 1 + p - h11
+    w = p * (1 - h11) - h01 * h10
+    h21 = jnp.sqrt(
+        k1 * k1 * (uu + 2 * q * tu + 2 * w * fu + q * q * tt + 2 * q * w * ft + w * w * ff) + EPSILON
+    )
+    k2 = k1 / h21
+    basis = jnp.stack(
+        [
+            first * (1.0 / beta),
+            second * k1 + first * (p * k1),
+            third * k2 + second * (q * k2) + first * (w * k2),
+        ]
+    )
     zero_entry = jnp.zeros((), jnp.float32)
     hess = jnp.stack(
-        [
-            jnp.stack([first_col[0][0], second_col[0][0]]),
-            jnp.stack([first_col[1], second_col[0][1]]),
-            jnp.stack([zero_entry, second_col[1]]),
-        ]
-    )
-    return (jnp.stack(basis_list), hess)
+        [jnp.stack([h00, h01]), jnp.stack([h10, h11]), jnp.stack([zero_entry, h21])]
+    )
+    return (basis, hess)
 
 
 def solution(mesh):

time: 1050 us -> 779 us (0.74)
  blocking collectives: 339 us -> 76 us
  other arithmetic: 210 us -> 192 us
  between operations: 8.7 us -> 20 us
  local copies, waits for them, and re-layouts: 372 us -> 361 us
    psum x5 -> x1, blocking collectives: 339 us -> 76 us  [shards(): lax.psum(jnp.stack([local_inner(first, first), local_inner(first, second)...]
  transfers between devices with their start and end apart: 24 -> 24, of which waited for: 0 -> 0; matrix products, arithmetic and copies ran while one was open for 4% -> 5% of each run, Pallas kernels for 0% -> 0%
where the time goes in v1:
time: 779 us; the launch traced here: 767 us
  local copies, waits for them, and re-layouts  361 us (46%)
  other arithmetic  192 us (25%)
  blocking collectives  76 us (10%)
  starting transfers between devices  68.4 us (9%)
  matrix products  49.6 us (6%)
  between operations  20 us (3%)
    gather x16, local copies, waits for them, and re-layouts, one_block(): gathered = jnp.take(inverse_table, block_class, axis=0)  191 us
    while x32, other arithmetic  134 us
    psum x1, blocking collectives, shards(): lax.psum(jnp.stack([local_inner(first, first), local_inner(first, second)...  76 us
    ppermute x24, starting transfers between devices, passed_along(): lax.ppermute(value, axis, [(source, source + steps) for source in range(l...  68.4 us
    gather x2, local copies, waits for them, and re-layouts, neighbour_traces(): picked = jnp.take(extended, jnp.maximum(links, 0), axis=1)  61 us
    dot_general x12, matrix products, neighbour_traces(): jnp.einsum('jk,ckf->cjf', turn_tables[option], shaped, precision=lax.Prec...  41.1 us
    gather x2, local copies, waits for them, and re-layouts, coupled_image(): jnp.take(own_traces, jnp.maximum(flat_lists, 0), axis=1) * list_mask  26.2 us
  transfers between devices with their start and end apart: 24, of which 0 were waited for; matrix products, arithmetic and copies ran while one was open for 5% of the time, Pallas kernels for 0%

profile of v1, /device:TPU:1, one launch (start us, length us, event | category | flops | bytes accessed | tf_op | source)
XLA Modules:
  0.0 767.2 jit_solution(8435320925283633594)
XLA Ops:
  12.3 13.1 %gather_fusion.4 = f32[3072,60]{1,0:T(8,128)} fusion(f32[60,8192]{0,1:T(8,128)} %copy.75, s32[3072]{0:T(1024)S(1)} %fusion.38), kind=kCustom, calls=%fused_computation.clone | custom fusion | bytes 1486848 | tf_op jit(solution)/shard_map/jit(_take)/gather | solution.py:160
  30.7 4.6 collective-permute-start
  76.3 10.7 %copy.91 = bf16[256,120,120]{2,1,0:T(8,128)(2,1)} copy(bf16[256,120,120]{0,2,1:T(8,128)(2,1)} %param.44) | data formatting | bytes 14745600 | tf_op jit(solution)/shard_map/while | solution.py:118
  90.3 4.6 pad_maximum_fusion
  94.9 30.5 %gather_fusion.5 = f32[8192,60]{1,0:T(8,128)} fusion(f32[60,11264]{0,1:T(8,128)} %pad_maximum_fusion, s32[8192]{0:T(1024)S(1)} %maximum_clamp_fusion), kind=kCustom, calls=%fused_computation.1.clone | custom fusion | bytes 3964928 | tf_op jit(solution)/shard_map/jit(_take)/gather | solution.py:84
  125.4 7.5 maximum_select_fusion
  169.2 167.2 %while.26 = (s32[]{:T(128)}, f32[120,2048]{1,0:T(8,128)S(1)}, bf16[120,2048]{1,0:T(8,128)(2,1)S(1)}, s32[2048]{0:T(1024)}, bf16[256,120,120]{2,1,0:T(8,128)(2,1)...) while((s32[]{:T(128)}, f32[120,2048]{1,0:T(8,128)S(1)}, bf16[120,2048]{1,0:T(8,128)(2,1)S(1)}, ...), condition=%wide.region_4.8_spmd, body=%wide.region_3.7_spmd.sunk | while | flops 14748166 | bytes 23294616 | solution.py:118
  170.0 11.9 %gather_fusion = bf16[256,120,120]{2,1,0:T(8,128)(2,1)} fusion(bf16[256,120,120]{2,1,0:T(8,128)(2,1)} %get-tuple-element.413, s32[1024]{0:T(1024)S(1)} %pad_clamp_fusion.5), kind=kCustom, calls=%fused_computation.2.clone.clone.1 | custom fusion | bytes 14746624 | tf_op jit(solution)/shard_map/while/body/eval_jaxpr/jit(_take)/gather | solution.py:113
  182.1 7.9 %multiply_reduce_fusion.14 = f32[256,120]{1,0:T(8,128)S(1)} fusion(f32[256,120]{1,0:T(8,128)S(1)} %copy.180, bf16[256,120,120]{2,1,0:T(8,128)(2,1)} %gather_fusion, pred[256]{0:T(512)(128)(4,1)S(1)} %get-tuple-element.383), kind=kLoop, calls=%fused_computation.8.clone.1 | loop fusion | flops 14714880 | bytes 7618816 | tf_op jit(solution)/shard_map/while
  190.9 11.9 %gather_fusion = bf16[256,120,120]{2,1,0:T(8,128)(2,1)} fusion(bf16[256,120,120]{2,1,0:T(8,128)(2,1)} %get-tuple-element.413, s32[1024]{0:T(1024)S(1)} %pad_clamp_fusion.5), kind=kCustom, calls=%fused_computation.2.clone.clone.1 | custom fusion | bytes 14746624 | tf_op jit(solution)/shard_map/while/body/eval_jaxpr/jit(_take)/gather | solution.py:113
  203.0 7.9 %multiply_reduce_fusion.14 = f32[256,120]{1,0:T(8,128)S(1)} fusion(f32[256,120]{1,0:T(8,128)S(1)} %copy.180, bf16[256,120,120]{2,1,0:T(8,128)(2,1)} %gather_fusion, pred[256]{0:T(512)(128)(4,1)S(1)} %get-tuple-element.383), kind=kLoop, calls=%fused_computation.8.clone.1 | loop fusion | flops 14714880 | bytes 7618816 | tf_op jit(solution)/shard_map/while
  211.8 11.9 %gather_fusion = bf16[256,120,120]{2,1,0:T(8,128)(2,1)} fusion(bf16[256,120,120]{2,1,0:T(8,128)(2,1)} %get-tuple-element.413, s32[1024]{0:T(1024)S(1)} %pad_clamp_fusion.5), kind=kCustom, calls=%fused_computation.2.clone.clone.1 | custom fusion | bytes 14746624 | tf_op jit(solution)/shard_map/while/body/eval_jaxpr/jit(_take)/gather | solution.py:113
  223.9 7.9 %multiply_reduce_fusion.14 = f32[256,120]{1,0:T(8,128)S(1)} fusion(f32[256,120]{1,0:T(8,128)S(1)} %copy.180, bf16[256,120,120]{2,1,0:T(8,128)(2,1)} %gather_fusion, pred[256]{0:T(512)(128)(4,1)S(1)} %get-tuple-element.383), kind=kLoop, calls=%fused_computation.8.clone.1 | loop fusion | flops 14714880 | bytes 7618816 | tf_op jit(solution)/shard_map/while
  232.8 11.9 %gather_fusion = bf16[256,120,120]{2,1,0:T(8,128)(2,1)} fusion(bf16[256,120,120]{2,1,0:T(8,128)(2,1)} %get-tuple-element.413, s32[1024]{0:T(1024)S(1)} %pad_clamp_fusion.5), kind=kCustom, calls=%fused_computation.2.clone.clone.1 | custom fusion | bytes 14746624 | tf_op jit(solution)/shard_map/while/body/eval_jaxpr/jit(_take)/gather | solution.py:113
  244.8 7.9 %multiply_reduce_fusion.14 = f32[256,120]{1,0:T(8,128)S(1)} fusion(f32[256,120]{1,0:T(8,128)S(1)} %copy.180, bf16[256,120,120]{2,1,0:T(8,128)(2,1)} %gather_fusion, pred[256]{0:T(512)(128)(4,1)S(1)} %get-tuple-element.383), kind=kLoop, calls=%fused_computation.8.clone.1 | loop fusion | flops 14714880 | bytes 7618816 | tf_op jit(solution)/shard_map/while
  253.7 11.9 %gather_fusion = bf16[256,120,120]{2,1,0:T(8,128)(2,1)} fusion(bf16[256,120,120]{2,1,0:T(8,128)(2,1)} %get-tuple-element.413, s32[1024]{0:T(1024)S(1)} %pad_clamp_fusion.5), kind=kCustom, calls=%fused_computation.2.clone.clone.1 | custom fusion | bytes 14746624 | tf_op jit(solution)/shard_map/while/body/eval_jaxpr/jit(_take)/gather | solution.py:113
  265.7 7.9 %multiply_reduce_fusion.14 = f32[256,120]{1,0:T(8,128)S(1)} fusion(f32[256,120]{1,0:T(8,128)S(1)} %copy.180, bf16[256,120,120]{2,1,0:T(8,128)(2,1)} %gather_fusion, pred[256]{0:T(512)(128)(4,1)S(1)} %get-tuple-element.383), kind=kLoop, calls=%fused_computation.8.clone.1 | loop fusion | flops 14714880 | bytes 7618816 | tf_op jit(solution)/shard_map/while
  274.6 11.9 %gather_fusion = bf16[256,120,120]{2,1,0:T(8,128)(2,1)} fusion(bf16[256,120,120]{2,1,0:T(8,128)(2,1)} %get-tuple-element.413, s32[1024]{0:T(1024)S(1)} %pad_clamp_fusion.5), kind=kCustom, calls=%fused_computation.2.clone.clone.1 | custom fusion | bytes 14746624 | tf_op jit(solution)/shard_map/while/body/eval_jaxpr/jit(_take)/gather | solution.py:113
  286.6 7.9 %multiply_reduce_fusion.14 = f32[256,120]{1,0:T(8,128)S(1)} fusion(f32[256,120]{1,0:T(8,128)S(1)} %copy.180, bf16[256,120,120]{2,1,0:T(8,128)(2,1)} %gather_fusion, pred[256]{0:T(512)(128)(4,1)S(1)} %get-tuple-element.383), kind=kLoop, calls=%fused_computation.8.clone.1 | loop fusion | flops 14714880 | bytes 7618816 | tf_op jit(solution)/shard_map/while
  295.5 11.9 %gather_fusion = bf16[256,120,120]{2,1,0:T(8,128)(2,1)} fusion(bf16[256,120,120]{2,1,0:T(8,128)(2,1)} %get-tuple-element.413, s32[1024]{0:T(1024)S(1)} %pad_clamp_fusion.5), kind=kCustom, calls=%fused_computation.2.clone.clone.1 | custom fusion | bytes 14746624 | tf_op jit(solution)/shard_map/while/body/eval_jaxpr/jit(_take)/gather | solution.py:113
  307.5 7.9 %multiply_reduce_fusion.14 = f32[256,120]{1,0:T(8,128)S(1)} fusion(f32[256,120]{1,0:T(8,128)S(1)} %copy.180, bf16[256,120,120]{2,1,0:T(8,128)(2,1)} %gather_fusion, pred[256]{0:T(512)(128)(4,1)S(1)} %get-tuple-element.383), kind=kLoop, calls=%fused_computation.8.clone.1 | loop fusion | flops 14714880 | bytes 7618816 | tf_op jit(solution)/shard_map/while
  316.4 11.9 %gather_fusion = bf16[256,120,120]{2,1,0:T(8,128)(2,1)} fusion(bf16[256,120,120]{2,1,0:T(8,128)(2,1)} %get-tuple-element.413, s32[1024]{0:T(1024)S(1)} %pad_clamp_fusion.5), kind=kCustom, calls=%fused_computation.2.clone.clone.1 | custom fusion | bytes 14746624 | tf_op jit(solution)/shard_map/while/body/eval_jaxpr/jit(_take)/gather | solution.py:113
  328.4 7.9 %multiply_reduce_fusion.14 = f32[256,120]{1,0:T(8,128)S(1)} fusion(f32[256,120]{1,0:T(8,128)S(1)} %copy.180, bf16[256,120,120]{2,1,0:T(8,128)(2,1)} %gather_fusion, pred[256]{0:T(512)(128)(4,1)S(1)} %get-tuple-element.383), kind=kLoop, calls=%fused_computation.8.clone.1 | loop fusion | flops 14714880 | bytes 7618816 | tf_op jit(solution)/shard_map/while
  345.2 13.1 %gather_fusion.6 = f32[3072,60]{1,0:T(8,128)} fusion(f32[60,8192]{0,1:T(8,128)} %copy.94, s32[3072]{0:T(1024)S(1)} %copy-done.23), kind=kCustom, calls=%fused_computation.3.clone | custom fusion | bytes 1486848 | tf_op jit(solution)/shard_map/jit(_take)/gather | solution.py:160
  362.1 4.5 collective-permute-start.12
  386.8 4.8 collective-permute-start.13
  393.0 7.0 collective-permute-start.20
  414.7 4.6 pad_maximum_fusion.1
  419.3 30.5 %gather_fusion.7 = f32[8192,60]{1,0:T(8,128)} fusion(f32[60,11264]{0,1:T(8,128)} %pad_maximum_fusion.1, s32[8192]{0:T(1024)S(1)} %copy-done.10), kind=kCustom, calls=%fused_computation.4.clone | custom fusion | bytes 3964928 | tf_op jit(solution)/shard_map/jit(_take)/gather | solution.py:84
  449.8 7.5 maximum_select_fusion.1
  494.9 174.0 %while.27 = (s32[]{:T(128)}, f32[120,2048]{1,0:T(8,128)S(1)}, bf16[120,2048]{1,0:T(8,128)(2,1)}, s32[2048]{0:T(1024)}, bf16[256,120,120]{2,1,0:T(8,128)(2,1)}, /*index=5*/s32[]{:T(128)}, s32[]{:T(128)}, s32[]{:T(128)}, s32[]{:T(128)}) while((s32[]{:T(128)}, f32[120,2048]{1,0:T(8,128)S(1)}, bf16[120,2048]{1,0:T(8,128)(2,1)}, ...), condition=%wide.region_10.14_spmd, body=%wide.region_9.13_spmd.sunk | while | flops 14748166 | bytes 23294616 | solution.py:118
  495.8 11.9 %gather_fusion.1 = bf16[256,120,120]{2,1,0:T(8,128)(2,1)} fusion(bf16[256,120,120]{2,1,0:T(8,128)(2,1)} %get-tuple-element.440, s32[1024]{0:T(1024)S(1)} %pad_clamp_fusion.6), kind=kCustom, calls=%fused_computation.5.clone.clone.1 | custom fusion | bytes 14746624 | tf_op jit(solution)/shard_map/while/body/eval_jaxpr/jit(_take)/gather | solution.py:113
  508.7 7.9 %multiply_reduce_fusion.15 = f32[256,120]{1,0:T(8,128)S(1)} fusion(f32[256,120]{1,0:T(8,128)S(1)} %copy.182, bf16[256,120,120]{2,1,0:T(8,128)(2,1)} %gather_fusion.1, pred[256]{0:T(512)(128)(4,1)S(1)} %get-tuple-element.390), kind=kLoop, calls=%fused_computation.14.clone.1 | loop fusion | flops 14714880 | bytes 7618816 | tf_op jit(solution)/shard_map/while
  517.6 11.9 %gather_fusion.1 = bf16[256,120,120]{2,1,0:T(8,128)(2,1)} fusion(bf16[256,120,120]{2,1,0:T(8,128)(2,1)} %get-tuple-element.440, s32[1024]{0:T(1024)S(1)} %pad_clamp_fusion.6), kind=kCustom, calls=%fused_computation.5.clone.clone.1 | custom fusion | bytes 14746624 | tf_op jit(solution)/shard_map/while/body/eval_jaxpr/jit(_take)/gather | solution.py:113
  530.4 7.9 %multiply_reduce_fusion.15 = f32[256,120]{1,0:T(8,128)S(1)} fusion(f32[256,120]{1,0:T(8,128)S(1)} %copy.182, bf16[256,120,120]{2,1,0:T(8,128)(2,1)} %gather_fusion.1, pred[256]{0:T(512)(128)(4,1)S(1)} %get-tuple-element.390), kind=kLoop, calls=%fused_computation.14.clone.1 | loop fusion | flops 14714880 | bytes 7618816 | tf_op jit(solution)/shard_map/while
  539.3 11.9 %gather_fusion.1 = bf16[256,120,120]{2,1,0:T(8,128)(2,1)} fusion(bf16[256,120,120]{2,1,0:T(8,128)(2,1)} %get-tuple-element.440, s32[1024]{0:T(1024)S(1)} %pad_clamp_fusion.6), kind=kCustom, calls=%fused_computation.5.clone.clone.1 | custom fusion | bytes 14746624 | tf_op jit(solution)/shard_map/while/body/eval_jaxpr/jit(_take)/gather | solution.py:113
  552.2 7.9 %multiply_reduce_fusion.15 = f32[256,120]{1,0:T(8,128)S(1)} fusion(f32[256,120]{1,0:T(8,128)S(1)} %copy.182, bf16[256,120,120]{2,1,0:T(8,128)(2,1)} %gather_fusion.1, pred[256]{0:T(512)(128)(4,1)S(1)} %get-tuple-element.390), kind=kLoop, calls=%fused_computation.14.clone.1 | loop fusion | flops 14714880 | bytes 7618816 | tf_op jit(solution)/shard_map/while
  561.0 11.9 %gather_fusion.1 = bf16[256,120,120]{2,1,0:T(8,128)(2,1)} fusion(bf16[256,120,120]{2,1,0:T(8,128)(2,1)} %get-tuple-element.440, s32[1024]{0:T(1024)S(1)} %pad_clamp_fusion.6), kind=kCustom, calls=%fused_computation.5.clone.clone.1 | custom fusion | bytes 14746624 | tf_op jit(solution)/shard_map/while/body/eval_jaxpr/jit(_take)/gather | solution.py:113
  573.9 7.9 %multiply_reduce_fusion.15 = f32[256,120]{1,0:T(8,128)S(1)} fusion(f32[256,120]{1,0:T(8,128)S(1)} %copy.182, bf16[256,120,120]{2,1,0:T(8,128)(2,1)} %gather_fusion.1, pred[256]{0:T(512)(128)(4,1)S(1)} %get-tuple-element.390), kind=kLoop, calls=%fused_computation.14.clone.1 | loop fusion | flops 14714880 | bytes 7618816 | tf_op jit(solution)/shard_map/while
  582.8 11.9 %gather_fusion.1 = bf16[256,120,120]{2,1,0:T(8,128)(2,1)} fusion(bf16[256,120,120]{2,1,0:T(8,128)(2,1)} %get-tuple-element.440, s32[1024]{0:T(1024)S(1)} %pad_clamp_fusion.6), kind=kCustom, calls=%fused_computation.5.clone.clone.1 | custom fusion | bytes 14746624 | tf_op jit(solution)/shard_map/while/body/eval_jaxpr/jit(_take)/gather | solution.py:113
  595.6 7.9 %multiply_reduce_fusion.15 = f32[256,120]{1,0:T(8,128)S(1)} fusion(f32[256,120]{1,0:T(8,128)S(1)} %copy.182, bf16[256,120,120]{2,1,0:T(8,128)(2,1)} %gather_fusion.1, pred[256]{0:T(512)(128)(4,1)S(1)} %get-tuple-element.390), kind=kLoop, calls=%fused_computation.14.clone.1 | loop fusion | flops 14714880 | bytes 7618816 | tf_op jit(solution)/shard_map/while
  604.5 11.9 %gather_fusion.1 = bf16[256,120,120]{2,1,0:T(8,128)(2,1)} fusion(bf16[256,120,120]{2,1,0:T(8,128)(2,1)} %get-tuple-element.440, s32[1024]{0:T(1024)S(1)} %pad_clamp_fusion.6), kind=kCustom, calls=%fused_computation.5.clone.clone.1 | custom fusion | bytes 14746624 | tf_op jit(solution)/shard_map/while/body/eval_jaxpr/jit(_take)/gather | solution.py:113
  617.4 7.9 %multiply_reduce_fusion.15 = f32[256,120]{1,0:T(8,128)S(1)} fusion(f32[256,120]{1,0:T(8,128)S(1)} %copy.182, bf16[256,120,120]{2,1,0:T(8,128)(2,1)} %gather_fusion.1, pred[256]{0:T(512)(128)(4,1)S(1)} %get-tuple-element.390), kind=kLoop, calls=%fused_computation.14.clone.1 | loop fusion | flops 14714880 | bytes 7618816 | tf_op jit(solution)/shard_map/while
  626.2 11.9 %gather_fusion.1 = bf16[256,120,120]{2,1,0:T(8,128)(2,1)} fusion(bf16[256,120,120]{2,1,0:T(8,128)(2,1)} %get-tuple-element.440, s32[1024]{0:T(1024)S(1)} %pad_clamp_fusion.6), kind=kCustom, calls=%fused_computation.5.clone.clone.1 | custom fusion | bytes 14746624 | tf_op jit(solution)/shard_map/while/body/eval_jaxpr/jit(_take)/gather | solution.py:113
  639.1 7.9 %multiply_reduce_fusion.15 = f32[256,120]{1,0:T(8,128)S(1)} fusion(f32[256,120]{1,0:T(8,128)S(1)} %copy.182, bf16[256,120,120]{2,1,0:T(8,128)(2,1)} %gather_fusion.1, pred[256]{0:T(512)(128)(4,1)S(1)} %get-tuple-element.390), kind=kLoop, calls=%fused_computation.14.clone.1 | loop fusion | flops 14714880 | bytes 7618816 | tf_op jit(solution)/shard_map/while
  648.0 11.9 %gather_fusion.1 = bf16[256,120,120]{2,1,0:T(8,128)(2,1)} fusion(bf16[256,120,120]{2,1,0:T(8,128)(2,1)} %get-tuple-element.440, s32[1024]{0:T(1024)S(1)} %pad_clamp_fusion.6), kind=kCustom, calls=%fused_computation.5.clone.clone.1 | custom fusion | bytes 14746624 | tf_op jit(solution)/shard_map/while/body/eval_jaxpr/jit(_take)/gather | solution.py:113
  660.8 7.9 %multiply_reduce_fusion.15 = f32[256,120]{1,0:T(8,128)S(1)} fusion(f32[256,120]{1,0:T(8,128)S(1)} %copy.182, bf16[256,120,120]{2,1,0:T(8,128)(2,1)} %gather_fusion.1, pred[256]{0:T(512)(128)(4,1)S(1)} %get-tuple-element.390), kind=kLoop, calls=%fused_computation.14.clone.1 | loop fusion | flops 14714880 | bytes 7618816 | tf_op jit(solution)/shard_map/while
  674.0 76.0 %psum.7 = f32[6]{0:T(128)S(1)} all-reduce(f32[6]{0:T(128)S(1)} %stack.175), channel_id=1, replica_groups=mesh['prow'=8,'pcol'=16] {'prow','pcol'}, use_global_device_ids=true, to_apply=%region_14.18 | all-reduce | flops 6 | bytes 48 | tf_op jit(solution)/shard_map/psum | solution.py:176
  (371 shorter events, 209.5 us)
Async XLA Ops:
  1.4 10.9 %copy-start.22 = (s32[3072]{0:T(1024)}, s32[3072]{0:T(1024)S(1)}, u32[]{:S(2)}) copy-start(s32[3072]{0:T(1024)S(1)} %fusion.38) | copy-start | bytes 36868
  1.4 24.0 %copy-start.54 = (pred[3072]{0:T(1024)(128)(4,1)}, pred[3072]{0:T(1024)(128)(4,1)S(1)}, u32[]{:S(2)}) copy-start(pred[3072]{0:T(1024)(128)(4,1)S(1)} %compare_and_fusion.2) | copy-start | bytes 9220
  12.3 13.1 %copy-start.20 = (f32[3072]{0:T(1024)}, f32[3072]{0:T(1024)S(1)}, u32[]{:S(2)}) copy-start(f32[3072]{0:T(1024)S(1)} %reshape.258) | copy-start | bytes 36868
  28.9 20.2 %copy-start.52 = (s32[8192]{0:T(1024)S(1)}, s32[8192]{0:T(1024)}, u32[]{:S(2)}) copy-start(s32[8192]{0:T(1024)} %param.39) | copy-start | bytes 98308
  28.9 20.8 %copy-start.7 = (f32[3,8192]{1,0:T(4,128)S(1)}, f32[3,8192]{1,0:T(4,128)}, u32[]{:S(2)}) copy-start(f32[3,8192]{1,0:T(4,128)} %param.40) | copy-start | bytes 294916
  28.9 20.9 %copy-start.19 = (s32[8192]{0:T(1024)S(1)}, s32[8192]{0:T(1024)}, u32[]{:S(2)}) copy-start(s32[8192]{0:T(1024)} %param.38) | copy-start | bytes 98308
  30.7 19.5 %collective-permute-start = (f32[60,384]{1,0:T(8,128)}, f32[60,384]{1,0:T(8,128)}, u32[]{:S(2)}, u32[]{:S(2)}) collective-permute-start(f32[60,384]{1,0:T(8,128)} %bitcast.159), channel_id=1, source_target_pairs={{0,16},{16,32},{32,48},{48,64},{64,80},{80,96},{96,112},{1,17},{17... | collective-permute-start | bytes 276488 | tf_op jit(solution)/shard_map/ppermute | solution.py:15
  36.0 18.6 %copy-start.53 = (f32[8192]{0:T(1024)S(1)}, f32[8192]{0:T(1024)}, u32[]{:S(2)}) copy-start(f32[8192]{0:T(1024)} %param.41) | copy-start | bytes 98308
  36.0 17.2 %collective-permute-start.3 = (f32[60,384]{1,0:T(8,128)}, f32[60,384]{1,0:T(8,128)}, u32[]{:S(2)}, u32[]{:S(2)}) collective-permute-start(f32[60,384]{1,0:T(8,128)} %bitcast.158), channel_id=1, source_target_pairs={{0,16},{16,32},{32,48},{48,64},{64,80},{80,96},{96,112},{1,17},{17... | collective-permute-start | bytes 276488 | tf_op jit(solution)/shard_map/ppermute | solution.py:15
  38.8 16.5 %collective-permute-start.7 = (f32[60,384]{1,0:T(8,128)}, f32[60,384]{1,0:T(8,128)}, u32[]{:S(2)}, u32[]{:S(2)}) collective-permute-start(f32[60,384]{1,0:T(8,128)} %bitcast.15), channel_id=1, source_target_pairs={{16,0},{32,16},{48,32},{64,48},{80,64},{96,80},{112,96},{17,1},{33... | collective-permute-start | bytes 276488 | tf_op jit(solution)/shard_map/ppermute | solution.py:15
  42.0 15.3 %collective-permute-start.10 = (f32[60,384]{1,0:T(8,128)S(1)}, f32[60,384]{1,0:T(8,128)}, u32[]{:S(2)}, u32[]{:S(2)}) collective-permute-start(f32[60,384]{1,0:T(8,128)S(1)} %bitcast.155), channel_id=1, source_target_pairs={{16,0},{32,16},{48,32},{64,48},{80,64},{96,80},{112,96},{17,1},{33... | collective-permute-start | bytes 276488 | tf_op jit(solution)/shard_map/ppermute | solution.py:15
  44.1 17.3 %collective-permute-start.2 = (f32[60,384]{1,0:T(8,128)S(1)}, f32[60,384]{1,0:T(8,128)S(1)}, u32[]{:S(2)}, u32[]{:S(2)}) collective-permute-start(f32[60,384]{1,0:T(8,128)S(1)} %bitcast.154), channel_id=1, source_target_pairs={{0,16},{16,32},{32,48},{48,64},{64,80},{80,96},{96,112},{1,17},{17... | collective-permute-start | bytes 276488 | tf_op jit(solution)/shard_map/ppermute | solution.py:15
  49.8 109.8 %copy-start.11 = (f32[1,8192]{1,0:T(1,128)}, f32[1,8192]{1,0:T(1,128)S(1)}, u32[]{:S(2)}) copy-start(f32[1,8192]{1,0:T(1,128)S(1)} %get-tuple-element.302) | copy-start | bytes 98308
  49.8 109.8 %copy-start.13 = (f32[1,8192]{1,0:T(1,128)}, f32[1,8192]{1,0:T(1,128)S(1)}, u32[]{:S(2)}) copy-start(f32[1,8192]{1,0:T(1,128)S(1)} %get-tuple-element.303) | copy-start | bytes 98308
  49.9 109.8 %copy-start.15 = (f32[1,8192]{1,0:T(1,128)}, f32[1,8192]{1,0:T(1,128)S(1)}, u32[]{:S(2)}) copy-start(f32[1,8192]{1,0:T(1,128)S(1)} %get-tuple-element.304) | copy-start | bytes 98308
  49.9 45.0 %copy-start.9 = (s32[8192]{0:T(1024)}, s32[8192]{0:T(1024)S(1)}, u32[]{:S(2)}) copy-start(s32[8192]{0:T(1024)S(1)} %maximum_clamp_fusion) | copy-start | bytes 98308
  50.2 12.5 %collective-permute-start.5 = (f32[60,384]{1,0:T(8,128)S(1)}, f32[60,384]{1,0:T(8,128)S(1)}, u32[]{:S(2)}, u32[]{:S(2)}) collective-permute-start(f32[60,384]{1,0:T(8,128)S(1)} %bitcast.160), channel_id=1, source_target_pairs={{0,1},{1,2},{2,3},{3,4},{4,5},{5,6},{6,7},{7,8},{8,9},{9,10},{10,1... | collective-permute-start | bytes 276488 | tf_op jit(solution)/shard_map/ppermute | solution.py:15
  53.3 13.3 %collective-permute-start.6 = (f32[60,384]{1,0:T(8,128)S(1)}, f32[60,384]{1,0:T(8,128)S(1)}, u32[]{:S(2)}, u32[]{:S(2)}) collective-permute-start(f32[60,384]{1,0:T(8,128)S(1)} %bitcast.156), channel_id=1, source_target_pairs={{1,0},{2,1},{3,2},{4,3},{5,4},{6,5},{7,6},{8,7},{9,8},{10,9},{11,1... | collective-permute-start | bytes 276488 | tf_op jit(solution)/shard_map/ppermute | solution.py:15
  55.4 31.8 %collective-permute-start.9 = (f32[60,384]{1,0:T(8,128)}, f32[60,384]{1,0:T(8,128)S(1)}, u32[]{:S(2)}, u32[]{:S(2)}) collective-permute-start(f32[60,384]{1,0:T(8,128)} %bitcast.16), channel_id=1, source_target_pairs={{16,0},{32,16},{48,32},{64,48},{80,64},{96,80},{112,96},{17,1},{33... | collective-permute-start | bytes 276488 | tf_op jit(solution)/shard_map/ppermute | solution.py:15
  57.3 30.0 %collective-permute-start.1 = (f32[60,384]{1,0:T(8,128)}, f32[60,384]{1,0:T(8,128)S(1)}, u32[]{:S(2)}, u32[]{:S(2)}) collective-permute-start(f32[60,384]{1,0:T(8,128)} %collective-permute-done), channel_id=1, source_target_pairs={{0,1},{1,2},{2,3},{3,4},{4,5},{5,6},{6,7},{7,8},{8,9},{9,10},{10,1... | collective-permute-start | bytes 276488 | tf_op jit(solution)/shard_map/ppermute | solution.py:15
  61.3 6.7 copy-start.24
  61.3 26.0 %collective-permute-start.4 = (f32[60,384]{1,0:T(8,128)}, f32[60,384]{1,0:T(8,128)S(1)}, u32[]{:S(2)}, u32[]{:S(2)}) collective-permute-start(f32[60,384]{1,0:T(8,128)} %collective-permute-done.3), channel_id=1, source_target_pairs={{1,0},{2,1},{3,2},{4,3},{5,4},{6,5},{7,6},{8,7},{9,8},{10,9},{11,1... | collective-permute-start | bytes 276488 | tf_op jit(solution)/shard_map/ppermute | solution.py:15
  62.6 24.8 %collective-permute-start.8 = (f32[60,384]{1,0:T(8,128)}, f32[60,384]{1,0:T(8,128)S(1)}, u32[]{:S(2)}, u32[]{:S(2)}) collective-permute-start(f32[60,384]{1,0:T(8,128)} %collective-permute-done.7), channel_id=1, source_target_pairs={{0,1},{1,2},{2,3},{3,4},{4,5},{5,6},{6,7},{7,8},{8,9},{9,10},{10,1... | collective-permute-start | bytes 276488 | tf_op jit(solution)/shard_map/ppermute | solution.py:15
  66.6 20.9 %collective-permute-start.11 = (f32[60,384]{1,0:T(8,128)}, f32[60,384]{1,0:T(8,128)}, u32[]{:S(2)}, u32[]{:S(2)}) collective-permute-start(f32[60,384]{1,0:T(8,128)} %collective-permute-done.10), channel_id=1, source_target_pairs={{1,0},{2,1},{3,2},{4,3},{5,4},{6,5},{7,6},{8,7},{9,8},{10,9},{11,1... | collective-permute-start | bytes 276488 | tf_op jit(solution)/shard_map/ppermute | solution.py:15
  68.0 57.4 %copy-start.26 = (pred[8192]{0:T(1024)(128)(4,1)}, pred[8192]{0:T(1024)(128)(4,1)S(1)}, u32[]{:S(2)}) copy-start(pred[8192]{0:T(1024)(128)(4,1)S(1)} %get-tuple-element.312) | copy-start | bytes 24580
  68.0 4.5 copy-start.3
  76.3 10.7 %copy-start.25 = (f32[60,384]{1,0:T(8,128)S(1)}, f32[60,384]{1,0:T(8,128)}, u32[]{:S(2)}) copy-start(f32[60,384]{1,0:T(8,128)} %copy-done.24) | copy-start | bytes 276484
  345.2 13.1 %copy-start.21 = (f32[3072]{0:T(1024)S(1)}, f32[3072]{0:T(1024)}, u32[]{:S(2)}) copy-start(f32[3072]{0:T(1024)} %copy-done.20) | copy-start | bytes 36868
  345.2 13.1 %copy-start.55 = (pred[3072]{0:T(1024)(128)(4,1)S(1)}, pred[3072]{0:T(1024)(128)(4,1)}, u32[]{:S(2)}) copy-start(pred[3072]{0:T(1024)(128)(4,1)} %copy-done.54) | copy-start | bytes 9220
  362.1 15.8 %collective-permute-start.12 = (f32[60,384]{1,0:T(8,128)}, f32[60,384]{1,0:T(8,128)}, u32[]{:S(2)}, u32[]{:S(2)}) collective-permute-start(f32[60,384]{1,0:T(8,128)} %bitcast.165), channel_id=1, source_target_pairs={{0,16},{16,32},{32,48},{48,64},{64,80},{80,96},{96,112},{1,17},{17... | collective-permute-start | bytes 276488 | tf_op jit(solution)/shard_map/ppermute | solution.py:15
  367.4 14.8 %collective-permute-start.15 = (f32[60,384]{1,0:T(8,128)}, f32[60,384]{1,0:T(8,128)S(1)}, u32[]{:S(2)}, u32[]{:S(2)}) collective-permute-start(f32[60,384]{1,0:T(8,128)} %bitcast.40), channel_id=1, source_target_pairs={{0,16},{16,32},{32,48},{48,64},{64,80},{80,96},{96,112},{1,17},{17... | collective-permute-start | bytes 276488 | tf_op jit(solution)/shard_map/ppermute | solution.py:15
  369.4 15.5 %collective-permute-start.19 = (f32[60,384]{1,0:T(8,128)S(1)}, f32[60,384]{1,0:T(8,128)}, u32[]{:S(2)}, u32[]{:S(2)}) collective-permute-start(f32[60,384]{1,0:T(8,128)S(1)} %bitcast.164), channel_id=1, source_target_pairs={{16,0},{32,16},{48,32},{64,48},{80,64},{96,80},{112,96},{17,1},{33... | collective-permute-start | bytes 276488 | tf_op jit(solution)/shard_map/ppermute | solution.py:15
  371.9 14.9 %collective-permute-start.22 = (f32[60,384]{1,0:T(8,128)S(1)}, f32[60,384]{1,0:T(8,128)}, u32[]{:S(2)}, u32[]{:S(2)}) collective-permute-start(f32[60,384]{1,0:T(8,128)S(1)} %bitcast.163), channel_id=1, source_target_pairs={{16,0},{32,16},{48,32},{64,48},{80,64},{96,80},{112,96},{17,1},{33... | collective-permute-start | bytes 276488 | tf_op jit(solution)/shard_map/ppermute | solution.py:15
  374.0 17.7 %collective-permute-start.14 = (f32[60,384]{1,0:T(8,128)S(1)}, f32[60,384]{1,0:T(8,128)S(1)}, u32[]{:S(2)}, u32[]{:S(2)}) collective-permute-start(f32[60,384]{1,0:T(8,128)S(1)} %bitcast.162), channel_id=1, source_target_pairs={{0,16},{16,32},{32,48},{48,64},{64,80},{80,96},{96,112},{1,17},{17... | collective-permute-start | bytes 276488 | tf_op jit(solution)/shard_map/ppermute | solution.py:15
  377.9 15.1 %collective-permute-start.17 = (f32[60,384]{1,0:T(8,128)S(1)}, f32[60,384]{1,0:T(8,128)S(1)}, u32[]{:S(2)}, u32[]{:S(2)}) collective-permute-start(f32[60,384]{1,0:T(8,128)S(1)} %bitcast.161), channel_id=1, source_target_pairs={{0,1},{1,2},{2,3},{3,4},{4,5},{5,6},{6,7},{7,8},{8,9},{9,10},{10,1... | collective-permute-start | bytes 276488 | tf_op jit(solution)/shard_map/ppermute | solution.py:15
  382.8 17.2 %collective-permute-start.18 = (f32[60,384]{1,0:T(8,128)S(1)}, f32[60,384]{1,0:T(8,128)S(1)}, u32[]{:S(2)}, u32[]{:S(2)}) collective-permute-start(f32[60,384]{1,0:T(8,128)S(1)} %bitcast.157), channel_id=1, source_target_pairs={{1,0},{2,1},{3,2},{4,3},{5,4},{6,5},{7,6},{8,7},{9,8},{10,9},{11,1... | collective-permute-start | bytes 276488 | tf_op jit(solution)/shard_map/ppermute | solution.py:15
  384.9 25.8 %collective-permute-start.21 = (f32[60,384]{1,0:T(8,128)}, f32[60,384]{1,0:T(8,128)S(1)}, u32[]{:S(2)}, u32[]{:S(2)}) collective-permute-start(f32[60,384]{1,0:T(8,128)} %bitcast.44), channel_id=1, source_target_pairs={{16,0},{32,16},{48,32},{64,48},{80,64},{96,80},{112,96},{17,1},{33... | collective-permute-start | bytes 276488 | tf_op jit(solution)/shard_map/ppermute | solution.py:15
  386.8 23.9 %collective-permute-start.13 = (f32[60,384]{1,0:T(8,128)}, f32[60,384]{1,0:T(8,128)S(1)}, u32[]{:S(2)}, u32[]{:S(2)}) collective-permute-start(f32[60,384]{1,0:T(8,128)} %collective-permute-done.12), channel_id=1, source_target_pairs={{0,1},{1,2},{2,3},{3,4},{4,5},{5,6},{6,7},{7,8},{8,9},{9,10},{10,1... | collective-permute-start | bytes 276488 | tf_op jit(solution)/shard_map/ppermute | solution.py:15
  391.7 19.1 %collective-permute-start.16 = (f32[60,384]{1,0:T(8,128)}, f32[60,384]{1,0:T(8,128)S(1)}, u32[]{:S(2)}, u32[]{:S(2)}) collective-permute-start(f32[60,384]{1,0:T(8,128)} %copy-done.57), channel_id=1, source_target_pairs={{1,0},{2,1},{3,2},{4,3},{5,4},{6,5},{7,6},{8,7},{9,8},{10,9},{11,1... | collective-permute-start | bytes 276488 | tf_op jit(solution)/shard_map/ppermute | solution.py:15
  393.0 17.9 %collective-permute-start.20 = (f32[60,384]{1,0:T(8,128)}, f32[60,384]{1,0:T(8,128)}, u32[]{:S(2)}, u32[]{:S(2)}) collective-permute-start(f32[60,384]{1,0:T(8,128)} %collective-permute-done.19), channel_id=1, source_target_pairs={{0,1},{1,2},{2,3},{3,4},{4,5},{5,6},{6,7},{7,8},{8,9},{9,10},{10,1... | collective-permute-start | bytes 276488 | tf_op jit(solution)/shard_map/ppermute | solution.py:15
  400.0 11.8 %collective-permute-start.23 = (f32[60,384]{1,0:T(8,128)}, f32[60,384]{1,0:T(8,128)}, u32[]{:S(2)}, u32[]{:S(2)}) collective-permute-start(f32[60,384]{1,0:T(8,128)} %collective-permute-done.22), channel_id=1, source_target_pairs={{1,0},{2,1},{3,2},{4,3},{5,4},{6,5},{7,6},{8,7},{9,8},{10,9},{11,1... | collective-permute-start | bytes 276488 | tf_op jit(solution)/shard_map/ppermute | solution.py:15
  402.7 4.5 copy-start.4
  414.7 4.6 copy-start.10
  419.3 30.5 %copy-start.27 = (pred[8192]{0:T(1024)(128)(4,1)S(1)}, pred[8192]{0:T(1024)(128)(4,1)}, u32[]{:S(2)}) copy-start(pred[8192]{0:T(1024)(128)(4,1)} %copy-done.26) | copy-start | bytes 24580
  473.1 3.9 copy-start.31
  473.1 3.9 copy-start.43
  494.9 174.0 %copy-start.1 = (f32[120,2048]{1,0:T(8,128)S(1)}, f32[120,2048]{1,0:T(8,128)}, u32[]{:S(2)}) copy-start(f32[120,2048]{1,0:T(8,128)} %copy-done) | copy-start | bytes 2949124
  494.9 174.0 %copy-start.2 = (f32[120,2048]{1,0:T(8,128)S(1)}, f32[120,2048]{1,0:T(8,128)}, u32[]{:S(2)}) copy-start(f32[120,2048]{1,0:T(8,128)} %param.35) | copy-start | bytes 2949124
  (34 other events, 93.3 us)

commit v2 on v0

v2 whole, which is shorter than its diff:
```python
import functools

import jax
import jax.numpy as jnp
import numpy as np
from jax import lax
from jax.experimental import pallas as pl
from jax.experimental.pallas import tpu as pltpu
from jax.sharding import PartitionSpec as P

EPSILON = 1e-06
PERMUTATIONS = ((0, 1, 2), (0, 2, 1), (1, 0, 2), (1, 2, 0), (2, 0, 1), (2, 1, 0))
OFFSETS = tuple(((direction // 3 - 1, direction % 3 - 1) for direction in (0, 1, 2, 3, 5, 6, 7, 8)))
MESH = pl.DeviceIdType.MESH
F32, BF16, I32 = jnp.float32, jnp.bfloat16, jnp.int32
VMEM_LIMIT = 48 * 1024 * 1024
UNK, CLASSES, LANES = 120, 256, 128
TILE = 16
COMP = 16
SIDE = 6 * COMP
LANE_BLOCK = 256


def trace_tables():
    element_points = [
        (coord_a, coord_b, coord_c, 3 - coord_a - coord_b - coord_c)
        for coord_a in range(4)
        for coord_b in range(4 - coord_a)
        for coord_c in range(4 - coord_a - coord_b)
    ]
    face_points = [
        (coord_a, coord_b, 3 - coord_a - coord_b)
        for coord_a in range(4)
        for coord_b in range(4 - coord_a)
    ]
    select_rows = []
    for opposite in range(4):
        corners = [vertex for vertex in range(4) if vertex != opposite]
        members = []
        for triple in face_points:
            coords = [0, 0, 0, 0]
            for position in range(3):
                coords[corners[position]] = triple[position]
            members.append(element_points.index(tuple(coords)))
        select_rows.append(members)
    turn_rows = [
        [
            face_points.index((triple[sigma_row[0]], triple[sigma_row[1]], triple[sigma_row[2]]))
            for triple in face_points
        ]
        for sigma_row in PERMUTATIONS
    ]
    return select_rows, turn_rows


def trace_selector():
    select_rows, _ = trace_tables()
    table = np.zeros((2 * LANES, 4 * LANES), np.float32)
    for side in range(4):
        for half in range(2):
            for c in range(6):
                for j in range(10):
                    column = side * LANES + half * 64 + c * 10 + j
                    table[c * 20 + select_rows[side][j], column] = 1.0
                    table[LANES + c * 20 + select_rows[side][j], column] = 1.0
    return table


def turn_selector():
    _, turn_rows = trace_tables()
    table = np.zeros((2, 6, SIDE, 2 * LANES), np.float32)
    for half in range(2):
        for option in range(6):
            for c in range(6):
                for j in range(10):
                    source = half * 64 + c * 10 + turn_rows[option][j]
                    table[half, option, c * COMP + j, source] = 1.0
                    table[half, option, c * COMP + j, LANES + source] = 1.0
    return table.reshape(2 * 6 * SIDE, 2 * LANES)


def lift_spreaders():
    rows = np.zeros((LANES, 20), np.float32)
    columns = np.zeros((4, 10, 4 * SIDE), np.float32)
    mask = np.zeros((LANES, 4 * SIDE), np.float32)
    for c in range(6):
        for i in range(20):
            rows[c * 20 + i, i] = 1.0
        for s in range(4):
            for j in range(10):
                columns[s, j, s * SIDE + c * COMP + j] = 1.0
            mask[c * 20 : c * 20 + 20, s * SIDE + c * COMP : s * SIDE + (c + 1) * COMP] = 1.0
    return rows, columns, mask


def split(value):
    high = value.astype(BF16)
    return high, (value - high.astype(F32)).astype(BF16)


def dot(a, b, dims=(((1,), (0,)), ((), ()))):
    return lax.dot_general(a, b, dims, preferred_element_type=F32)


NT = (((1,), (1,)), ((), ()))


def live_lanes(count, first, width):
    return ((lax.broadcasted_iota(I32, (1, width), 1) + first) < count).astype(F32)


def prep_kernel(
    count_ref, field_ref, class_ref, lift_ref, spread_ref, column_ref, mask_ref,
    rows_ref, pos_ref, tile_ref, lift_hi_ref, lift_lo_ref,
):
    elements = field_ref.shape[1]
    blocks = elements // LANES
    count = count_ref[0]
    for block in range(blocks):
        lanes = slice(block * LANES, (block + 1) * LANES)
        value = field_ref[:, lanes] * live_lanes(count, block * LANES, LANES)
        value = jnp.concatenate([value, jnp.zeros((LANES - UNK, LANES), F32)], axis=0)
        rows_ref[lanes, :] = value.T

    class_row = lax.broadcasted_iota(I32, (CLASSES, LANES), 0)
    totals = jnp.zeros((CLASSES, LANES), F32)
    for block in range(blocks):
        totals = totals + (class_ref[block : block + 1, :] == class_row).astype(F32)
    total = jnp.sum(totals, axis=1, keepdims=True)
    tiles = jnp.floor((total + (TILE - 1)) * (1.0 / TILE))
    tiles = jnp.broadcast_to(tiles, (CLASSES, LANES))
    lower = (
        lax.broadcasted_iota(I32, (CLASSES, CLASSES), 1)
        < lax.broadcasted_iota(I32, (CLASSES, CLASSES), 0)
    ).astype(BF16)
    start = dot(lower, tiles.astype(BF16))
    end = start + tiles
    earlier = (
        lax.broadcasted_iota(I32, (LANES, 2 * LANES), 0)
        < lax.broadcasted_iota(I32, (LANES, 2 * LANES), 1)
    ).astype(BF16)
    carry = start * TILE
    for block in range(blocks):
        member = (class_ref[block : block + 1, :] == class_row).astype(F32)
        ranks = dot(member.astype(BF16), earlier)
        position = jnp.sum(member * (ranks[:, :LANES] + carry), axis=0, keepdims=True)
        pos_ref[block : block + 1, :] = position.astype(I32)
        carry = carry + ranks[:, LANES:]
    for row in range(3):
        tile = (lax.broadcasted_iota(I32, (CLASSES, LANES), 1) + row * LANES).astype(F32)
        owner = jnp.sum((end <= tile).astype(F32), axis=0, keepdims=True)
        tile_ref[row : row + 1, :] = jnp.minimum(owner.astype(I32), CLASSES - 1)
    tile_ref[3:4, :] = end[CLASSES - 1 :, :].astype(I32)
    tile_ref[4:, :] = jnp.zeros((4, LANES), I32)

    spread = jnp.zeros((LANES, 4 * SIDE), F32)
    for side in range(4):
        rows = lax.dot_general(
            spread_ref[...], lift_ref[side], (((1,), (0,)), ((), ())),
            precision=lax.Precision.HIGHEST, preferred_element_type=F32,
        )
        spread = spread + lax.dot_general(
            rows, column_ref[side], (((1,), (0,)), ((), ())),
            precision=lax.Precision.HIGHEST, preferred_element_type=F32,
        )
    high, low = split(spread * mask_ref[...])
    lift_hi_ref[...] = high
    lift_lo_ref[...] = low


def prepare(part_count, right_side, elem_class, lift):
    elements = right_side.shape[1]
    rows, columns, mask = lift_spreaders()
    vmem = pl.BlockSpec(memory_space=pltpu.VMEM)
    return pl.pallas_call(
        prep_kernel,
        out_shape=(
            jax.ShapeDtypeStruct((elements, LANES), F32),
            jax.ShapeDtypeStruct((elements // LANES, LANES), I32),
            jax.ShapeDtypeStruct((8, LANES), I32),
            jax.ShapeDtypeStruct((LANES, 4 * SIDE), BF16),
            jax.ShapeDtypeStruct((LANES, 4 * SIDE), BF16),
        ),
        in_specs=[pl.BlockSpec(memory_space=pltpu.SMEM)] + [vmem] * 6,
        out_specs=(vmem,) * 5,
        compiler_params=pltpu.CompilerParams(vmem_limit_bytes=VMEM_LIMIT),
        name="prepare",
    )(
        part_count, right_side, elem_class.reshape(elements // LANES, LANES), lift,
        jnp.asarray(rows), jnp.asarray(columns), jnp.asarray(mask),
    )


def write_traces(rows_ref, selector_ref, table_ref, first):
    elements = rows_ref.shape[0]

    def block(index, carry):
        base = pl.multiple_of(index * LANES, LANES)
        high, low = split(rows_ref[pl.ds(base, LANES), :])
        traces = dot(jnp.concatenate([high, low], axis=1), selector_ref[...])
        for side in range(4):
            table_ref[pl.ds(first + side * elements + base, LANES), :] = traces[
                :, side * LANES : (side + 1) * LANES
            ]
        return carry

    lax.fori_loop(0, elements // LANES, block, 0)


def gather_pairs(table_ref, index_ref, out_ref, first_a, first_b, out_first, count):
    left = lax.broadcasted_iota(I32, (1, LANES), 1) < 64
    unroll = 16

    def block(index, carry):
        base = pl.multiple_of(index * unroll, unroll)
        for step in range(unroll):
            row_a = table_ref[pl.ds(index_ref[first_a + base + step], 1), :]
            row_b = table_ref[pl.ds(index_ref[first_b + base + step], 1), :]
            out_ref[pl.ds(out_first + base + step, 1), :] = jnp.where(left, row_a, row_b)
        return carry

    lax.fori_loop(0, count // unroll, block, 0)


def exchange_kernel(
    grid_rows, grid_columns, rows_ref, selector_ref, list_ref, received_ref,
    table_ref, outgoing_ref, send_sem, recv_sem,
):
    slots = outgoing_ref.shape[1]
    row, column = lax.axis_index("prow"), lax.axis_index("pcol")

    def present(index):
        a, b = OFFSETS[index]
        inside = None
        for at, step, size in ((row, a, grid_rows), (column, b, grid_columns)):
            if step == 0:
                continue
            term = at > 0 if step < 0 else at < size - 1
            inside = term if inside is None else jnp.logical_and(inside, term)
        return inside

    def partner(index):
        a, b = OFFSETS[index]
        return (row + a, column + b)

    def transfer(index):
        return pltpu.make_async_remote_copy(
            src_ref=outgoing_ref.at[index],
            dst_ref=received_ref.at[7 - index],
            send_sem=send_sem.at[index],
            recv_sem=recv_sem.at[7 - index],
            device_id=partner(index),
            device_id_type=MESH,
        )

    barrier = pltpu.get_barrier_semaphore()
    for index in range(8):
        @pl.when(present(index))
        def _(index=index):
            pl.semaphore_signal(barrier, inc=1, device_id=partner(index), device_id_type=MESH)

    write_traces(rows_ref, selector_ref, table_ref, 0)

    near_rows = 1 + (row > 0).astype(I32) + (row < grid_rows - 1).astype(I32)
    near_columns = 1 + (column > 0).astype(I32) + (column < grid_columns - 1).astype(I32)
    pl.semaphore_wait(barrier, near_rows * near_columns - 1)

    for index in (0, 2, 5, 7, 3, 4, 1, 6):
        first = index * 2 * slots
        gather_pairs(
            table_ref, list_ref, outgoing_ref.at[index], first, first + slots, 0, slots
        )

        @pl.when(present(index))
        def _(index=index):
            transfer(index).start()

    for index in range(8):
        @pl.when(present(index))
        def _(index=index):
            transfer(index).wait_send()
            transfer(7 - index).wait_recv()


def exchange(rows, selector, lists):
    slots = lists.shape[0] // 16
    vmem = pl.BlockSpec(memory_space=pltpu.VMEM)
    return pl.pallas_call(
        functools.partial(exchange_kernel, lax.axis_size("prow"), lax.axis_size("pcol")),
        out_shape=jax.ShapeDtypeStruct((8, slots, LANES), F32),
        in_specs=[vmem, vmem, pl.BlockSpec(memory_space=pltpu.SMEM)],
        out_specs=vmem,
        scratch_shapes=[
            pltpu.VMEM((4 * rows.shape[0], LANES), F32),
            pltpu.VMEM((8, slots, LANES), F32),
            pltpu.SemaphoreType.DMA((8,)),
            pltpu.SemaphoreType.DMA((8,)),
        ],
        compiler_params=pltpu.CompilerParams(
            collective_id=0, has_side_effects=True, vmem_limit_bytes=VMEM_LIMIT
        ),
        name="exchange",
    )(rows, selector, lists)


def face_flux(nodes, normal, scale, sign):
    electric = [nodes[c * COMP : (c + 1) * COMP] * sign for c in range(3)]
    magnetic = [nodes[(3 + c) * COMP : (4 + c) * COMP] for c in range(3)]
    along_e = normal[0] * electric[0] + normal[1] * electric[1] + normal[2] * electric[2]
    along_h = normal[0] * magnetic[0] + normal[1] * magnetic[1] + normal[2] * magnetic[2]
    flux = []
    for c in range(3):
        a, b = (c + 1) % 3, (c + 2) % 3
        cross = normal[a] * magnetic[b] - normal[b] * magnetic[a]
        flux.append(scale * (electric[c] - normal[c] * along_e - cross))
    for c in range(3):
        a, b = (c + 1) % 3, (c + 2) % 3
        cross = normal[a] * electric[b] - normal[b] * electric[a]
        flux.append(scale * (magnetic[c] - normal[c] * along_h + cross))
    return jnp.concatenate(flux, axis=0)


def image_kernel(
    count_ref, index_ref, pos_ref, tile_ref,
    rows_ref, received_ref, selector_ref, turn_ref, lift_hi_ref, lift_lo_ref,
    link_ref, orient_ref, normal_ref, quotient_ref, inverse_hbm,
    image_ref,
    table_ref, picked_ref, coupled_ref, sorted_ref, solved_ref, inverse_ref, inverse_sem,
):
    elements = rows_ref.shape[0]
    remote = received_ref.shape[0] * 2
    inverse_copy = pltpu.make_async_copy(inverse_hbm, inverse_ref, inverse_sem)
    inverse_copy.start()

    write_traces(rows_ref, selector_ref, table_ref, remote)

    slots = remote // 16
    left = lax.broadcasted_iota(I32, (slots, LANES), 1) < 64
    for index in range(8):
        packed = received_ref[index * slots : (index + 1) * slots, :]
        swapped = pltpu.roll(packed, 64, 1)
        first = index * 2 * slots
        table_ref[first : first + slots, :] = jnp.where(left, packed, swapped)
        table_ref[first + slots : first + 2 * slots, :] = jnp.where(left, swapped, packed)

    gather_pairs(table_ref, index_ref, picked_ref, 0, 2 * elements, 0, 2 * elements)

    count = count_ref[0]

    def lane_block(index, carry):
        base = pl.multiple_of(index * LANE_BLOCK, LANE_BLOCK)
        alive = ((lax.broadcasted_iota(I32, (1, LANE_BLOCK), 1) + base) < count).astype(F32)
        fluxes = [None] * 4
        for pair in range(2):
            high, low = split(picked_ref[pl.ds(pair * elements + base, LANE_BLOCK), :])
            stacked = jnp.concatenate([high, low], axis=1)
            for half in range(2):
                side = pair + 2 * half
                lanes = pl.ds(side * elements + base, LANE_BLOCK)
                turned = dot(turn_ref[half * 6 * SIDE : (half + 1) * 6 * SIDE, :], stacked, NT)
                orient = orient_ref[:, lanes]
                nodes = turned[:SIDE]
                for option in range(1, 6):
                    nodes = jnp.where(
                        orient == option, turned[option * SIDE : (option + 1) * SIDE], nodes
                    )
                scale = 0.5 * quotient_ref[:, lanes] * alive
                sign = jnp.where(link_ref[:, lanes] < 0, -1.0, 1.0)
                normal = [normal_ref[c : c + 1, lanes] for c in range(3)]
                fluxes[side] = face_flux(nodes, normal, scale, sign)
        high, low = split(jnp.concatenate(fluxes, axis=0))
        coupled = dot(lift_hi_ref[...], high) + dot(lift_hi_ref[...], low) + dot(lift_lo_ref[...], high)
        coupled_ref[pl.ds(base, LANE_BLOCK), :] = coupled.T
        return carry

    lax.fori_loop(0, elements // LANE_BLOCK, lane_block, 0)

    unroll = 16

    def place(index, carry):
        base = pl.multiple_of(index * unroll, unroll)
        for step in range(unroll):
            sorted_ref[pl.ds(pos_ref[base + step], 1), :] = coupled_ref[pl.ds(base + step, 1), :]
        return carry

    lax.fori_loop(0, elements // unroll, place, 0)
    inverse_copy.wait()

    def solve(index, carry):
        base = pl.multiple_of(index * TILE, TILE)
        high, low = split(sorted_ref[pl.ds(base, TILE), :])
        both = jnp.concatenate([high, low], axis=0)[:, :UNK]
        result = dot(both, inverse_ref[tile_ref[index]], NT)
        solved_ref[pl.ds(base, TILE), :UNK] = result[:TILE] + result[TILE:]
        return carry

    group = 4
    groups = (tile_ref[3 * LANES] + (group - 1)) // group

    def solve_group(index, carry):
        for step in range(group):
            solve(index * group + step, 0)
        return carry

    lax.fori_loop(0, groups, solve_group, 0)

    keep = lax.broadcasted_iota(I32, (1, LANES), 1) < UNK

    def fetch(index, carry):
        base = pl.multiple_of(index * unroll, unroll)
        for step in range(unroll):
            value = solved_ref[pl.ds(pos_ref[base + step], 1), :]
            image_ref[pl.ds(base + step, 1), :] = jnp.where(keep, value, 0.0)
        return carry

    lax.fori_loop(0, elements // unroll, fetch, 0)


def image(part_count, indices, pos, tiles, rows, received, selector, turns, lift_hi, lift_lo,
          link, orient, normal, quotient, inverse_table):
    elements = rows.shape[0]
    remote = received.shape[0] * received.shape[1] * 2
    slots = 3 * LANES * TILE
    vmem = pl.BlockSpec(memory_space=pltpu.VMEM)
    smem = pl.BlockSpec(memory_space=pltpu.SMEM)
    return pl.pallas_call(
        image_kernel,
        out_shape=jax.ShapeDtypeStruct((elements, LANES), F32),
        in_specs=[smem] * 4 + [vmem] * 10 + [pl.BlockSpec(memory_space=pl.ANY)],
        out_specs=vmem,
        scratch_shapes=[
            pltpu.VMEM((remote + 4 * elements, LANES), F32),
            pltpu.VMEM((2 * elements, LANES), F32),
            pltpu.VMEM((elements, LANES), F32),
            pltpu.VMEM((slots, LANES), F32),
            pltpu.VMEM((slots, LANES), F32),
            pltpu.VMEM(inverse_table.shape, BF16),
            pltpu.SemaphoreType.DMA(()),
        ],
        compiler_params=pltpu.CompilerParams(vmem_limit_bytes=VMEM_LIMIT),
        name="image",
    )(
        part_count, indices, pos, tiles, rows, received.reshape(-1, LANES), selector, turns,
        lift_hi, lift_lo, link.reshape(1, -1), orient.reshape(1, -1), normal,
        quotient.reshape(1, -1), inverse_table,
    )


def gram_kernel(first_ref, second_ref, third_ref, second_out, third_out, gram_ref):
    elements = first_ref.shape[0]

    def block(index, sums):
        base = pl.multiple_of(index * LANES, LANES)
        lanes = pl.ds(base, LANES)
        f, t, u = first_ref[lanes, :], second_ref[lanes, :], third_ref[lanes, :]
        second_out[:, lanes] = t.T[:UNK]
        third_out[:, lanes] = u.T[:UNK]
        pairs = (f * f, f * t, t * t, f * u, t * u, u * u)
        return tuple(
            total + jnp.sum(pair.reshape(LANES // 8, 8, LANES), axis=0)
            for total, pair in zip(sums, pairs)
        )

    zero = jnp.zeros((8, LANES), F32)
    sums = lax.fori_loop(0, elements // LANES, block, (zero,) * 6)
    for index in range(6):
        gram_ref[index : index + 1, :] = jnp.sum(sums[index], axis=0, keepdims=True)
    gram_ref[6:, :] = jnp.zeros((2, LANES), F32)


def gram_partials(first, second, third):
    elements = first.shape[0]
    vmem = pl.BlockSpec(memory_space=pltpu.VMEM)
    return pl.pallas_call(
        gram_kernel,
        out_shape=(
            jax.ShapeDtypeStruct((UNK, elements), F32),
            jax.ShapeDtypeStruct((UNK, elements), F32),
            jax.ShapeDtypeStruct((8, LANES), F32),
        ),
        in_specs=[vmem] * 3,
        out_specs=(vmem,) * 3,
        compiler_params=pltpu.CompilerParams(vmem_limit_bytes=VMEM_LIMIT),
        name="gram",
    )(first, second, third)


def total_kernel(grid_rows, grid_columns, part_ref, total_ref, over_rows, over_columns,
                 send_row, recv_row, send_column, recv_column):
    row, column = lax.axis_index("prow"), lax.axis_index("pcol")

    def row_partner(step):
        return lax.rem(row + step, grid_rows)

    def column_partner(step):
        return lax.rem(column + step, grid_columns)

    barrier = pltpu.get_barrier_semaphore()
    for step in range(1, grid_rows):
        pl.semaphore_signal(
            barrier, inc=1, device_id=(row_partner(step), column), device_id_type=MESH
        )
    for step in range(1, grid_columns):
        pl.semaphore_signal(
            barrier, inc=1, device_id=(row, column_partner(step)), device_id_type=MESH
        )
    pl.semaphore_wait(barrier, grid_rows + grid_columns - 2)

    def row_copy(step):
        return pltpu.make_async_remote_copy(
            src_ref=part_ref,
            dst_ref=over_rows.at[step],
            send_sem=send_row.at[step],
            recv_sem=recv_row.at[step],
            device_id=(row_partner(step), column),
            device_id_type=MESH,
        )

    for step in range(1, grid_rows):
        row_copy(step).start()
    over_rows[0] = part_ref[...]
    for step in range(1, grid_rows):
        row_copy(step).wait()
    total = over_rows[row]
    for source in range(1, grid_rows):
        total = total + over_rows[lax.rem(row - source + grid_rows, grid_rows)]
    over_columns[0] = total

    def column_copy(step):
        return pltpu.make_async_remote_copy(
            src_ref=over_columns.at[0],
            dst_ref=over_columns.at[step],
            send_sem=send_column.at[step],
            recv_sem=recv_column.at[step],
            device_id=(row, column_partner(step)),
            device_id_type=MESH,
        )

    for step in range(1, grid_columns):
        column_copy(step).start()
    for step in range(1, grid_columns):
        column_copy(step).wait()
    total = over_columns[column]
    for source in range(1, grid_columns):
        total = total + over_columns[lax.rem(column - source + grid_columns, grid_columns)]
    total_ref[...] = total


def total_over_devices(part):
    grid_rows, grid_columns = lax.axis_size("prow"), lax.axis_size("pcol")
    vmem = pl.BlockSpec(memory_space=pltpu.VMEM)
    return pl.pallas_call(
        functools.partial(total_kernel, grid_rows, grid_columns),
        out_shape=jax.ShapeDtypeStruct(part.shape, F32),
        in_specs=[vmem],
        out_specs=vmem,
        scratch_shapes=[
            pltpu.VMEM((grid_rows,) + part.shape, F32),
            pltpu.VMEM((grid_columns,) + part.shape, F32),
            pltpu.SemaphoreType.DMA((grid_rows,)),
            pltpu.SemaphoreType.DMA((grid_rows,)),
            pltpu.SemaphoreType.DMA((grid_columns,)),
            pltpu.SemaphoreType.DMA((grid_columns,)),
        ],
        compiler_params=pltpu.CompilerParams(collective_id=1, has_side_effects=True),
        name="total",
    )(part)


def finish_kernel(weight, count_ref, total_ref, field_ref, second_ref, third_ref, basis_ref, hess_ref):
    width = field_ref.shape[1]
    gram = jnp.sum(total_ref[...], axis=1, keepdims=True) * weight
    ff, ft, tt, fu, tu, uu = (gram[index : index + 1, :] for index in range(6))
    beta = jnp.sqrt(ff + EPSILON)
    square = beta * beta
    h00 = (ff + ft) / square
    p = (EPSILON - ft) / square
    h10 = jnp.sqrt((tt + 2 * p * ft + p * p * ff) / square + EPSILON)
    k1 = 1.0 / (beta * h10)
    h01 = k1 / beta * (fu + (1 + p) * ft + p * ff)
    h11 = k1 * k1 * (tu + (1 + p) * tt + p * ft + p * fu + p * (1 + p) * ft + p * p * ff)
    q = 1 + p - h11
    w = p * (1 - h11) - h01 * h10
    h21 = jnp.sqrt(
        k1 * k1 * (uu + 2 * q * tu + 2 * w * fu + q * q * tt + 2 * q * w * ft + w * w * ff)
        + EPSILON
    )
    k2 = k1 / h21

    alive = live_lanes(count_ref[0], pl.program_id(0) * width, width)
    f = field_ref[...] * alive
    t = second_ref[...]
    basis_ref[0] = f * (1.0 / beta)
    basis_ref[1] = t * k1 + f * (p * k1)
    basis_ref[2] = third_ref[...] * k2 + t * (q * k2) + f * (w * k2)

    at_row = lax.broadcasted_iota(I32, (3, 2), 0)
    at_column = lax.broadcasted_iota(I32, (3, 2), 1)
    hess = jnp.zeros((3, 2), F32)
    for i, j, value in ((0, 0, h00), (1, 0, h10), (0, 1, h01), (1, 1, h11), (2, 1, h21)):
        hess = jnp.where(jnp.logical_and(at_row == i, at_column == j), value, hess)
    hess_ref[...] = hess


def finish(weight, part_count, total, right_side, second, third):
    elements = right_side.shape[1]
    width = 512
    field = pl.BlockSpec((UNK, width), lambda i: (0, i))
    return pl.pallas_call(
        functools.partial(finish_kernel, weight),
        grid=(elements // width,),
        out_shape=(
            jax.ShapeDtypeStruct((3, UNK, elements), F32),
            jax.ShapeDtypeStruct((3, 2), F32),
        ),
        in_specs=[
            pl.BlockSpec(memory_space=pltpu.SMEM),
            pl.BlockSpec((8, LANES), lambda i: (0, 0)),
            field, field, field,
        ],
        out_specs=(
            pl.BlockSpec((3, UNK, width), lambda i: (0, 0, i)),
            pl.BlockSpec((3, 2), lambda i: (0, 0)),
        ),
        compiler_params=pltpu.CompilerParams(vmem_limit_bytes=VMEM_LIMIT),
        name="finish",
    )(part_count, total, right_side, second, third)


def shards(
    right_side,
    part_count,
    elem_class,
    face_link,
    face_orient,
    face_normal,
    boundary_metric_quotient,
    bound_face,
    lift,
    inverse_table,
):
    unknowns, elements = right_side.shape
    all_subdomains = lax.axis_size("prow") * lax.axis_size("pcol")
    weight = 1.0 / (unknowns * elements * all_subdomains)
    lists = jnp.maximum(bound_face.reshape(-1), 0)
    remote = lists.shape[0]
    faces = face_link.shape[0]
    indices = jnp.where(face_link < 0, jnp.arange(faces, dtype=I32) + remote, face_link)
    selector = jnp.asarray(trace_selector(), BF16)
    turns = jnp.asarray(turn_selector(), BF16)

    first, pos, tiles, lift_hi, lift_lo = prepare(part_count, right_side, elem_class, lift)
    pos, tiles = pos.reshape(-1), tiles.reshape(-1)

    def coupled_image(rows):
        received = exchange(rows, selector, lists)
        return image(
            part_count, indices, pos, tiles, rows, received, selector, turns, lift_hi, lift_lo,
            face_link, face_orient, face_normal, boundary_metric_quotient, inverse_table,
        )

    second = coupled_image(first)
    third = coupled_image(second)
    second_columns, third_columns, part = gram_partials(first, second, third)
    total = total_over_devices(part)
    return finish(weight, part_count, total, right_side, second_columns, third_columns)


def solution(mesh):
    in_specs = (
        P(None, ("prow", "pcol")),
        P(("prow", "pcol")),
        P(("prow", "pcol")),
        P(("prow", "pcol")),
        P(("prow", "pcol")),
        P(None, ("prow", "pcol")),
        P(("prow", "pcol")),
        P(("prow", "pcol"), None, None),
        P(),
        P(),
    )
    out_specs = (P(None, None, ("prow", "pcol")), P())
    return jax.shard_map(shards, mesh=mesh, in_specs=in_specs, out_specs=out_specs, check_vma=False)
```

time: 1050 us -> 151 us (0.14)
  local copies, waits for them, and re-layouts: 372 us -> 21.1 us
  blocking collectives: 339 us -> 0 us
  other arithmetic: 210 us -> 1.47 us
  Pallas kernels: 0 us -> 126 us
  starting transfers between devices: 58.9 us -> 0 us
  matrix products: 52 us -> 0 us
    psum x5 -> x0, blocking collectives: 339 us -> none  [the longest x2 144 us: shards(): coefficients = lax.psum(local_dots, ('prow', 'pcol'))]
    gather x22 -> x0, local copies, waits for them, and re-layouts: 284 us -> none  [the longest x16 191 us: one_block(): gathered = jnp.take(inverse_table, block_class, axis=0)]
    while x32 -> x0, other arithmetic: 134 us -> none
    pallas_call x0 -> x8, Pallas kernels: none -> 126 us  [the longest x2 74 us: image(): pl.pallas_call(image_kernel, out_shape=jax.ShapeDtypeStruct((elements, LA...]
    ppermute x24 -> x0, starting transfers between devices: 58.9 us -> none  [passed_along(): lax.ppermute(value, axis, [(source, source + steps) for source in range(l...]
    dot_general x14 -> x0, matrix products: 52 us -> none  [the longest x12 43.5 us: neighbour_traces(): jnp.einsum('jk,ckf->cjf', turn_tables[option], shaped, precision=lax.Prec...]
    reshape x6 -> x0, local copies, waits for them, and re-layouts: 18.4 us -> none  [the longest x4 13.1 us: shards(): own_traces = current[trace_index].reshape(60, 4 * elements)]
    select_n x2 -> x1, other arithmetic: 15 us -> 0.76 us  [shards(): jnp.where(face_link < 0, jnp.arange(faces, dtype=I32) + remote, face_link)]
  transfers between devices with their start and end apart: 24 -> 0, of which waited for: 0 -> 0; matrix products, arithmetic and copies ran while one was open for 4% -> 0% of each run, Pallas kernels for 0% -> 0%
where the time goes in v2:
time: 151 us; the launch traced here: 150 us
  Pallas kernels  126 us (83%)
  local copies, waits for them, and re-layouts  21.1 us (14%)
    pallas_call x2, Pallas kernels, image(): pl.pallas_call(image_kernel, out_shape=jax.ShapeDtypeStruct((elements, LA...  74 us
    pallas_call x2, Pallas kernels, exchange(): pl.pallas_call(functools.partial(exchange_kernel, lax.axis_size('prow'),...  25.2 us
    unnamed x36, local copies, waits for them, and re-layouts  20.5 us
    pallas_call x1, Pallas kernels, total_over_devices(): pl.pallas_call(functools.partial(total_kernel, grid_rows, grid_columns),...  20 us

profile of v2, /device:TPU:1, one launch (start us, length us, event | category | flops | bytes accessed | tf_op | source)
XLA Modules:
  0.0 150.1 jit_solution(8837776798003621561)
XLA Ops:
  1.3 0.7 broadcast_maximum_fusion
  2.0 0.8 compare_select_fusion.index_ref
  2.8 0.8 copy.17.lift_ref
  3.6 0.0 copy-start.2
  3.6 1.2 copy-done.2
  4.8 0.0 copy-start.9
  4.8 0.9 copy-done.9
  5.7 0.0 copy-start.12
  5.7 0.9 copy-done.12
  6.6 0.0 copy-start.13
  6.6 0.8 copy-done.13
  7.5 0.0 copy-start.15
  7.5 0.7 copy-done.15
  8.2 2.4 %prepare.1 = (f32[2048,128]{1,0:T(8,128)S(1)}, s32[16,128]{1,0:T(8,128)S(1)}, s32[8,128]{1,0:T(8,128)S(1)}, bf16[128,384]{1,0:T(8,128)(2,1)S(1)}, bf16[128,384]{1,0:T(8,128)(2,1)S(1)}) custom-call(s32[1]{0:T(128)S(6)} %copy.21.count_ref, f32[120,2048]{1,0:T(8,128)S(1)} %copy-done.2, s32[16,128]{1,0:T(8,128)S(1)} %bitcast.20, ...), custom_call_target="tpu_custom_call" | custom-call | tf_op jit(solution)/shard_map/prepare/pallas_call | solution.py:175
  10.6 0.0 copy-start
  10.6 0.9 copy-done
  11.5 13.0 %exchange.2 = f32[8,192,128]{2,1,0:T(8,128)S(1)} custom-call(f32[2048,128]{1,0:T(8,128)S(1)} %get-tuple-element.10.rows_ref.first_ref, bf16[256,512]{1,0:T(8,128)(2,1)S(1)} %copy-done, s32[3072]{0:T(1024)S(1)} %max.10.list_ref), custom_call_target="tpu_custom_call" | custom-call | tf_op jit(solution)/shard_map/exchange/pallas_call | solution.py:288
  24.5 0.0 copy-start.1
  24.5 0.0 copy-start.4
  24.5 0.0 copy-start.7
  24.5 0.0 copy-start.8
  24.5 0.0 copy-start.10
  24.6 0.0 copy-start.11
  24.6 10.7 %copy.18.inverse_hbm = bf16[256,120,120]{2,1,0:T(8,128)(2,1)} copy(bf16[256,120,120]{0,2,1:T(8,128)(2,1)} %param.24) | data formatting | bytes 14745600 | tf_op args[9]
  35.2 0.0 copy-done.1
  35.2 0.0 copy-done.4
  35.2 0.0 copy-done.7
  35.2 0.0 copy-done.8
  35.3 0.0 copy-done.10
  35.3 0.0 copy-done.11
  35.3 37.0 %image.2.rows_ref.second_ref = f32[2048,128]{1,0:T(8,128)S(1)} custom-call(s32[1]{0:T(128)S(6)} %copy.21.count_ref, s32[8192]{0:T(1024)S(1)} %compare_select_fusion.index_ref, s32[2048]{0:T(1024)S(1)} %bitcast.16, s32[1024]{0:T(1024)S(1)} %bitcast.18, f32[2048,128]{1,0:T(8,128)S(1)} %get-tuple-element.10.rows_ref.first_ref, f32[1536,128]{1,0:T(8,128)S(1)} %bitcast.9, ...), custom_call_target="tpu_custom_call" | custom-call | tf_op jit(solution)/shard_map/image/pallas_call | solution.py:426
  72.3 12.3 %exchange.3 = f32[8,192,128]{2,1,0:T(8,128)S(1)} custom-call(f32[2048,128]{1,0:T(8,128)S(1)} %image.2.rows_ref.second_ref, bf16[256,512]{1,0:T(8,128)(2,1)S(1)} %copy-done.1, s32[3072]{0:T(1024)S(1)} %max.10.list_ref), custom_call_target="tpu_custom_call" | custom-call | tf_op jit(solution)/shard_map/exchange/pallas_call | solution.py:288
  84.5 0.0 copy-start.3
  84.6 37.0 %image.3.third_ref = f32[2048,128]{1,0:T(8,128)S(1)} custom-call(s32[1]{0:T(128)S(6)} %copy.21.count_ref, s32[8192]{0:T(1024)S(1)} %compare_select_fusion.index_ref, s32[2048]{0:T(1024)S(1)} %bitcast.17, s32[1024]{0:T(1024)S(1)} %bitcast.19, f32[2048,128]{1,0:T(8,128)S(1)} %image.2.rows_ref.second_ref, f32[1536,128]{1,0:T(8,128)S(1)} %bitcast.8, ...), custom_call_target="tpu_custom_call" | custom-call | tf_op jit(solution)/shard_map/image/pallas_call | solution.py:426
  121.6 1.6 %gram.1 = (f32[120,2048]{1,0:T(8,128)S(1)}, f32[120,2048]{1,0:T(8,128)S(1)}, f32[8,128]{1,0:T(8,128)S(1)}) custom-call(f32[2048,128]{1,0:T(8,128)S(1)} %get-tuple-element.10.rows_ref.first_ref, f32[2048,128]{1,0:T(8,128)S(1)} %image.2.rows_ref.second_ref, f32[2048,128]{1,0:T(8,128)S(1)} %image.3.third_ref), custom_call_target="tpu_custom_call" | custom-call | tf_op jit(solution)/shard_map/gram/pallas_call | solution.py:474
  123.1 0.0 copy-start.5
  123.2 0.9 copy-done.5
  124.1 0.0 copy-start.16
  124.1 0.6 copy-done.16
  124.7 20.0 %total.1.total_ref = f32[8,128]{1,0:T(8,128)} custom-call(f32[8,128]{1,0:T(8,128)} %copy-done.16), custom_call_target="tpu_custom_call" | custom-call | tf_op jit(solution)/shard_map/total/pallas_call | solution.py:552
  144.7 0.0 copy-done.3
  144.7 0.0 copy-start.6
  144.7 1.2 copy-done.6
  145.9 0.0 copy-start.14
  145.9 0.7 copy-done.14
  146.6 2.8 %finish.1 = (f32[3,120,2048]{2,1,0:T(8,128)}, f32[3,2]{1,0:T(4,128)S(1)}) custom-call(s32[1]{0:T(128)S(6)} %copy.21.count_ref, f32[8,128]{1,0:T(8,128)S(1)} %copy-done.14, f32[120,2048]{1,0:T(8,128)S(1)} %copy-done.3, f32[120,2048]{1,0:T(8,128)S(1)} %get-tuple-element.16.second_ref, f32[120,2048]{1,0:T(8,128)S(1)} %copy-done.6), custom_call_target="tpu_custom_call" | custom-call | tf_op jit(solution)/shard_map/finish/pallas_call | solution.py:609
  149.4 0.6 copy.20
  (1 shorter events, 0.0 us)
Async XLA Ops:
  3.6 1.2 copy-start.2
  4.8 0.9 copy-start.9
  5.7 0.9 copy-start.12
  6.6 0.8 copy-start.13
  7.5 0.7 copy-start.15
  10.6 1.0 copy-start
  24.5 10.8 %copy-start.1 = (bf16[256,512]{1,0:T(8,128)(2,1)S(1)}, bf16[256,512]{1,0:T(8,128)(2,1)}, u32[]{:S(2)}) copy-start(bf16[256,512]{1,0:T(8,128)(2,1)} %constant.6.clone.selector_ref) | copy-start | bytes 786436
  24.5 10.7 %copy-start.4 = (bf16[1152,256]{1,0:T(8,128)(2,1)S(1)}, bf16[1152,256]{1,0:T(8,128)(2,1)}, u32[]{:S(2)}) copy-start(bf16[1152,256]{1,0:T(8,128)(2,1)} %constant.16.clone.turn_ref) | copy-start | bytes 1769476
  24.5 10.7 %copy-start.7 = (f32[3,8192]{1,0:T(4,128)S(1)}, f32[3,8192]{1,0:T(4,128)}, u32[]{:S(2)}) copy-start(f32[3,8192]{1,0:T(4,128)} %normal_ref.3) | copy-start | bytes 294916
  24.5 10.7 %copy-start.8 = (s32[8192]{0:T(1024)S(1)}, s32[8192]{0:T(1024)}, u32[]{:S(2)}) copy-start(s32[8192]{0:T(1024)} %param.18) | copy-start | bytes 98308
  24.5 10.7 %copy-start.10 = (s32[8192]{0:T(1024)S(1)}, s32[8192]{0:T(1024)}, u32[]{:S(2)}) copy-start(s32[8192]{0:T(1024)} %param.19) | copy-start | bytes 98308
  24.6 10.7 %copy-start.11 = (f32[8192]{0:T(1024)S(1)}, f32[8192]{0:T(1024)}, u32[]{:S(2)}) copy-start(f32[8192]{0:T(1024)} %param.21) | copy-start | bytes 98308
  84.5 60.2 %copy-start.3 = (f32[120,2048]{1,0:T(8,128)S(1)}, f32[120,2048]{1,0:T(8,128)}, u32[]{:S(2)}) copy-start(f32[120,2048]{1,0:T(8,128)} %field_ref.3) | copy-start | bytes 2949124
  123.1 0.9 copy-start.5
  124.1 0.6 copy-start.16
  144.7 1.2 copy-start.6
  145.9 0.7 copy-start.14

commit v3 on v2

v3 whole, which is shorter than its diff:
```python
import functools

import jax
import jax.numpy as jnp
import numpy as np
from jax import lax
from jax.experimental import pallas as pl
from jax.experimental.pallas import tpu as pltpu
from jax.sharding import PartitionSpec as P

EPSILON = 1e-06
PERMUTATIONS = ((0, 1, 2), (0, 2, 1), (1, 0, 2), (1, 2, 0), (2, 0, 1), (2, 1, 0))
OFFSETS = tuple(((direction // 3 - 1, direction % 3 - 1) for direction in (0, 1, 2, 3, 5, 6, 7, 8)))
MESH = pl.DeviceIdType.MESH
F32, BF16, I32 = jnp.float32, jnp.bfloat16, jnp.int32
MIB = 1024 * 1024
UNK, CLASSES, LANES = 120, 256, 128
TILE = 16
HALF = 64
GROUP = 32
TILE_ROWS = 12 * GROUP
NODE_PITCH = 136
FLUX_PITCH = 264
STAGE_PITCH = 24


def trace_tables():
    element_points = [
        (coord_a, coord_b, coord_c, 3 - coord_a - coord_b - coord_c)
        for coord_a in range(4)
        for coord_b in range(4 - coord_a)
        for coord_c in range(4 - coord_a - coord_b)
    ]
    face_points = [
        (coord_a, coord_b, 3 - coord_a - coord_b)
        for coord_a in range(4)
        for coord_b in range(4 - coord_a)
    ]
    select_rows = []
    for opposite in range(4):
        corners = [vertex for vertex in range(4) if vertex != opposite]
        members = []
        for triple in face_points:
            coords = [0, 0, 0, 0]
            for position in range(3):
                coords[corners[position]] = triple[position]
            members.append(element_points.index(tuple(coords)))
        select_rows.append(members)
    turn_rows = [
        [
            face_points.index((triple[sigma_row[0]], triple[sigma_row[1]], triple[sigma_row[2]]))
            for triple in face_points
        ]
        for sigma_row in PERMUTATIONS
    ]
    return select_rows, turn_rows


def trace_selector():
    select_rows, _ = trace_tables()
    table = np.zeros((2 * LANES, 4 * HALF), np.float32)
    for side in range(4):
        for c in range(6):
            for j in range(10):
                column = side * HALF + c * 10 + j
                table[c * 20 + select_rows[side][j], column] = 1.0
                table[LANES + c * 20 + select_rows[side][j], column] = 1.0
    return table


def split(value):
    high = value.astype(BF16)
    return high, (value - high.astype(F32)).astype(BF16)


def dot(a, b, dims=(((1,), (0,)), ((), ()))):
    return lax.dot_general(a, b, dims, preferred_element_type=F32)


NT = (((1,), (1,)), ((), ()))
VMEM = pl.BlockSpec(memory_space=pltpu.VMEM)
SMEM = pl.BlockSpec(memory_space=pltpu.SMEM)
ANY = pl.BlockSpec(memory_space=pl.ANY)


def live_lanes(count, first, width):
    return ((lax.broadcasted_iota(I32, (1, width), 1) + first) < count).astype(F32)


def prep_kernel(
    remote, count_ref, field_hbm, class_ref, lift_ref, link_ref,
    rows_ref, pos_ref, tile_ref, index_ref, lift_hi_ref, lift_lo_ref,
    field_ref, spread_ref, field_sem,
):
    elements = field_ref.shape[1]
    blocks = elements // LANES
    count = count_ref[0]
    field_copy = pltpu.make_async_copy(field_hbm, field_ref, field_sem)
    field_copy.start()

    class_row = lax.broadcasted_iota(I32, (CLASSES, LANES), 0)
    totals = jnp.zeros((CLASSES, LANES), F32)
    for block in range(blocks):
        totals = totals + (class_ref[block : block + 1, :] == class_row).astype(F32)
    total = jnp.sum(totals, axis=1, keepdims=True)
    tiles = jnp.floor((total + (TILE - 1)) * (1.0 / TILE))
    tiles = jnp.broadcast_to(tiles, (CLASSES, LANES))
    lower = (
        lax.broadcasted_iota(I32, (CLASSES, CLASSES), 1)
        < lax.broadcasted_iota(I32, (CLASSES, CLASSES), 0)
    ).astype(BF16)
    start = dot(lower, tiles.astype(BF16))
    end = start + tiles
    earlier = (
        lax.broadcasted_iota(I32, (LANES, 2 * LANES), 0)
        < lax.broadcasted_iota(I32, (LANES, 2 * LANES), 1)
    ).astype(BF16)
    carry = start * TILE
    for block in range(blocks):
        member = (class_ref[block : block + 1, :] == class_row).astype(F32)
        ranks = dot(member.astype(BF16), earlier)
        position = jnp.sum(member * (ranks[:, :LANES] + carry), axis=0, keepdims=True)
        pos_ref[block : block + 1, :] = position.astype(I32)
        carry = carry + ranks[:, LANES:]
    tile_ref[...] = jnp.zeros((8, LANES), I32)
    for row in range(4):
        tile = (lax.broadcasted_iota(I32, (CLASSES, LANES), 1) + row * LANES).astype(F32)
        owner = jnp.sum((end <= tile).astype(F32), axis=0, keepdims=True)
        tile_ref[row : row + 1, :] = jnp.minimum(owner.astype(I32), CLASSES - 1)
    tile_ref[4:5, :] = end[CLASSES - 1 :, :].astype(I32)

    link = link_ref[...]
    own = (
        lax.broadcasted_iota(I32, link.shape, 0) * LANES
        + lax.broadcasted_iota(I32, link.shape, 1)
        + remote
    )
    index_ref[...] = jnp.where(link < 0, own, link)

    spread_ref[...] = jnp.zeros(spread_ref.shape, F32)
    for side in range(4):
        block = lift_ref[side]
        for c in range(6):
            first = side * HALF + c * 10
            spread_ref[c * 20 : (c + 1) * 20, first : first + 10] = block
    high, low = split(spread_ref[...])
    lift_hi_ref[...] = high
    lift_lo_ref[...] = low

    field_copy.wait()
    for block in range(blocks):
        lanes = slice(block * LANES, (block + 1) * LANES)
        value = field_ref[:, lanes] * live_lanes(count, block * LANES, LANES)
        value = jnp.concatenate([value, jnp.zeros((LANES - UNK, LANES), F32)], axis=0)
        rows_ref[lanes, :] = value.T


def prepare(part_count, right_side, elem_class, lift, link, remote):
    elements = right_side.shape[1]
    faces = link.shape[0]
    return pl.pallas_call(
        functools.partial(prep_kernel, remote),
        out_shape=(
            jax.ShapeDtypeStruct((elements, LANES), F32),
            jax.ShapeDtypeStruct((elements // LANES, LANES), I32),
            jax.ShapeDtypeStruct((8, LANES), I32),
            jax.ShapeDtypeStruct((faces // LANES, LANES), I32),
            jax.ShapeDtypeStruct((LANES, 4 * HALF), BF16),
            jax.ShapeDtypeStruct((LANES, 4 * HALF), BF16),
        ),
        in_specs=[SMEM, ANY, VMEM, VMEM, VMEM],
        out_specs=(VMEM,) * 6,
        scratch_shapes=[
            pltpu.VMEM(right_side.shape, F32),
            pltpu.VMEM((LANES, 4 * HALF), F32),
            pltpu.SemaphoreType.DMA(()),
        ],
        compiler_params=pltpu.CompilerParams(vmem_limit_bytes=8 * MIB),
        name="prepare",
    )(
        part_count, right_side, elem_class.reshape(elements // LANES, LANES), lift,
        link.reshape(faces // LANES, LANES),
    )


def write_traces(rows_ref, selector_ref, table_ref, first):
    elements = rows_ref.shape[0]
    width = 2 * LANES
    left = lax.broadcasted_iota(I32, (width, LANES), 1) < HALF

    def block(index, carry):
        base = pl.multiple_of(index * width, width)
        high, low = split(rows_ref[pl.ds(base, width), :])
        traces = dot(jnp.concatenate([high, low], axis=1), selector_ref[...])
        for pair in range(2):
            both = traces[:, pair * LANES : (pair + 1) * LANES]
            swapped = pltpu.roll(both, HALF, 1)
            even, odd = first + 2 * pair * elements, first + (2 * pair + 1) * elements
            table_ref[pl.ds(even + base, width), :] = jnp.where(left, both, swapped)
            table_ref[pl.ds(odd + base, width), :] = jnp.where(left, swapped, both)
        return carry

    lax.fori_loop(0, elements // width, block, 0, unroll=4)


def gather_pairs(table_ref, index_ref, out_ref, first_a, first_b, offset, count, unroll):
    left = lax.broadcasted_iota(I32, (1, LANES), 1) < HALF

    def block(index, carry):
        base = pl.multiple_of(index * unroll, unroll)
        for step in range(unroll):
            row_a = table_ref[pl.ds(index_ref[first_a + base + step] + offset, 1), :]
            row_b = table_ref[pl.ds(index_ref[first_b + base + step] + offset, 1), :]
            out_ref[pl.ds(base + step, 1), :] = jnp.where(left, row_a, row_b)
        return carry

    lax.fori_loop(0, count // unroll, block, 0)


def class_major(native_ref, stage_ref, class_ref):
    rows = 16
    pad = jnp.zeros((LANES - UNK, CLASSES), F32)

    def chunk(index, carry):
        for row in range(rows):
            source = index * rows + row
            value = native_ref[jnp.minimum(source, UNK - 1)].astype(F32)
            value = jnp.where(source < UNK, value, 0.0)
            value = jnp.concatenate([value, pad], axis=0).T
            stage_ref[pl.ds(row, CLASSES, stride=STAGE_PITCH), :] = value
        first = pl.multiple_of(index * rows, rows)
        stage = stage_ref[...].reshape(CLASSES, STAGE_PITCH, LANES)[:, :rows].astype(BF16)
        class_ref[:, pl.ds(first, rows), :] = stage
        return carry

    lax.fori_loop(0, LANES // rows, chunk, 0)


def exchange_kernel(grid_rows, grid_columns, with_classes, *refs):
    if with_classes:
        (rows_ref, selector_ref, list_ref, native_hbm, table_ref, class_ref,
         outgoing_ref, received_ref, send_sem, recv_sem, native_ref, stage_ref, native_sem) = refs
        native_copy = pltpu.make_async_copy(native_hbm, native_ref, native_sem)
        native_copy.start()
    else:
        (rows_ref, selector_ref, list_ref, table_ref,
         outgoing_ref, received_ref, send_sem, recv_sem) = refs
    slots = outgoing_ref.shape[1]
    row, column = lax.axis_index("prow"), lax.axis_index("pcol")

    def present(index):
        a, b = OFFSETS[index]
        inside = None
        for at, step, size in ((row, a, grid_rows), (column, b, grid_columns)):
            if step == 0:
                continue
            term = at > 0 if step < 0 else at < size - 1
            inside = term if inside is None else jnp.logical_and(inside, term)
        return inside

    def partner(index):
        a, b = OFFSETS[index]
        return (row + a, column + b)

    def transfer(index):
        return pltpu.make_async_remote_copy(
            src_ref=outgoing_ref.at[index],
            dst_ref=received_ref.at[7 - index],
            send_sem=send_sem.at[index],
            recv_sem=recv_sem.at[7 - index],
            device_id=partner(index),
            device_id_type=MESH,
        )

    barrier = pltpu.get_barrier_semaphore()
    for index in range(8):
        @pl.when(present(index))
        def _(index=index):
            pl.semaphore_signal(barrier, inc=1, device_id=partner(index), device_id_type=MESH)

    write_traces(rows_ref, selector_ref, table_ref, 16 * slots)

    near_rows = 1 + (row > 0).astype(I32) + (row < grid_rows - 1).astype(I32)
    near_columns = 1 + (column > 0).astype(I32) + (column < grid_columns - 1).astype(I32)
    pl.semaphore_wait(barrier, near_rows * near_columns - 1)

    for index in (0, 2, 5, 7, 3, 4, 1, 6):
        first = index * 2 * slots
        gather_pairs(
            table_ref, list_ref, outgoing_ref.at[index], first, first + slots, 0, slots, 32
        )

        @pl.when(present(index))
        def _(index=index):
            transfer(index).start()

    if with_classes:
        native_copy.wait()
        class_major(native_ref, stage_ref, class_ref)

    left = lax.broadcasted_iota(I32, (slots, LANES), 1) < HALF
    for index in (1, 6, 3, 4, 0, 2, 5, 7):
        @pl.when(present(index))
        def _(index=index):
            transfer(7 - index).wait_recv()
            packed = received_ref[index]
            swapped = pltpu.roll(packed, HALF, 1)
            first = index * 2 * slots
            table_ref[first : first + slots, :] = jnp.where(left, packed, swapped)
            table_ref[first + slots : first + 2 * slots, :] = jnp.where(left, swapped, packed)

    for index in range(8):
        @pl.when(present(index))
        def _(index=index):
            transfer(index).wait_send()


def exchange(rows, selector, lists, native=None):
    slots = lists.shape[0] // 16
    with_classes = native is not None
    out_shape = [jax.ShapeDtypeStruct((16 * slots + 4 * rows.shape[0], LANES), F32)]
    scratch = [
        pltpu.VMEM((8, slots, LANES), F32),
        pltpu.VMEM((8, slots, LANES), F32),
        pltpu.SemaphoreType.DMA((8,)),
        pltpu.SemaphoreType.DMA((8,)),
    ]
    operands = [rows, selector, lists]
    if with_classes:
        out_shape.append(jax.ShapeDtypeStruct((CLASSES, LANES, LANES), BF16))
        scratch += [
            pltpu.VMEM(native.shape, BF16),
            pltpu.VMEM((CLASSES * STAGE_PITCH, LANES), F32),
            pltpu.SemaphoreType.DMA(()),
        ]
        operands.append(native)
    return pl.pallas_call(
        functools.partial(
            exchange_kernel, lax.axis_size("prow"), lax.axis_size("pcol"), with_classes
        ),
        out_shape=tuple(out_shape),
        in_specs=[VMEM, VMEM, SMEM] + [ANY] * with_classes,
        out_specs=(VMEM,) * len(out_shape),
        scratch_shapes=scratch,
        compiler_params=pltpu.CompilerParams(
            collective_id=2 if with_classes else 0, has_side_effects=True,
            vmem_limit_bytes=(36 if with_classes else 16) * MIB,
        ),
        name="exchange_first" if with_classes else "exchange",
    )(*operands)


def turn_choices():
    _, turn_rows = trace_tables()
    choices = []
    for j in range(10):
        sources = {}
        for option in range(6):
            sources.setdefault(turn_rows[option][j], []).append(option)
        choices.append([(source, tuple(options)) for source, options in sources.items()])
    return choices


def turn_faces(node_ref, first, stride, orient):
    masks = {}

    def mask(options):
        if options not in masks:
            value = orient == options[0]
            for option in options[1:]:
                value = jnp.logical_or(value, orient == option)
            masks[options] = value
        return masks[options]

    choices = turn_choices()
    for c in range(6):
        at = [pl.ds(first + c * 10 + j, 8, stride=stride) for j in range(10)]
        nodes = [node_ref[at[j], :] for j in range(10)]
        for j in range(10):
            (source, _), *others = choices[j]
            value = nodes[source]
            for source, options in others:
                value = jnp.where(mask(options), nodes[source], value)
            if others:
                node_ref[at[j], :] = value


def face_flux(electric, magnetic, normal, scale):
    along_e = normal[0] * electric[0] + normal[1] * electric[1] + normal[2] * electric[2]
    along_h = normal[0] * magnetic[0] + normal[1] * magnetic[1] + normal[2] * magnetic[2]
    flux = []
    for c in range(3):
        a, b = (c + 1) % 3, (c + 2) % 3
        cross = normal[a] * magnetic[b] - normal[b] * magnetic[a]
        flux.append(scale * (electric[c] - normal[c] * along_e - cross))
    for c in range(3):
        a, b = (c + 1) % 3, (c + 2) % 3
        cross = normal[a] * electric[b] - normal[b] * electric[a]
        flux.append(scale * (magnetic[c] - normal[c] * along_h + cross))
    return flux


def image_kernel(
    count_ref, index_ref, pos_ref, tile_ref,
    table_ref, lift_hi_ref, lift_lo_ref,
    link_ref, orient_ref, normal_ref, quotient_ref, class_ref,
    image_ref,
    picked_ref, node_ref, flux_ref, coupled_ref, sorted_ref, solved_ref,
):
    elements = image_ref.shape[0]
    blocks = elements // LANES
    chunks = blocks // 8

    gather_pairs(table_ref, index_ref, picked_ref, 0, 2 * elements, 0, 2 * elements, 64)

    def transpose(index, carry):
        for step in range(4):
            block = index * 4 + step
            rows = pl.ds(pl.multiple_of(block * LANES, LANES), LANES)
            target = pl.multiple_of(block * NODE_PITCH, 8)
            node_ref[pl.ds(target, LANES), :] = picked_ref[rows, :].T
        return carry

    lax.fori_loop(0, 2 * blocks // 4, transpose, 0)

    for block in range(blocks):
        for side in range(4):
            last = block * FLUX_PITCH + (side + 1) * HALF
            flux_ref[last - 8 : last, :] = jnp.zeros((8, LANES), F32)

    count = count_ref[0]
    lane = (
        lax.broadcasted_iota(I32, (8, LANES), 0) * LANES + lax.broadcasted_iota(I32, (8, LANES), 1)
    )

    def chunk(index, carry):
        side, part = index // chunks, index % chunks
        pair, half = side % 2, side // 2
        faces = pl.ds(pl.multiple_of(side * blocks + part * 8, 8), 8)
        first = (pair * blocks + part * 8) * NODE_PITCH + half * HALF
        turn_faces(node_ref, first, NODE_PITCH, orient_ref[faces, :])
        alive = ((lane + part * (8 * LANES)) < count).astype(F32)
        scale = 0.5 * quotient_ref[faces, :] * alive
        sign = jnp.where(link_ref[faces, :] < 0, -1.0, 1.0)
        normal = [normal_ref[c, faces, :] for c in range(3)]
        target = part * (8 * FLUX_PITCH) + side * HALF
        for j in range(10):
            nodes = [node_ref[pl.ds(first + c * 10 + j, 8, stride=NODE_PITCH), :] for c in range(6)]
            electric = [value * sign for value in nodes[:3]]
            flux = face_flux(electric, nodes[3:], normal, scale)
            for c in range(6):
                flux_ref[pl.ds(target + c * 10 + j, 8, stride=FLUX_PITCH), :] = flux[c]
        return carry

    lax.fori_loop(0, 4 * chunks, chunk, 0)

    def lift(index, carry):
        rows = 4 * HALF
        first = pl.multiple_of(index * (2 * FLUX_PITCH), 8)
        second = pl.multiple_of(first + FLUX_PITCH, 8)
        value = jnp.concatenate(
            [flux_ref[pl.ds(first, rows), :], flux_ref[pl.ds(second, rows), :]], axis=1
        )
        high, low = split(value)
        coupled = dot(lift_hi_ref[...], high) + dot(lift_hi_ref[...], low) + dot(lift_lo_ref[...], high)
        base = pl.multiple_of(index * (2 * LANES), 2 * LANES)
        coupled_ref[pl.ds(base, 2 * LANES), :] = coupled.T
        return carry

    lax.fori_loop(0, blocks // 2, lift, 0, unroll=4)

    unroll = 16

    def place(index, carry):
        base = pl.multiple_of(index * unroll, unroll)
        for step in range(unroll):
            sorted_ref[pl.ds(pos_ref[base + step], 1), :] = coupled_ref[pl.ds(base + step, 1), :]
        return carry

    lax.fori_loop(0, elements // unroll, place, 0)

    def solve(index, carry):
        for step in range(GROUP):
            tile = index * GROUP + step
            base = pl.multiple_of(tile * TILE, TILE)
            high, low = split(sorted_ref[pl.ds(base, TILE), :])
            result = dot(jnp.concatenate([high, low], axis=0), class_ref[tile_ref[tile]], NT)
            solved_ref[pl.ds(base, TILE), :] = result[:TILE] + result[TILE:]
        return carry

    lax.fori_loop(0, (tile_ref[4 * LANES] + (GROUP - 1)) // GROUP, solve, 0)

    def fetch(index, carry):
        base = pl.multiple_of(index * unroll, unroll)
        for step in range(unroll):
            image_ref[pl.ds(base + step, 1), :] = solved_ref[pl.ds(pos_ref[base + step], 1), :]
        return carry

    lax.fori_loop(0, elements // unroll, fetch, 0)


def image(part_count, indices, pos, tiles, table, lift_hi, lift_lo,
          link, orient, normal, quotient, classes):
    elements = pos.shape[0]
    slots = TILE_ROWS * TILE
    return pl.pallas_call(
        image_kernel,
        out_shape=jax.ShapeDtypeStruct((elements, LANES), F32),
        in_specs=[SMEM] * 4 + [VMEM] * 8,
        out_specs=VMEM,
        scratch_shapes=[
            pltpu.VMEM((2 * elements, LANES), F32),
            pltpu.VMEM((2 * elements // LANES * NODE_PITCH, LANES), F32),
            pltpu.VMEM((elements // LANES * FLUX_PITCH, LANES), F32),
            pltpu.VMEM((elements, LANES), F32),
            pltpu.VMEM((slots, LANES), F32),
            pltpu.VMEM((slots, LANES), F32),
        ],
        compiler_params=pltpu.CompilerParams(vmem_limit_bytes=24 * MIB),
        name="image",
    )(
        part_count, indices, pos, tiles, table, lift_hi, lift_lo,
        link.reshape(-1, LANES), orient.reshape(-1, LANES), normal.reshape(3, -1, LANES),
        quotient.reshape(-1, LANES), classes,
    )


def gram_partials(first_ref, second_ref, third_ref, gram_ref):
    elements = first_ref.shape[0]

    def block(index, sums):
        rows = pl.ds(pl.multiple_of(index * LANES, LANES), LANES)
        f, t, u = first_ref[rows, :], second_ref[rows, :], third_ref[rows, :]
        pairs = (f * f, f * t, t * t, f * u, t * u, u * u)
        return tuple(
            total + jnp.sum(pair.reshape(LANES // 8, 8, LANES), axis=0)
            for total, pair in zip(sums, pairs)
        )

    zero = jnp.zeros((8, LANES), F32)
    sums = lax.fori_loop(0, elements // LANES, block, (zero,) * 6)
    for index in range(6):
        gram_ref[index : index + 1, :] = jnp.sum(sums[index], axis=0, keepdims=True)
    gram_ref[6:, :] = jnp.zeros((2, LANES), F32)


def total_kernel(grid_rows, grid_columns, first_ref, second_ref, third_ref, total_ref,
                 part_ref, over_rows, over_columns, send_row, recv_row, send_column, recv_column):
    row, column = lax.axis_index("prow"), lax.axis_index("pcol")

    def row_partner(step):
        return lax.rem(row + step, grid_rows)

    def column_partner(step):
        return lax.rem(column + step, grid_columns)

    barrier = pltpu.get_barrier_semaphore()
    for step in range(1, grid_rows):
        pl.semaphore_signal(
            barrier, inc=1, device_id=(row_partner(step), column), device_id_type=MESH
        )
    for step in range(1, grid_columns):
        pl.semaphore_signal(
            barrier, inc=1, device_id=(row, column_partner(step)), device_id_type=MESH
        )
    gram_partials(first_ref, second_ref, third_ref, part_ref)
    pl.semaphore_wait(barrier, grid_rows + grid_columns - 2)

    def row_copy(step):
        return pltpu.make_async_remote_copy(
            src_ref=part_ref,
            dst_ref=over_rows.at[step],
            send_sem=send_row.at[step],
            recv_sem=recv_row.at[step],
            device_id=(row_partner(step), column),
            device_id_type=MESH,
        )

    for step in range(1, grid_rows):
        row_copy(step).start()
    over_rows[0] = part_ref[...]
    for step in range(1, grid_rows):
        row_copy(step).wait()
    total = over_rows[row]
    for source in range(1, grid_rows):
        total = total + over_rows[lax.rem(row - source + grid_rows, grid_rows)]
    over_columns[0] = total

    def column_copy(step):
        return pltpu.make_async_remote_copy(
            src_ref=over_columns.at[0],
            dst_ref=over_columns.at[step],
            send_sem=send_column.at[step],
            recv_sem=recv_column.at[step],
            device_id=(row, column_partner(step)),
            device_id_type=MESH,
        )

    for step in range(1, grid_columns):
        column_copy(step).start()
    for step in range(1, grid_columns):
        column_copy(step).wait()
    total = over_columns[column]
    for source in range(1, grid_columns):
        total = total + over_columns[lax.rem(column - source + grid_columns, grid_columns)]
    total_ref[...] = total


def total_over_devices(first, second, third):
    grid_rows, grid_columns = lax.axis_size("prow"), lax.axis_size("pcol")
    part = (8, LANES)
    return pl.pallas_call(
        functools.partial(total_kernel, grid_rows, grid_columns),
        out_shape=jax.ShapeDtypeStruct(part, F32),
        in_specs=[VMEM] * 3,
        out_specs=VMEM,
        scratch_shapes=[
            pltpu.VMEM(part, F32),
            pltpu.VMEM((grid_rows,) + part, F32),
            pltpu.VMEM((grid_columns,) + part, F32),
            pltpu.SemaphoreType.DMA((grid_rows,)),
            pltpu.SemaphoreType.DMA((grid_rows,)),
            pltpu.SemaphoreType.DMA((grid_columns,)),
            pltpu.SemaphoreType.DMA((grid_columns,)),
        ],
        compiler_params=pltpu.CompilerParams(
            collective_id=1, has_side_effects=True, vmem_limit_bytes=8 * MIB
        ),
        name="total",
    )(first, second, third)


def finish_kernel(weight, count_ref, total_ref, field_ref, second_ref, third_ref, basis_ref, hess_ref):
    width = field_ref.shape[1]
    gram = jnp.sum(total_ref[...], axis=1, keepdims=True) * weight
    ff, ft, tt, fu, tu, uu = (gram[index : index + 1, :] for index in range(6))
    beta = jnp.sqrt(ff + EPSILON)
    square = beta * beta
    h00 = (ff + ft) / square
    p = (EPSILON - ft) / square
    h10 = jnp.sqrt((tt + 2 * p * ft + p * p * ff) / square + EPSILON)
    k1 = 1.0 / (beta * h10)
    h01 = k1 / beta * (fu + (1 + p) * ft + p * ff)
    h11 = k1 * k1 * (tu + (1 + p) * tt + p * ft + p * fu + p * (1 + p) * ft + p * p * ff)
    q = 1 + p - h11
    w = p * (1 - h11) - h01 * h10
    h21 = jnp.sqrt(
        k1 * k1 * (uu + 2 * q * tu + 2 * w * fu + q * q * tt + 2 * q * w * ft + w * w * ff)
        + EPSILON
    )
    k2 = k1 / h21

    alive = live_lanes(count_ref[0], pl.program_id(0) * width, width)
    f = field_ref[...] * alive
    t, u = second_ref[...].T[:UNK], third_ref[...].T[:UNK]
    basis_ref[0] = f * (1.0 / beta)
    basis_ref[1] = t * k1 + f * (p * k1)
    basis_ref[2] = u * k2 + t * (q * k2) + f * (w * k2)

    at_row = lax.broadcasted_iota(I32, (3, 2), 0)
    at_column = lax.broadcasted_iota(I32, (3, 2), 1)
    hess = jnp.zeros((3, 2), F32)
    for i, j, value in ((0, 0, h00), (1, 0, h10), (0, 1, h01), (1, 1, h11), (2, 1, h21)):
        hess = jnp.where(jnp.logical_and(at_row == i, at_column == j), value, hess)
    hess_ref[...] = hess


def finish(weight, part_count, total, right_side, second, third):
    elements = right_side.shape[1]
    width = 512
    rows = pl.BlockSpec((width, LANES), lambda i: (i, 0))
    field = pl.BlockSpec((UNK, width), lambda i: (0, i))
    return pl.pallas_call(
        functools.partial(finish_kernel, weight),
        grid=(elements // width,),
        out_shape=(
            jax.ShapeDtypeStruct((3, UNK, elements), F32),
            jax.ShapeDtypeStruct((3, 2), F32),
        ),
        in_specs=[
            pl.BlockSpec(memory_space=pltpu.SMEM),
            pl.BlockSpec((8, LANES), lambda i: (0, 0)),
            field, rows, rows,
        ],
        out_specs=(
            pl.BlockSpec((3, UNK, width), lambda i: (0, 0, i)),
            pl.BlockSpec((3, 2), lambda i: (0, 0)),
        ),
        compiler_params=pltpu.CompilerParams(vmem_limit_bytes=12 * MIB),
        name="finish",
    )(part_count, total, right_side, second, third)


def shards(
    right_side,
    part_count,
    elem_class,
    face_link,
    face_orient,
    face_normal,
    boundary_metric_quotient,
    bound_face,
    lift,
    inverse_table,
):
    unknowns, elements = right_side.shape
    all_subdomains = lax.axis_size("prow") * lax.axis_size("pcol")
    weight = 1.0 / (unknowns * elements * all_subdomains)
    lists = bound_face.reshape(-1)
    lists = jnp.maximum(lists, 0) + lists.shape[0]
    selector = jnp.asarray(trace_selector(), BF16)
    native = jnp.transpose(inverse_table, (1, 2, 0))

    first, pos, tiles, indices, lift_hi, lift_lo = prepare(
        part_count, right_side, elem_class, lift, face_link, lists.shape[0]
    )
    pos, tiles, indices = pos.reshape(-1), tiles.reshape(-1), indices.reshape(-1)
    first_table, classes = exchange(first, selector, lists, native)

    def operator_image(table):
        return image(
            part_count, indices, pos, tiles, table, lift_hi, lift_lo, face_link, face_orient,
            face_normal, boundary_metric_quotient, classes,
        )

    second = operator_image(first_table)
    (second_table,) = exchange(second, selector, lists)
    third = operator_image(second_table)
    total = total_over_devices(first, second, third)
    return finish(weight, part_count, total, right_side, second, third)


def solution(mesh):
    in_specs = (
        P(None, ("prow", "pcol")),
        P(("prow", "pcol")),
        P(("prow", "pcol")),
        P(("prow", "pcol")),
        P(("prow", "pcol")),
        P(None, ("prow", "pcol")),
        P(("prow", "pcol")),
        P(("prow", "pcol"), None, None),
        P(),
        P(),
    )
    out_specs = (P(None, None, ("prow", "pcol")), P())
    return jax.shard_map(shards, mesh=mesh, in_specs=in_specs, out_specs=out_specs, check_vma=False)
```

time: 151 us -> 111 us (0.74)
  Pallas kernels: 126 us -> 96.3 us
  local copies, waits for them, and re-layouts: 21.1 us -> 12.4 us
    pallas_call x2, Pallas kernels: 74 us -> 43.6 us  [image(): pl.pallas_call(image_kernel, out_shape=jax.ShapeDtypeStruct((elements, LA...]
    unnamed x36 -> x26, local copies, waits for them, and re-layouts: 20.5 us -> 11.8 us
    pallas_call x2, Pallas kernels: 25.2 us -> 28 us  [exchange(): pl.pallas_call(functools.partial(exchange_kernel, lax.axis_size('prow'),...]
    pallas_call x2 -> x1, Pallas kernels: 3.98 us -> 1.9 us  [prepare(): pl.pallas_call(functools.partial(prep_kernel, remote), out_shape=(jax.Sha...]
where the time goes in v3:
time: 111 us
  Pallas kernels  96.3 us (87%)
  local copies, waits for them, and re-layouts  12.4 us (11%)
  between operations  1.44 us (1%)
    pallas_call x2, Pallas kernels, image(): pl.pallas_call(image_kernel, out_shape=jax.ShapeDtypeStruct((elements, LA...  43.6 us
    pallas_call x2, Pallas kernels, exchange(): pl.pallas_call(functools.partial(exchange_kernel, lax.axis_size('prow'),...  28 us
    pallas_call x1, Pallas kernels, total_over_devices(): pl.pallas_call(functools.partial(total_kernel, grid_rows, grid_columns),...  20.1 us
    unnamed x26, local copies, waits for them, and re-layouts  11.8 us
    pallas_call x1, Pallas kernels, finish(): pl.pallas_call(functools.partial(finish_kernel, weight), grid=(elements /...  2.71 us

profile of v3, /device:TPU:1, one launch (start us, length us, event | category | flops | bytes accessed | tf_op | source)
XLA Modules:
  0.0 110.9 jit_solution(4287259597126324078)
XLA Ops:
  0.6 0.0 copy-start.10
  0.6 0.0 copy-start.9
  0.7 0.0 copy-start.8
  1.3 0.7 maximum_add_fusion
  2.0 0.8 copy.13.lift_ref
  2.9 0.9 copy.17
  3.8 0.0 copy-start.3
  3.8 1.2 %copy-done.3 = f32[120,2048]{1,0:T(8,128)S(1)} copy-done((f32[120,2048]{1,0:T(8,128)S(1)}, f32[120,2048]{1,0:T(8,128)}, u32[]{:S(2)}) %copy-start.3) | copy-done | bytes 983064
  5.0 0.0 copy-start.7
  5.0 0.8 copy-done.7
  5.7 0.0 copy-start.11
  5.7 0.7 copy-done.11
  6.4 1.9 %prepare.1 = (f32[2048,128]{1,0:T(8,128)S(1)}, s32[16,128]{1,0:T(8,128)S(1)}, s32[8,128]{1,0:T(8,128)S(1)}, s32[64,128]{1,0:T(8,128)S(1)}, bf16[128,256]{1,0:T(8,128)(2,1)S(1)}, /*index=5*/bf16[128,256]{1,0:T(8,128)(2,1)S(1)}) custom-call(s32[1]{0:T(128)S(6)} %copy.18.count_ref, f32[120,2048]{1,0:T(8,128)S(1)} %copy-done.3, s32[16,128]{1,0:T(8,128)S(1)} %bitcast.28, ...), custom_call_target="tpu_custom_call" | custom-call | tf_op jit(solution)/shard_map/prepare/pallas_call | solution.py:161
  8.3 0.0 copy-start.2
  8.4 3.1 %copy-done.2 = bf16[256,120,120]{0,2,1:T(8,128)(2,1)S(1)} copy-done((bf16[256,120,120]{0,2,1:T(8,128)(2,1)S(1)}, bf16[256,120,120]{0,2,1:T(8,128)(2,1)}, u32[]{:S(2)}) %copy-start.2) | copy-done | bytes 7372824
  11.4 0.0 copy-start.5
  11.4 0.9 copy-done.5
  12.3 16.4 %exchange_first.1 = (f32[11264,128]{1,0:T(8,128)S(1)}, bf16[256,128,128]{2,1,0:T(8,128)(2,1)}) custom-call(f32[2048,128]{1,0:T(8,128)S(1)} %get-tuple-element.10.refs_0_.first_ref, bf16[256,256]{1,0:T(8,128)(2,1)S(1)} %copy-done.5, s32[3072]{0:T(1024)S(1)} %add.10.refs_2_, bf16[120,120,256]{2,1,0:T(8,128)(2,1)S(1)} %bitcast.12), custom_call_target="tpu_custom_call" | custom-call | tf_op jit(solution)/shard_map/exchange_first/pallas_call | solution.py:337
  28.7 0.0 copy-done.10
  28.7 0.0 copy-done.9
  28.8 0.0 copy-done.8
  28.8 0.0 copy-start
  28.8 3.4 %copy-done = bf16[256,128,128]{2,1,0:T(8,128)(2,1)S(1)} copy-done((bf16[256,128,128]{2,1,0:T(8,128)(2,1)S(1)}, bf16[256,128,128]{2,1,0:T(8,128)(2,1)}, u32[]{:S(2)}) %copy-start) | copy-done | bytes 8388632
  32.1 0.0 copy-start.6
  32.1 0.0 copy-start.1
  32.2 21.8 %image.2.refs_0_.second_ref = f32[2048,128]{1,0:T(8,128)S(1)} custom-call(s32[1]{0:T(128)S(6)} %copy.18.count_ref, s32[8192]{0:T(1024)S(1)} %bitcast.22, s32[2048]{0:T(1024)S(1)} %bitcast.24, s32[1024]{0:T(1024)S(1)} %bitcast.26, f32[11264,128]{1,0:T(8,128)S(1)} %get-tuple-element.14.table_ref, bf16[128,256]{1,0:T(8,128)(2,1)S(1)} %get-tuple-element.15.lift_hi_ref, ...), custom_call_target="tpu_custom_call" | custom-call | tf_op jit(solution)/shard_map/image/pallas_call | solution.py:506
  54.0 0.0 copy-done.6
  54.0 11.6 %exchange.1.table_ref = f32[11264,128]{1,0:T(8,128)S(1)} custom-call(f32[2048,128]{1,0:T(8,128)S(1)} %image.2.refs_0_.second_ref, bf16[256,256]{1,0:T(8,128)(2,1)S(1)} %copy-done.6, s32[3072]{0:T(1024)S(1)} %add.10.refs_2_), custom_call_target="tpu_custom_call" | custom-call | tf_op jit(solution)/shard_map/exchange/pallas_call | solution.py:337
  65.6 0.0 copy-done.1
  65.6 0.0 copy-start.4
  65.6 21.8 %image.3.third_ref = f32[2048,128]{1,0:T(8,128)S(1)} custom-call(s32[1]{0:T(128)S(6)} %copy.18.count_ref, s32[8192]{0:T(1024)S(1)} %bitcast.23, s32[2048]{0:T(1024)S(1)} %bitcast.25, s32[1024]{0:T(1024)S(1)} %bitcast.27, f32[11264,128]{1,0:T(8,128)S(1)} %exchange.1.table_ref, bf16[128,256]{1,0:T(8,128)(2,1)S(1)} %get-tuple-element.15.lift_hi_ref, ...), custom_call_target="tpu_custom_call" | custom-call | tf_op jit(solution)/shard_map/image/pallas_call | solution.py:506
  87.4 20.1 %total.1.total_ref = f32[8,128]{1,0:T(8,128)S(1)} custom-call(f32[2048,128]{1,0:T(8,128)S(1)} %get-tuple-element.10.refs_0_.first_ref, f32[2048,128]{1,0:T(8,128)S(1)} %image.2.refs_0_.second_ref, f32[2048,128]{1,0:T(8,128)S(1)} %image.3.third_ref), custom_call_target="tpu_custom_call" | custom-call | tf_op jit(solution)/shard_map/total/pallas_call | solution.py:612
  107.5 0.0 copy-done.4
  107.5 2.7 %finish.1 = (f32[3,120,2048]{2,1,0:T(8,128)}, f32[3,2]{1,0:T(4,128)S(1)}) custom-call(s32[1]{0:T(128)S(6)} %copy.18.count_ref, f32[8,128]{1,0:T(8,128)S(1)} %total.1.total_ref, f32[120,2048]{1,0:T(8,128)S(1)} %copy-done.4, f32[2048,128]{1,0:T(8,128)S(1)} %image.2.refs_0_.second_ref, f32[2048,128]{1,0:T(8,128)S(1)} %image.3.third_ref), custom_call_target="tpu_custom_call" | custom-call | tf_op jit(solution)/shard_map/finish/pallas_call | solution.py:673
  110.2 0.6 copy.14
  (1 shorter events, 0.0 us)
Async XLA Ops:
  0.6 28.1 %copy-start.10 = (f32[8192]{0:T(1024)S(1)}, f32[8192]{0:T(1024)}, u32[]{:S(2)}) copy-start(f32[8192]{0:T(1024)} %param.17) | copy-start | bytes 98308
  0.6 28.1 %copy-start.9 = (s32[8192]{0:T(1024)S(1)}, s32[8192]{0:T(1024)}, u32[]{:S(2)}) copy-start(s32[8192]{0:T(1024)} %param.15) | copy-start | bytes 98308
  0.7 28.1 %copy-start.8 = (s32[8192]{0:T(1024)S(1)}, s32[8192]{0:T(1024)}, u32[]{:S(2)}) copy-start(s32[8192]{0:T(1024)} %param.14) | copy-start | bytes 98308
  3.8 1.2 %copy-start.3 = (f32[120,2048]{1,0:T(8,128)S(1)}, f32[120,2048]{1,0:T(8,128)}, u32[]{:S(2)}) copy-start(f32[120,2048]{1,0:T(8,128)} %field_ref.1) | copy-start | bytes 2949124
  5.0 0.8 copy-start.7
  5.7 0.7 copy-start.11
  8.3 3.1 %copy-start.2 = (bf16[256,120,120]{0,2,1:T(8,128)(2,1)S(1)}, bf16[256,120,120]{0,2,1:T(8,128)(2,1)}, u32[]{:S(2)}) copy-start(bf16[256,120,120]{0,2,1:T(8,128)(2,1)} %param.20) | copy-start | bytes 22118404
  11.4 0.9 copy-start.5
  28.8 3.4 %copy-start = (bf16[256,128,128]{2,1,0:T(8,128)(2,1)S(1)}, bf16[256,128,128]{2,1,0:T(8,128)(2,1)}, u32[]{:S(2)}) copy-start(bf16[256,128,128]{2,1,0:T(8,128)(2,1)} %get-tuple-element.17.class_ref) | copy-start | bytes 25165828
  32.1 21.8 %copy-start.6 = (bf16[256,256]{1,0:T(8,128)(2,1)S(1)}, bf16[256,256]{1,0:T(8,128)(2,1)}, u32[]{:S(2)}) copy-start(bf16[256,256]{1,0:T(8,128)(2,1)} %constant.6.clone.refs_1_) | copy-start | bytes 393220
  32.1 33.4 %copy-start.1 = (bf16[256,128,128]{2,1,0:T(8,128)(2,1)S(1)}, bf16[256,128,128]{2,1,0:T(8,128)(2,1)}, u32[]{:S(2)}) copy-start(bf16[256,128,128]{2,1,0:T(8,128)(2,1)} %get-tuple-element.17.class_ref) | copy-start | bytes 25165828
  65.6 41.9 %copy-start.4 = (f32[120,2048]{1,0:T(8,128)S(1)}, f32[120,2048]{1,0:T(8,128)}, u32[]{:S(2)}) copy-start(f32[120,2048]{1,0:T(8,128)} %field_ref.1) | copy-start | bytes 2949124

commit v4 on v3

--- a/solution.py
+++ b/solution.py
@@ -22,6 +22,7 @@
 NODE_PITCH = 136
 FLUX_PITCH = 264
 STAGE_PITCH = 24
+CHUNK = 16
 
 
 def trace_tables():
@@ -58,14 +59,16 @@
 
 def trace_selector():
     select_rows, _ = trace_tables()
-    table = np.zeros((2 * LANES, 4 * HALF), np.float32)
+    column = lax.broadcasted_iota(I32, (1, 4 * HALF), 1)
+    source = jnp.full((1, 4 * HALF), -1, I32)
     for side in range(4):
-        for c in range(6):
-            for j in range(10):
-                column = side * HALF + c * 10 + j
-                table[c * 20 + select_rows[side][j], column] = 1.0
-                table[LANES + c * 20 + select_rows[side][j], column] = 1.0
-    return table
+        for j in range(10):
+            for c in range(6):
+                here = column == side * HALF + c * 10 + j
+                source = jnp.where(here, c * 20 + select_rows[side][j], source)
+    row = lax.broadcasted_iota(I32, (2 * LANES, 4 * HALF), 0)
+    row = jnp.where(row >= LANES, row - LANES, row)
+    return (row == source).astype(F32).astype(BF16)
 
 
 def split(value):
@@ -77,26 +80,61 @@
     return lax.dot_general(a, b, dims, preferred_element_type=F32)
 
 
-NT = (((1,), (1,)), ((), ()))
 VMEM = pl.BlockSpec(memory_space=pltpu.VMEM)
 SMEM = pl.BlockSpec(memory_space=pltpu.SMEM)
 ANY = pl.BlockSpec(memory_space=pl.ANY)
+HBM = pl.BlockSpec(memory_space=pltpu.HBM)
+
+
+def cost(microseconds):
+    return pl.CostEstimate(
+        flops=0, transcendentals=0, bytes_accessed=int(microseconds * 3_000_000)
+    )
 
 
 def live_lanes(count, first, width):
     return ((lax.broadcasted_iota(I32, (1, width), 1) + first) < count).astype(F32)
 
 
+def rows_kernel(remote, count_ref, field_ref, list_ref, rows_ref, slot_ref, selector_ref):
+    blocks = field_ref.shape[1] // LANES
+    count = count_ref[0]
+    for block in range(blocks):
+        lanes = slice(block * LANES, (block + 1) * LANES)
+        value = field_ref[:, lanes] * live_lanes(count, block * LANES, LANES)
+        value = jnp.concatenate([value, jnp.zeros((LANES - UNK, LANES), F32)], axis=0)
+        rows_ref[lanes, :] = value.T
+    per_list = list_ref.shape[1] // LANES
+    for index in range(8):
+        for part in range(per_list):
+            row = index * per_list + part
+            face = list_ref[index : index + 1, part * LANES : (part + 1) * LANES]
+            slot_ref[row : row + 1, :] = jnp.maximum(face, 0) + remote
+    selector_ref[...] = trace_selector()
+
+
+def first_rows(part_count, right_side, lists):
+    remote = lists.shape[0] * lists.shape[1]
+    return pl.pallas_call(
+        functools.partial(rows_kernel, remote),
+        out_shape=(
+            jax.ShapeDtypeStruct((right_side.shape[1], LANES), F32),
+            jax.ShapeDtypeStruct((remote // LANES, LANES), I32),
+            jax.ShapeDtypeStruct((2 * LANES, 4 * HALF), BF16),
+        ),
+        in_specs=[SMEM, VMEM, VMEM],
+        out_specs=(VMEM,) * 3,
+        compiler_params=pltpu.CompilerParams(vmem_limit_bytes=4 * MIB),
+        cost_estimate=cost(2),
+        name="first_rows",
+    )(part_count, right_side, lists)
+
+
 def prep_kernel(
-    remote, count_ref, field_hbm, class_ref, lift_ref, link_ref,
-    rows_ref, pos_ref, tile_ref, index_ref, lift_hi_ref, lift_lo_ref,
-    field_ref, spread_ref, field_sem,
+    remote, _, class_ref, lift_ref, link_ref, normal_ref,
+    pos_ref, tile_ref, index_ref, lift_hi_ref, lift_lo_ref, plane_ref, spread_ref,
 ):
-    elements = field_ref.shape[1]
-    blocks = elements // LANES
-    count = count_ref[0]
-    field_copy = pltpu.make_async_copy(field_hbm, field_ref, field_sem)
-    field_copy.start()
+    blocks = class_ref.shape[0]
 
     class_row = lax.broadcasted_iota(I32, (CLASSES, LANES), 0)
     totals = jnp.zeros((CLASSES, LANES), F32)
@@ -129,6 +167,16 @@
         tile_ref[row : row + 1, :] = jnp.minimum(owner.astype(I32), CLASSES - 1)
     tile_ref[4:5, :] = end[CLASSES - 1 :, :].astype(I32)
 
+    spread_ref[...] = jnp.zeros(spread_ref.shape, F32)
+    for side in range(4):
+        block = lift_ref[:, side, :]
+        for c in range(6):
+            first = side * HALF + c * 10
+            spread_ref[first : first + 10, c * 20 : (c + 1) * 20] = block
+    high, low = split(spread_ref[...].T)
+    lift_hi_ref[...] = high
+    lift_lo_ref[...] = low
+
     link = link_ref[...]
     own = (
         lax.broadcasted_iota(I32, link.shape, 0) * LANES
@@ -137,49 +185,32 @@
     )
     index_ref[...] = jnp.where(link < 0, own, link)
 
-    spread_ref[...] = jnp.zeros(spread_ref.shape, F32)
-    for side in range(4):
-        block = lift_ref[side]
-        for c in range(6):
-            first = side * HALF + c * 10
-            spread_ref[c * 20 : (c + 1) * 20, first : first + 10] = block
-    high, low = split(spread_ref[...])
-    lift_hi_ref[...] = high
-    lift_lo_ref[...] = low
-
-    field_copy.wait()
-    for block in range(blocks):
-        lanes = slice(block * LANES, (block + 1) * LANES)
-        value = field_ref[:, lanes] * live_lanes(count, block * LANES, LANES)
-        value = jnp.concatenate([value, jnp.zeros((LANES - UNK, LANES), F32)], axis=0)
-        rows_ref[lanes, :] = value.T
-
-
-def prepare(part_count, right_side, elem_class, lift, link, remote):
-    elements = right_side.shape[1]
-    faces = link.shape[0]
+    for c in range(3):
+        for row in range(link.shape[0]):
+            plane_ref[c, row : row + 1, :] = normal_ref[c : c + 1, row * LANES : (row + 1) * LANES]
+
+
+def prepare(after, elem_class, lift, link, normal, remote):
+    elements, faces = elem_class.shape[0], link.shape[0]
     return pl.pallas_call(
         functools.partial(prep_kernel, remote),
         out_shape=(
-            jax.ShapeDtypeStruct((elements, LANES), F32),
             jax.ShapeDtypeStruct((elements // LANES, LANES), I32),
             jax.ShapeDtypeStruct((8, LANES), I32),
             jax.ShapeDtypeStruct((faces // LANES, LANES), I32),
             jax.ShapeDtypeStruct((LANES, 4 * HALF), BF16),
             jax.ShapeDtypeStruct((LANES, 4 * HALF), BF16),
+            jax.ShapeDtypeStruct((3, faces // LANES, LANES), F32),
         ),
-        in_specs=[SMEM, ANY, VMEM, VMEM, VMEM],
+        in_specs=[ANY] + [VMEM] * 4,
         out_specs=(VMEM,) * 6,
-        scratch_shapes=[
-            pltpu.VMEM(right_side.shape, F32),
-            pltpu.VMEM((LANES, 4 * HALF), F32),
-            pltpu.SemaphoreType.DMA(()),
-        ],
-        compiler_params=pltpu.CompilerParams(vmem_limit_bytes=8 * MIB),
+        scratch_shapes=[pltpu.VMEM((4 * HALF, LANES), F32)],
+        compiler_params=pltpu.CompilerParams(vmem_limit_bytes=4 * MIB),
+        cost_estimate=cost(3),
         name="prepare",
     )(
-        part_count, right_side, elem_class.reshape(elements // LANES, LANES), lift,
-        link.reshape(faces // LANES, LANES),
+        after, elem_class.reshape(elements // LANES, LANES), jnp.transpose(lift, (2, 0, 1)),
+        link.reshape(faces // LANES, LANES), normal,
     )
 
 
@@ -217,34 +248,57 @@
     lax.fori_loop(0, count // unroll, block, 0)
 
 
-def class_major(native_ref, stage_ref, class_ref):
-    rows = 16
-    pad = jnp.zeros((LANES - UNK, CLASSES), F32)
-
-    def chunk(index, carry):
-        for row in range(rows):
-            source = index * rows + row
-            value = native_ref[jnp.minimum(source, UNK - 1)].astype(F32)
-            value = jnp.where(source < UNK, value, 0.0)
-            value = jnp.concatenate([value, pad], axis=0).T
-            stage_ref[pl.ds(row, CLASSES, stride=STAGE_PITCH), :] = value
-        first = pl.multiple_of(index * rows, rows)
-        stage = stage_ref[...].reshape(CLASSES, STAGE_PITCH, LANES)[:, :rows].astype(BF16)
-        class_ref[:, pl.ds(first, rows), :] = stage
-        return carry
-
-    lax.fori_loop(0, LANES // rows, chunk, 0)
+def class_major(native_ref, turned_ref, stage_ref, part_ref, class_hbm, sems):
+    for half in range(2):
+        for row in range(CHUNK):
+            last = row * NODE_PITCH + UNK
+            turned_ref[half, last : last + LANES - UNK, :] = jnp.zeros((LANES - UNK, LANES), F32)
+
+    def store(first):
+        slot = first // CHUNK % 2
+        target = class_hbm.at[:, pl.ds(first, CHUNK), :]
+        return pltpu.make_async_copy(part_ref.at[slot], target, sems.at[slot])
+
+    for first in range(0, LANES, CHUNK):
+        count = min(CHUNK, UNK - first)
+
+        def collect(index, carry):
+            value = native_ref[index, first : first + count, :].astype(F32)
+            if count < CHUNK:
+                value = jnp.concatenate([value, jnp.zeros((CHUNK - count, CLASSES), F32)], axis=0)
+            for half in range(2):
+                turned_ref[half, pl.ds(index, CHUNK, stride=NODE_PITCH), :] = value[
+                    :, half * LANES : (half + 1) * LANES
+                ]
+            return carry
+
+        lax.fori_loop(0, UNK, collect, 0, unroll=24)
+
+        for row in range(CHUNK):
+            for half in range(2):
+                target = pl.ds(half * LANES * STAGE_PITCH + row, LANES, stride=STAGE_PITCH)
+                rows = slice(row * NODE_PITCH, row * NODE_PITCH + LANES)
+                stage_ref[target, :] = turned_ref[half, rows, :].T
+        stage = stage_ref[...].reshape(CLASSES, STAGE_PITCH, LANES)[:, :CHUNK]
+        if first >= 2 * CHUNK:
+            store(first - 2 * CHUNK).wait()
+        part_ref[first // CHUNK % 2] = stage.astype(BF16)
+        store(first).start()
+    return [store(LANES - 2 * CHUNK), store(LANES - CHUNK)]
 
 
 def exchange_kernel(grid_rows, grid_columns, with_classes, *refs):
     if with_classes:
-        (rows_ref, selector_ref, list_ref, native_hbm, table_ref, class_ref,
-         outgoing_ref, received_ref, send_sem, recv_sem, native_ref, stage_ref, native_sem) = refs
+        (rows_ref, selector_ref, list_any, native_hbm, table_ref, class_hbm,
+         list_ref, outgoing_ref, received_ref, local_sem, send_sem, recv_sem,
+         native_ref, turned_ref, stage_ref, part_ref, native_sem, part_sems) = refs
         native_copy = pltpu.make_async_copy(native_hbm, native_ref, native_sem)
         native_copy.start()
     else:
-        (rows_ref, selector_ref, list_ref, table_ref,
-         outgoing_ref, received_ref, send_sem, recv_sem) = refs
+        (rows_ref, selector_ref, list_any, table_ref,
+         list_ref, outgoing_ref, received_ref, local_sem, send_sem, recv_sem) = refs
+    list_copy = pltpu.make_async_copy(list_any, list_ref, local_sem)
+    list_copy.start()
     slots = outgoing_ref.shape[1]
     row, column = lax.axis_index("prow"), lax.axis_index("pcol")
 
@@ -279,24 +333,33 @@
             pl.semaphore_signal(barrier, inc=1, device_id=partner(index), device_id_type=MESH)
 
     write_traces(rows_ref, selector_ref, table_ref, 16 * slots)
-
-    near_rows = 1 + (row > 0).astype(I32) + (row < grid_rows - 1).astype(I32)
-    near_columns = 1 + (column > 0).astype(I32) + (column < grid_columns - 1).astype(I32)
-    pl.semaphore_wait(barrier, near_rows * near_columns - 1)
-
-    for index in (0, 2, 5, 7, 3, 4, 1, 6):
+    list_copy.wait()
+
+    def gather(index):
         first = index * 2 * slots
         gather_pairs(
             table_ref, list_ref, outgoing_ref.at[index], first, first + slots, 0, slots, 32
         )
 
+    early, late = (0, 2, 5, 7), (3, 4, 1, 6)
+    for index in early:
+        gather(index)
+
+    near_rows = 1 + (row > 0).astype(I32) + (row < grid_rows - 1).astype(I32)
+    near_columns = 1 + (column > 0).astype(I32) + (column < grid_columns - 1).astype(I32)
+    pl.semaphore_wait(barrier, near_rows * near_columns - 1)
+
+    for index in early + late:
+        if index in late:
+            gather(index)
+
         @pl.when(present(index))
         def _(index=index):
             transfer(index).start()
 
     if with_classes:
         native_copy.wait()
-        class_major(native_ref, stage_ref, class_ref)
+        stores = class_major(native_ref, turned_ref, stage_ref, part_ref, class_hbm, part_sems)
 
     left = lax.broadcasted_iota(I32, (slots, LANES), 1) < HALF
     for index in (1, 6, 3, 4, 0, 2, 5, 7):
@@ -314,14 +377,20 @@
         def _(index=index):
             transfer(index).wait_send()
 
+    if with_classes:
+        for store in stores:
+            store.wait()
+
 
 def exchange(rows, selector, lists, native=None):
     slots = lists.shape[0] // 16
     with_classes = native is not None
     out_shape = [jax.ShapeDtypeStruct((16 * slots + 4 * rows.shape[0], LANES), F32)]
     scratch = [
+        pltpu.SMEM(lists.shape, I32),
         pltpu.VMEM((8, slots, LANES), F32),
         pltpu.VMEM((8, slots, LANES), F32),
+        pltpu.SemaphoreType.DMA(()),
         pltpu.SemaphoreType.DMA((8,)),
         pltpu.SemaphoreType.DMA((8,)),
     ]
@@ -330,8 +399,11 @@
         out_shape.append(jax.ShapeDtypeStruct((CLASSES, LANES, LANES), BF16))
         scratch += [
             pltpu.VMEM(native.shape, BF16),
+            pltpu.VMEM((2, CHUNK * NODE_PITCH, LANES), F32),
             pltpu.VMEM((CLASSES * STAGE_PITCH, LANES), F32),
+            pltpu.VMEM((2, CLASSES, CHUNK, LANES), BF16),
             pltpu.SemaphoreType.DMA(()),
+            pltpu.SemaphoreType.DMA((2,)),
         ]
         operands.append(native)
     return pl.pallas_call(
@@ -339,13 +411,14 @@
             exchange_kernel, lax.axis_size("prow"), lax.axis_size("pcol"), with_classes
         ),
         out_shape=tuple(out_shape),
-        in_specs=[VMEM, VMEM, SMEM] + [ANY] * with_classes,
-        out_specs=(VMEM,) * len(out_shape),
+        in_specs=[VMEM, VMEM, ANY] + [HBM] * with_classes,
+        out_specs=(VMEM,) + (HBM,) * with_classes,
         scratch_shapes=scratch,
         compiler_params=pltpu.CompilerParams(
             collective_id=2 if with_classes else 0, has_side_effects=True,
-            vmem_limit_bytes=(36 if with_classes else 16) * MIB,
+            vmem_limit_bytes=(44 if with_classes else 8) * MIB,
         ),
+        cost_estimate=cost(14),
         name="exchange_first" if with_classes else "exchange",
     )(*operands)
 
@@ -401,16 +474,24 @@
 
 
 def image_kernel(
-    count_ref, index_ref, pos_ref, tile_ref,
+    count_ref, index_any, pos_any, tile_any,
     table_ref, lift_hi_ref, lift_lo_ref,
-    link_ref, orient_ref, normal_ref, quotient_ref, class_ref,
+    link_ref, orient_ref, normal_ref, quotient_ref, class_hbm,
     image_ref,
+    index_ref, pos_ref, tile_ref, smem_sems, class_ref, class_sem,
     picked_ref, node_ref, flux_ref, coupled_ref, sorted_ref, solved_ref,
 ):
+    index_copy = pltpu.make_async_copy(index_any, index_ref, smem_sems.at[0])
+    pos_copy = pltpu.make_async_copy(pos_any, pos_ref, smem_sems.at[1])
+    tile_copy = pltpu.make_async_copy(tile_any, tile_ref, smem_sems.at[2])
+    class_copy = pltpu.make_async_copy(class_hbm, class_ref, class_sem)
+    for copy in (index_copy, pos_copy, tile_copy, class_copy):
+        copy.start()
     elements = image_ref.shape[0]
     blocks = elements // LANES
     chunks = blocks // 8
 
+    index_copy.wait()
     gather_pairs(table_ref, index_ref, picked_ref, 0, 2 * elements, 0, 2 * elements, 64)
 
     def transpose(index, carry):
@@ -470,6 +551,8 @@
     lax.fori_loop(0, blocks // 2, lift, 0, unroll=4)
 
     unroll = 16
+    pos_copy.wait()
+    tile_copy.wait()
 
     def place(index, carry):
         base = pl.multiple_of(index * unroll, unroll)
@@ -479,12 +562,14 @@
 
     lax.fori_loop(0, elements // unroll, place, 0)
 
+    class_copy.wait()
+
     def solve(index, carry):
         for step in range(GROUP):
             tile = index * GROUP + step
             base = pl.multiple_of(tile * TILE, TILE)
             high, low = split(sorted_ref[pl.ds(base, TILE), :])
-            result = dot(jnp.concatenate([high, low], axis=0), class_ref[tile_ref[tile]], NT)
+            result = dot(jnp.concatenate([high, low], axis=0), class_ref[tile_ref[tile]])
             solved_ref[pl.ds(base, TILE), :] = result[:TILE] + result[TILE:]
         return carry
 
@@ -506,9 +591,15 @@
     return pl.pallas_call(
         image_kernel,
         out_shape=jax.ShapeDtypeStruct((elements, LANES), F32),
-        in_specs=[SMEM] * 4 + [VMEM] * 8,
+        in_specs=[SMEM] + [ANY] * 3 + [VMEM] * 7 + [HBM],
         out_specs=VMEM,
         scratch_shapes=[
+            pltpu.SMEM(indices.shape, I32),
+            pltpu.SMEM(pos.shape, I32),
+            pltpu.SMEM(tiles.shape, I32),
+            pltpu.SemaphoreType.DMA((3,)),
+            pltpu.VMEM(classes.shape, BF16),
+            pltpu.SemaphoreType.DMA(()),
             pltpu.VMEM((2 * elements, LANES), F32),
             pltpu.VMEM((2 * elements // LANES * NODE_PITCH, LANES), F32),
             pltpu.VMEM((elements // LANES * FLUX_PITCH, LANES), F32),
@@ -516,21 +607,24 @@
             pltpu.VMEM((slots, LANES), F32),
             pltpu.VMEM((slots, LANES), F32),
         ],
-        compiler_params=pltpu.CompilerParams(vmem_limit_bytes=24 * MIB),
+        compiler_params=pltpu.CompilerParams(vmem_limit_bytes=44 * MIB),
+        cost_estimate=cost(20),
         name="image",
     )(
         part_count, indices, pos, tiles, table, lift_hi, lift_lo,
-        link.reshape(-1, LANES), orient.reshape(-1, LANES), normal.reshape(3, -1, LANES),
+        link.reshape(-1, LANES), orient.reshape(-1, LANES), normal,
         quotient.reshape(-1, LANES), classes,
     )
 
 
-def gram_partials(first_ref, second_ref, third_ref, gram_ref):
+def gram_partials(first_ref, second_ref, third_ref, second_out, third_out, gram_ref):
     elements = first_ref.shape[0]
 
     def block(index, sums):
         rows = pl.ds(pl.multiple_of(index * LANES, LANES), LANES)
         f, t, u = first_ref[rows, :], second_ref[rows, :], third_ref[rows, :]
+        second_out[:, rows] = t.T[:UNK]
+        third_out[:, rows] = u.T[:UNK]
         pairs = (f * f, f * t, t * t, f * u, t * u, u * u)
         return tuple(
             total + jnp.sum(pair.reshape(LANES // 8, 8, LANES), axis=0)
@@ -544,8 +638,8 @@
     gram_ref[6:, :] = jnp.zeros((2, LANES), F32)
 
 
-def total_kernel(grid_rows, grid_columns, first_ref, second_ref, third_ref, total_ref,
-                 part_ref, over_rows, over_columns, send_row, recv_row, send_column, recv_column):
+def total_kernel(grid_rows, grid_columns, first_ref, second_ref, third_ref,
+                 total_ref, second_out, third_out, part_ref, over_rows, over_columns, send_row, recv_row, send_column, recv_column):
     row, column = lax.axis_index("prow"), lax.axis_index("pcol")
 
     def row_partner(step):
@@ -563,24 +657,27 @@
         pl.semaphore_signal(
             barrier, inc=1, device_id=(row, column_partner(step)), device_id_type=MESH
         )
-    gram_partials(first_ref, second_ref, third_ref, part_ref)
+    gram_partials(first_ref, second_ref, third_ref, second_out, third_out, part_ref)
     pl.semaphore_wait(barrier, grid_rows + grid_columns - 2)
 
     def row_copy(step):
         return pltpu.make_async_remote_copy(
             src_ref=part_ref,
             dst_ref=over_rows.at[step],
-            send_sem=send_row.at[step],
-            recv_sem=recv_row.at[step],
+            send_sem=send_row,
+            recv_sem=recv_row,
             device_id=(row_partner(step), column),
             device_id_type=MESH,
         )
 
+    def wait_all(buffer, count, sem):
+        landed = buffer.at[pl.ds(1, count)]
+        pltpu.make_async_copy(landed, landed, sem).wait()
+
     for step in range(1, grid_rows):
         row_copy(step).start()
     over_rows[0] = part_ref[...]
-    for step in range(1, grid_rows):
-        row_copy(step).wait()
+    wait_all(over_rows, grid_rows - 1, recv_row)
     total = over_rows[row]
     for source in range(1, grid_rows):
         total = total + over_rows[lax.rem(row - source + grid_rows, grid_rows)]
@@ -590,20 +687,21 @@
         return pltpu.make_async_remote_copy(
             src_ref=over_columns.at[0],
             dst_ref=over_columns.at[step],
-            send_sem=send_column.at[step],
-            recv_sem=recv_column.at[step],
+            send_sem=send_column,
+            recv_sem=recv_column,
             device_id=(row, column_partner(step)),
             device_id_type=MESH,
         )
 
     for step in range(1, grid_columns):
         column_copy(step).start()
-    for step in range(1, grid_columns):
-        column_copy(step).wait()
+    wait_all(over_columns, grid_columns - 1, recv_column)
     total = over_columns[column]
     for source in range(1, grid_columns):
         total = total + over_columns[lax.rem(column - source + grid_columns, grid_columns)]
     total_ref[...] = total
+    wait_all(over_rows, grid_rows - 1, send_row)
+    wait_all(over_columns, grid_columns - 1, send_column)
 
 
 def total_over_devices(first, second, third):
@@ -611,21 +709,26 @@
     part = (8, LANES)
     return pl.pallas_call(
         functools.partial(total_kernel, grid_rows, grid_columns),
-        out_shape=jax.ShapeDtypeStruct(part, F32),
+        out_shape=(
+            jax.ShapeDtypeStruct(part, F32),
+            jax.ShapeDtypeStruct((UNK, first.shape[0]), F32),
+            jax.ShapeDtypeStruct((UNK, first.shape[0]), F32),
+        ),
         in_specs=[VMEM] * 3,
-        out_specs=VMEM,
+        out_specs=(VMEM,) * 3,
         scratch_shapes=[
             pltpu.VMEM(part, F32),
             pltpu.VMEM((grid_rows,) + part, F32),
             pltpu.VMEM((grid_columns,) + part, F32),
-            pltpu.SemaphoreType.DMA((grid_rows,)),
-            pltpu.SemaphoreType.DMA((grid_rows,)),
-            pltpu.SemaphoreType.DMA((grid_columns,)),
-            pltpu.SemaphoreType.DMA((grid_columns,)),
+            pltpu.SemaphoreType.DMA(()),
+            pltpu.SemaphoreType.DMA(()),
+            pltpu.SemaphoreType.DMA(()),
+            pltpu.SemaphoreType.DMA(()),
         ],
         compiler_params=pltpu.CompilerParams(
             collective_id=1, has_side_effects=True, vmem_limit_bytes=8 * MIB
         ),
+        cost_estimate=cost(12),
         name="total",
     )(first, second, third)
 
@@ -652,14 +755,14 @@
 
     alive = live_lanes(count_ref[0], pl.program_id(0) * width, width)
     f = field_ref[...] * alive
-    t, u = second_ref[...].T[:UNK], third_ref[...].T[:UNK]
+    t, u = second_ref[...], third_ref[...]
     basis_ref[0] = f * (1.0 / beta)
     basis_ref[1] = t * k1 + f * (p * k1)
     basis_ref[2] = u * k2 + t * (q * k2) + f * (w * k2)
 
-    at_row = lax.broadcasted_iota(I32, (3, 2), 0)
-    at_column = lax.broadcasted_iota(I32, (3, 2), 1)
-    hess = jnp.zeros((3, 2), F32)
+    at_row = lax.broadcasted_iota(I32, (2, 3), 1)
+    at_column = lax.broadcasted_iota(I32, (2, 3), 0)
+    hess = jnp.zeros((2, 3), F32)
     for i, j, value in ((0, 0, h00), (1, 0, h10), (0, 1, h01), (1, 1, h11), (2, 1, h21)):
         hess = jnp.where(jnp.logical_and(at_row == i, at_column == j), value, hess)
     hess_ref[...] = hess
@@ -667,24 +770,23 @@
 
 def finish(weight, part_count, total, right_side, second, third):
     elements = right_side.shape[1]
-    width = 512
-    rows = pl.BlockSpec((width, LANES), lambda i: (i, 0))
+    width = 256
     field = pl.BlockSpec((UNK, width), lambda i: (0, i))
     return pl.pallas_call(
         functools.partial(finish_kernel, weight),
         grid=(elements // width,),
         out_shape=(
             jax.ShapeDtypeStruct((3, UNK, elements), F32),
-            jax.ShapeDtypeStruct((3, 2), F32),
+            jax.ShapeDtypeStruct((2, 3), F32),
         ),
         in_specs=[
             pl.BlockSpec(memory_space=pltpu.SMEM),
             pl.BlockSpec((8, LANES), lambda i: (0, 0)),
-            field, rows, rows,
+            field, field, field,
         ],
         out_specs=(
             pl.BlockSpec((3, UNK, width), lambda i: (0, 0, i)),
-            pl.BlockSpec((3, 2), lambda i: (0, 0)),
+            pl.BlockSpec((2, 3), lambda i: (0, 0)),
         ),
         compiler_params=pltpu.CompilerParams(vmem_limit_bytes=12 * MIB),
         name="finish",
@@ -706,28 +808,27 @@
     unknowns, elements = right_side.shape
     all_subdomains = lax.axis_size("prow") * lax.axis_size("pcol")
     weight = 1.0 / (unknowns * elements * all_subdomains)
-    lists = bound_face.reshape(-1)
-    lists = jnp.maximum(lists, 0) + lists.shape[0]
-    selector = jnp.asarray(trace_selector(), BF16)
     native = jnp.transpose(inverse_table, (1, 2, 0))
-
-    first, pos, tiles, indices, lift_hi, lift_lo = prepare(
-        part_count, right_side, elem_class, lift, face_link, lists.shape[0]
+    first, lists, selector = first_rows(part_count, right_side, bound_face[0])
+    lists = lists.reshape(-1)
+    first_table, classes = exchange(first, selector, lists, native)
+    pos, tiles, indices, lift_hi, lift_lo, normal = prepare(
+        first_table, elem_class, lift, face_link, face_normal, lists.shape[0]
     )
     pos, tiles, indices = pos.reshape(-1), tiles.reshape(-1), indices.reshape(-1)
-    first_table, classes = exchange(first, selector, lists, native)
 
     def operator_image(table):
         return image(
             part_count, indices, pos, tiles, table, lift_hi, lift_lo, face_link, face_orient,
-            face_normal, boundary_metric_quotient, classes,
+            normal, boundary_metric_quotient, classes,
         )
 
     second = operator_image(first_table)
     (second_table,) = exchange(second, selector, lists)
     third = operator_image(second_table)
-    total = total_over_devices(first, second, third)
-    return finish(weight, part_count, total, right_side, second, third)
+    total, second_columns, third_columns = total_over_devices(first, second, third)
+    basis, hess = finish(weight, part_count, total, right_side, second_columns, third_columns)
+    return (basis, hess.T)
 
 
 def solution(mesh):

time: 111 us -> 91.3 us (0.82)
  local copies, waits for them, and re-layouts: 12.4 us -> 1.94 us
  Pallas kernels: 96.3 us -> 87.7 us
    unnamed x26 -> x18, local copies, waits for them, and re-layouts: 11.8 us -> 1.94 us
    pallas_call x2, Pallas kernels: 43.6 us -> 38.3 us  [image(): pl.pallas_call(image_kernel, out_shape=jax.ShapeDtypeStruct((elements, LA...]
    pallas_call x1, Pallas kernels: 20.1 us -> 17.2 us  [total_over_devices(): pl.pallas_call(functools.partial(total_kernel, grid_rows, grid_columns),...]
    pallas_call x2, Pallas kernels: 28 us -> 26.2 us  [exchange(): pl.pallas_call(functools.partial(exchange_kernel, lax.axis_size('prow'),...]
    pallas_call x1, Pallas kernels: 2.71 us -> 4.24 us  [finish(): pl.pallas_call(functools.partial(finish_kernel, weight), grid=(elements /...]
where the time goes in v4:
time: 91.3 us; the launch traced here: 91.1 us
  Pallas kernels  87.7 us (96%)
  local copies, waits for them, and re-layouts  1.94 us (2%)
  between operations  1.44 us (2%)
    pallas_call x2, Pallas kernels, image(): pl.pallas_call(image_kernel, out_shape=jax.ShapeDtypeStruct((elements, LA...  38.3 us
    pallas_call x2, Pallas kernels, exchange(): pl.pallas_call(functools.partial(exchange_kernel, lax.axis_size('prow'),...  26.2 us
    pallas_call x1, Pallas kernels, total_over_devices(): pl.pallas_call(functools.partial(total_kernel, grid_rows, grid_columns),...  17.2 us
    pallas_call x1, Pallas kernels, finish(): pl.pallas_call(functools.partial(finish_kernel, weight), grid=(elements /...  4.24 us
    unnamed x18, local copies, waits for them, and re-layouts  1.94 us

profile of v4, /device:TPU:1, one launch (start us, length us, event | category | flops | bytes accessed | tf_op | source)
XLA Modules:
  0.0 91.1 jit_solution(3011908255214031108)
XLA Ops:
  0.6 0.0 copy-start.8
  1.3 0.0 copy-start
  1.3 1.2 %copy-done = f32[120,2048]{1,0:T(8,128)S(1)} copy-done((f32[120,2048]{1,0:T(8,128)S(1)}, f32[120,2048]{1,0:T(8,128)}, u32[]{:S(2)}) %copy-start) | copy-done | bytes 983064
  2.5 0.0 copy-start.7
  2.5 0.7 copy-done.7
  3.2 0.0 copy-start.2
  3.2 0.0 copy-start.5
  3.2 0.0 copy-start.6
  3.2 0.4 first_rows.1
  3.7 0.0 copy-start.3
  3.7 0.0 copy-start.4
  3.7 15.9 %exchange_first.1 = (f32[11264,128]{1,0:T(8,128)S(1)}, bf16[256,128,128]{2,1,0:T(8,128)(2,1)}) custom-call(f32[2048,128]{1,0:T(8,128)S(1)} %get-tuple-element.18.refs_0_.first_ref, bf16[256,256]{1,0:T(8,128)(2,1)S(1)} %get-tuple-element.19.refs_1_, s32[3072]{0:T(1024)S(1)} %bitcast.21, bf16[120,120,256]{2,1,0:T(8,128)(2,1)} %bitcast.30), custom_call_target="tpu_custom_call" | custom-call | bytes 42000000 | tf_op jit(solution)/shard_map/exchange_first/pallas_call | solution.py:409
  19.6 0.0 copy-done.8
  19.6 0.0 copy-done.2
  19.6 0.0 copy-done.5
  19.6 0.0 copy-done.6
  19.6 1.3 %prepare.1 = (s32[16,128]{1,0:T(8,128)S(1)}, s32[8,128]{1,0:T(8,128)S(1)}, s32[64,128]{1,0:T(8,128)S(1)}, bf16[128,256]{1,0:T(8,128)(2,1)S(1)}, bf16[128,256]{1,0:T(8,128)(2,1)S(1)}, /*index=5*/f32[3,64,128]{2,1,0:T(8,128)S(1)}) custom-call(f32[11264,128]{1,0:T(8,128)S(1)} %get-tuple-element.21._.table_ref, s32[16,128]{1,0:T(8,128)S(1)} %bitcast.29, ...), custom_call_target="tpu_custom_call" | custom-call | bytes 9000000 | tf_op jit(solution)/shard_map/prepare/pallas_call | solution.py:195
  20.9 0.0 copy-done.3
  21.0 0.0 copy-done.4
  21.0 19.2 %image.2.refs_0_.second_ref = f32[2048,128]{1,0:T(8,128)S(1)} custom-call(s32[1]{0:T(128)S(6)} %copy.12.count_ref, s32[8192]{0:T(1024)S(1)} %bitcast.19, s32[2048]{0:T(1024)S(1)} %bitcast.23, s32[1024]{0:T(1024)S(1)} %bitcast.26, f32[11264,128]{1,0:T(8,128)S(1)} %get-tuple-element.21._.table_ref, bf16[128,256]{1,0:T(8,128)(2,1)S(1)} %get-tuple-element.25.lift_hi_ref, ...), custom_call_target="tpu_custom_call" | custom-call | bytes 60000000 | tf_op jit(solution)/shard_map/image/pallas_call | solution.py:591
  40.1 10.3 %exchange.1.table_ref = f32[11264,128]{1,0:T(8,128)S(1)} custom-call(f32[2048,128]{1,0:T(8,128)S(1)} %image.2.refs_0_.second_ref, bf16[256,256]{1,0:T(8,128)(2,1)S(1)} %get-tuple-element.19.refs_1_, s32[3072]{0:T(1024)S(1)} %bitcast.22), custom_call_target="tpu_custom_call" | custom-call | bytes 42000000 | tf_op jit(solution)/shard_map/exchange/pallas_call | solution.py:409
  50.5 0.0 copy-start.1
  50.5 19.1 %image.3.third_ref = f32[2048,128]{1,0:T(8,128)S(1)} custom-call(s32[1]{0:T(128)S(6)} %copy.12.count_ref, s32[8192]{0:T(1024)S(1)} %bitcast.20, s32[2048]{0:T(1024)S(1)} %bitcast.24, s32[1024]{0:T(1024)S(1)} %bitcast.27, f32[11264,128]{1,0:T(8,128)S(1)} %exchange.1.table_ref, bf16[128,256]{1,0:T(8,128)(2,1)S(1)} %get-tuple-element.25.lift_hi_ref, ...), custom_call_target="tpu_custom_call" | custom-call | bytes 60000000 | tf_op jit(solution)/shard_map/image/pallas_call | solution.py:591
  69.6 17.2 %total.1 = (f32[8,128]{1,0:T(8,128)S(1)}, f32[120,2048]{1,0:T(8,128)S(1)}, f32[120,2048]{1,0:T(8,128)S(1)}) custom-call(f32[2048,128]{1,0:T(8,128)S(1)} %get-tuple-element.18.refs_0_.first_ref, f32[2048,128]{1,0:T(8,128)S(1)} %image.2.refs_0_.second_ref, f32[2048,128]{1,0:T(8,128)S(1)} %image.3.third_ref), custom_call_target="tpu_custom_call" | custom-call | bytes 36000000 | tf_op jit(solution)/shard_map/total/pallas_call | solution.py:710
  86.8 0.0 copy-done.1
  86.9 4.2 %finish.1 = (f32[3,120,2048]{2,1,0:T(8,128)}, f32[2,3]{1,0:T(2,128)}) custom-call(s32[1]{0:T(128)S(6)} %copy.12.count_ref, f32[8,128]{1,0:T(8,128)S(1)} %get-tuple-element.29.total_ref, f32[120,2048]{1,0:T(8,128)S(1)} %copy-done.1, f32[120,2048]{1,0:T(8,128)S(1)} %get-tuple-element.30.second_ref, f32[120,2048]{1,0:T(8,128)S(1)} %get-tuple-element.31.third_ref), custom_call_target="tpu_custom_call" | custom-call | tf_op jit(solution)/shard_map/finish/pallas_call | solution.py:775
Async XLA Ops:
  0.6 19.0 %copy-start.8 = (s32[2048]{0:T(1024)S(1)}, s32[2048]{0:T(1024)}, u32[]{:S(2)}) copy-start(s32[2048]{0:T(1024)} %param.12) | copy-start | bytes 24580
  1.3 1.2 %copy-start = (f32[120,2048]{1,0:T(8,128)S(1)}, f32[120,2048]{1,0:T(8,128)}, u32[]{:S(2)}) copy-start(f32[120,2048]{1,0:T(8,128)} %field_ref.3) | copy-start | bytes 2949124
  2.5 0.7 copy-start.7
  3.2 16.4 %copy-start.2 = (s32[8192]{0:T(1024)S(1)}, s32[8192]{0:T(1024)}, u32[]{:S(2)}) copy-start(s32[8192]{0:T(1024)} %param.13) | copy-start | bytes 98308
  3.2 16.4 %copy-start.5 = (f32[3,8192]{1,0:T(4,128)S(1)}, f32[3,8192]{1,0:T(4,128)}, u32[]{:S(2)}) copy-start(f32[3,8192]{1,0:T(4,128)} %normal_ref.1) | copy-start | bytes 294916
  3.2 16.4 %copy-start.6 = (f32[4,20,10]{1,0,2:T(4,128)S(1)}, f32[4,20,10]{1,0,2:T(4,128)}, u32[]{:S(2)}) copy-start(f32[4,20,10]{1,0,2:T(4,128)} %param.18) | copy-start | bytes 9604
  3.7 17.3 %copy-start.3 = (s32[8192]{0:T(1024)S(1)}, s32[8192]{0:T(1024)}, u32[]{:S(2)}) copy-start(s32[8192]{0:T(1024)} %param.14) | copy-start | bytes 98308
  3.7 17.3 %copy-start.4 = (f32[8192]{0:T(1024)S(1)}, f32[8192]{0:T(1024)}, u32[]{:S(2)}) copy-start(f32[8192]{0:T(1024)} %param.16) | copy-start | bytes 98308
  50.5 36.4 %copy-start.1 = (f32[120,2048]{1,0:T(8,128)S(1)}, f32[120,2048]{1,0:T(8,128)}, u32[]{:S(2)}) copy-start(f32[120,2048]{1,0:T(8,128)} %field_ref.3) | copy-start | bytes 2949124

commit v5 on v4

--- a/solution.py
+++ b/solution.py
@@ -22,6 +22,7 @@
 NODE_PITCH = 136
 FLUX_PITCH = 264
 STAGE_PITCH = 24
+SLAB = 24
 CHUNK = 16
 
 
@@ -248,6 +249,18 @@
     lax.fori_loop(0, count // unroll, block, 0)
 
 
+def element_order(solved_ref, pos_ref, rows_ref):
+    unroll = 32
+
+    def fetch(index, carry):
+        base = pl.multiple_of(index * unroll, unroll)
+        for step in range(unroll):
+            rows_ref[pl.ds(base + step, 1), :] = solved_ref[pl.ds(pos_ref[base + step], 1), :]
+        return carry
+
+    lax.fori_loop(0, rows_ref.shape[0] // unroll, fetch, 0)
+
+
 def class_major(native_ref, turned_ref, stage_ref, part_ref, class_hbm, sems):
     for half in range(2):
         for row in range(CHUNK):
@@ -295,8 +308,11 @@
         native_copy = pltpu.make_async_copy(native_hbm, native_ref, native_sem)
         native_copy.start()
     else:
-        (rows_ref, selector_ref, list_any, table_ref,
-         list_ref, outgoing_ref, received_ref, local_sem, send_sem, recv_sem) = refs
+        (solved_ref, pos_any, selector_ref, list_any, table_ref, rows_ref,
+         list_ref, outgoing_ref, received_ref, local_sem, send_sem, recv_sem,
+         pos_ref, pos_sem) = refs
+        pos_copy = pltpu.make_async_copy(pos_any, pos_ref, pos_sem)
+        pos_copy.start()
     list_copy = pltpu.make_async_copy(list_any, list_ref, local_sem)
     list_copy.start()
     slots = outgoing_ref.shape[1]
@@ -332,6 +348,9 @@
         def _(index=index):
             pl.semaphore_signal(barrier, inc=1, device_id=partner(index), device_id_type=MESH)
 
+    if not with_classes:
+        pos_copy.wait()
+        element_order(solved_ref, pos_ref, rows_ref)
     write_traces(rows_ref, selector_ref, table_ref, 16 * slots)
     list_copy.wait()
 
@@ -341,7 +360,7 @@
             table_ref, list_ref, outgoing_ref.at[index], first, first + slots, 0, slots, 32
         )
 
-    early, late = (0, 2, 5, 7), (3, 4, 1, 6)
+    early, late = ((0, 2, 5, 7), (3, 4, 1, 6)) if with_classes else ((0,), (2, 5, 7, 3, 4, 1, 6))
     for index in early:
         gather(index)
 
@@ -382,10 +401,11 @@
             store.wait()
 
 
-def exchange(rows, selector, lists, native=None):
+def exchange(rows, selector, lists, native=None, pos=None):
     slots = lists.shape[0] // 16
     with_classes = native is not None
-    out_shape = [jax.ShapeDtypeStruct((16 * slots + 4 * rows.shape[0], LANES), F32)]
+    elements = rows.shape[0] if with_classes else pos.shape[0]
+    out_shape = [jax.ShapeDtypeStruct((16 * slots + 4 * elements, LANES), F32)]
     scratch = [
         pltpu.SMEM(lists.shape, I32),
         pltpu.VMEM((8, slots, LANES), F32),
@@ -394,8 +414,9 @@
         pltpu.SemaphoreType.DMA((8,)),
         pltpu.SemaphoreType.DMA((8,)),
     ]
-    operands = [rows, selector, lists]
     if with_classes:
+        operands = [rows, selector, lists, native]
+        in_specs, out_specs = [VMEM, VMEM, ANY, HBM], (VMEM, HBM)
         out_shape.append(jax.ShapeDtypeStruct((CLASSES, LANES, LANES), BF16))
         scratch += [
             pltpu.VMEM(native.shape, BF16),
@@ -405,14 +426,18 @@
             pltpu.SemaphoreType.DMA(()),
             pltpu.SemaphoreType.DMA((2,)),
         ]
-        operands.append(native)
+    else:
+        operands = [rows, pos, selector, lists]
+        in_specs, out_specs = [VMEM, ANY, VMEM, ANY], (VMEM, VMEM)
+        out_shape.append(jax.ShapeDtypeStruct((elements, LANES), F32))
+        scratch += [pltpu.SMEM(pos.shape, I32), pltpu.SemaphoreType.DMA(())]
     return pl.pallas_call(
         functools.partial(
             exchange_kernel, lax.axis_size("prow"), lax.axis_size("pcol"), with_classes
         ),
         out_shape=tuple(out_shape),
-        in_specs=[VMEM, VMEM, ANY] + [HBM] * with_classes,
-        out_specs=(VMEM,) + (HBM,) * with_classes,
+        in_specs=in_specs,
+        out_specs=out_specs,
         scratch_shapes=scratch,
         compiler_params=pltpu.CompilerParams(
             collective_id=2 if with_classes else 0, has_side_effects=True,
@@ -477,9 +502,9 @@
     count_ref, index_any, pos_any, tile_any,
     table_ref, lift_hi_ref, lift_lo_ref,
     link_ref, orient_ref, normal_ref, quotient_ref, class_hbm,
-    image_ref,
+    solved_ref,
     index_ref, pos_ref, tile_ref, smem_sems, class_ref, class_sem,
-    picked_ref, node_ref, flux_ref, coupled_ref, sorted_ref, solved_ref,
+    picked_ref, node_ref, flux_ref, coupled_ref, sorted_ref,
 ):
     index_copy = pltpu.make_async_copy(index_any, index_ref, smem_sems.at[0])
     pos_copy = pltpu.make_async_copy(pos_any, pos_ref, smem_sems.at[1])
@@ -487,7 +512,7 @@
     class_copy = pltpu.make_async_copy(class_hbm, class_ref, class_sem)
     for copy in (index_copy, pos_copy, tile_copy, class_copy):
         copy.start()
-    elements = image_ref.shape[0]
+    elements = coupled_ref.shape[0]
     blocks = elements // LANES
     chunks = blocks // 8
 
@@ -575,14 +600,6 @@
 
     lax.fori_loop(0, (tile_ref[4 * LANES] + (GROUP - 1)) // GROUP, solve, 0)
 
-    def fetch(index, carry):
-        base = pl.multiple_of(index * unroll, unroll)
-        for step in range(unroll):
-            image_ref[pl.ds(base + step, 1), :] = solved_ref[pl.ds(pos_ref[base + step], 1), :]
-        return carry
-
-    lax.fori_loop(0, elements // unroll, fetch, 0)
-
 
 def image(part_count, indices, pos, tiles, table, lift_hi, lift_lo,
           link, orient, normal, quotient, classes):
@@ -590,7 +607,7 @@
     slots = TILE_ROWS * TILE
     return pl.pallas_call(
         image_kernel,
-        out_shape=jax.ShapeDtypeStruct((elements, LANES), F32),
+        out_shape=jax.ShapeDtypeStruct((slots, LANES), F32),
         in_specs=[SMEM] + [ANY] * 3 + [VMEM] * 7 + [HBM],
         out_specs=VMEM,
         scratch_shapes=[
@@ -605,7 +622,6 @@
             pltpu.VMEM((elements // LANES * FLUX_PITCH, LANES), F32),
             pltpu.VMEM((elements, LANES), F32),
             pltpu.VMEM((slots, LANES), F32),
-            pltpu.VMEM((slots, LANES), F32),
         ],
         compiler_params=pltpu.CompilerParams(vmem_limit_bytes=44 * MIB),
         cost_estimate=cost(20),
@@ -638,9 +654,11 @@
     gram_ref[6:, :] = jnp.zeros((2, LANES), F32)
 
 
-def total_kernel(grid_rows, grid_columns, first_ref, second_ref, third_ref,
-                 total_ref, second_out, third_out, part_ref, over_rows, over_columns, send_row, recv_row, send_column, recv_column):
+def total_kernel(grid_rows, grid_columns, first_ref, second_ref, solved_ref, pos_any,
+                 total_ref, second_out, third_out, third_ref, pos_ref, pos_sem, part_ref, over_rows, over_columns, send_row, recv_row, send_column, recv_column):
     row, column = lax.axis_index("prow"), lax.axis_index("pcol")
+    pos_copy = pltpu.make_async_copy(pos_any, pos_ref, pos_sem)
+    pos_copy.start()
 
     def row_partner(step):
         return lax.rem(row + step, grid_rows)
@@ -657,6 +675,8 @@
         pl.semaphore_signal(
             barrier, inc=1, device_id=(row, column_partner(step)), device_id_type=MESH
         )
+    pos_copy.wait()
+    element_order(solved_ref, pos_ref, third_ref)
     gram_partials(first_ref, second_ref, third_ref, second_out, third_out, part_ref)
     pl.semaphore_wait(barrier, grid_rows + grid_columns - 2)
 
@@ -704,7 +724,7 @@
     wait_all(over_columns, grid_columns - 1, send_column)
 
 
-def total_over_devices(first, second, third):
+def total_over_devices(first, second, solved, pos):
     grid_rows, grid_columns = lax.axis_size("prow"), lax.axis_size("pcol")
     part = (8, LANES)
     return pl.pallas_call(
@@ -714,9 +734,12 @@
             jax.ShapeDtypeStruct((UNK, first.shape[0]), F32),
             jax.ShapeDtypeStruct((UNK, first.shape[0]), F32),
         ),
-        in_specs=[VMEM] * 3,
+        in_specs=[VMEM] * 3 + [ANY],
         out_specs=(VMEM,) * 3,
         scratch_shapes=[
+            pltpu.VMEM(first.shape, F32),
+            pltpu.SMEM(pos.shape, I32),
+            pltpu.SemaphoreType.DMA(()),
             pltpu.VMEM(part, F32),
             pltpu.VMEM((grid_rows,) + part, F32),
             pltpu.VMEM((grid_columns,) + part, F32),
@@ -730,10 +753,13 @@
         ),
         cost_estimate=cost(12),
         name="total",
-    )(first, second, third)
-
-
-def finish_kernel(weight, count_ref, total_ref, field_ref, second_ref, third_ref, basis_ref, hess_ref):
+    )(first, second, solved, pos)
+
+
+def finish_kernel(
+    weight, count_ref, total_ref, field_ref, second_ref, third_ref, basis_hbm, hess_ref,
+    basis_ref, sems,
+):
     width = field_ref.shape[1]
     gram = jnp.sum(total_ref[...], axis=1, keepdims=True) * weight
     ff, ft, tt, fu, tu, uu = (gram[index : index + 1, :] for index in range(6))
@@ -753,12 +779,20 @@
     )
     k2 = k1 / h21
 
-    alive = live_lanes(count_ref[0], pl.program_id(0) * width, width)
-    f = field_ref[...] * alive
-    t, u = second_ref[...], third_ref[...]
-    basis_ref[0] = f * (1.0 / beta)
-    basis_ref[1] = t * k1 + f * (p * k1)
-    basis_ref[2] = u * k2 + t * (q * k2) + f * (w * k2)
+    alive = live_lanes(count_ref[0], 0, width)
+    copies = []
+    for first in range(0, UNK, SLAB):
+        rows = pl.ds(first, SLAB)
+        f = field_ref[rows, :] * alive
+        t, u = second_ref[rows, :], third_ref[rows, :]
+        basis_ref[0, rows, :] = f * (1.0 / beta)
+        basis_ref[1, rows, :] = t * k1 + f * (p * k1)
+        basis_ref[2, rows, :] = u * k2 + t * (q * k2) + f * (w * k2)
+        at = (slice(None), rows, slice(None))
+        copies.append(
+            pltpu.make_async_copy(basis_ref.at[at], basis_hbm.at[at], sems.at[first // SLAB])
+        )
+        copies[-1].start()
 
     at_row = lax.broadcasted_iota(I32, (2, 3), 1)
     at_column = lax.broadcasted_iota(I32, (2, 3), 0)
@@ -766,28 +800,24 @@
     for i, j, value in ((0, 0, h00), (1, 0, h10), (0, 1, h01), (1, 1, h11), (2, 1, h21)):
         hess = jnp.where(jnp.logical_and(at_row == i, at_column == j), value, hess)
     hess_ref[...] = hess
+    for copy in copies:
+        copy.wait()
 
 
 def finish(weight, part_count, total, right_side, second, third):
     elements = right_side.shape[1]
-    width = 256
-    field = pl.BlockSpec((UNK, width), lambda i: (0, i))
     return pl.pallas_call(
         functools.partial(finish_kernel, weight),
-        grid=(elements // width,),
         out_shape=(
             jax.ShapeDtypeStruct((3, UNK, elements), F32),
             jax.ShapeDtypeStruct((2, 3), F32),
         ),
-        in_specs=[
-            pl.BlockSpec(memory_space=pltpu.SMEM),
-            pl.BlockSpec((8, LANES), lambda i: (0, 0)),
-            field, field, field,
+        in_specs=[SMEM] + [VMEM] * 4,
+        out_specs=(HBM, VMEM),
+        scratch_shapes=[
+            pltpu.VMEM((3, UNK, elements), F32),
+            pltpu.SemaphoreType.DMA((UNK // SLAB,)),
         ],
-        out_specs=(
-            pl.BlockSpec((3, UNK, width), lambda i: (0, 0, i)),
-            pl.BlockSpec((2, 3), lambda i: (0, 0)),
-        ),
         compiler_params=pltpu.CompilerParams(vmem_limit_bytes=12 * MIB),
         name="finish",
     )(part_count, total, right_side, second, third)
@@ -823,10 +853,10 @@
             normal, boundary_metric_quotient, classes,
         )
 
-    second = operator_image(first_table)
-    (second_table,) = exchange(second, selector, lists)
-    third = operator_image(second_table)
-    total, second_columns, third_columns = total_over_devices(first, second, third)
+    solved = operator_image(first_table)
+    second_table, second = exchange(solved, selector, lists, pos=pos)
+    solved = operator_image(second_table)
+    total, second_columns, third_columns = total_over_devices(first, second, solved, pos)
     basis, hess = finish(weight, part_count, total, right_side, second_columns, third_columns)
     return (basis, hess.T)
 

time: 91.3 us -> 88.3 us (0.967)
  Pallas kernels: 87.7 us -> 84.6 us
    pallas_call x3, Pallas kernels: 42.5 us -> 36.5 us  [the longest x2 34 us: image(): pl.pallas_call(image_kernel, out_shape=jax.ShapeDtypeStruct((slots, LANES...]
    pallas_call x2, Pallas kernels: 26.2 us -> 28.2 us  [exchange(): pl.pallas_call(functools.partial(exchange_kernel, lax.axis_size('prow'),...]
where the time goes in v5:
time: 88.3 us; the launch traced here: 88.1 us
  Pallas kernels  84.6 us (96%)
  local copies, waits for them, and re-layouts  1.94 us (2%)
  between operations  1.6 us (2%)
    pallas_call x2, Pallas kernels, image(): pl.pallas_call(image_kernel, out_shape=jax.ShapeDtypeStruct((slots, LANES...  34 us
    pallas_call x2, Pallas kernels, exchange(): pl.pallas_call(functools.partial(exchange_kernel, lax.axis_size('prow'),...  28.2 us
    pallas_call x1, Pallas kernels, total_over_devices(): pl.pallas_call(functools.partial(total_kernel, grid_rows, grid_columns),...  18.1 us
    pallas_call x1, Pallas kernels, finish(): pl.pallas_call(functools.partial(finish_kernel, weight), out_shape=(jax.S...  2.53 us
    unnamed x18, local copies, waits for them, and re-layouts  1.94 us

profile of v5, /device:TPU:1, one launch (start us, length us, event | category | flops | bytes accessed | tf_op | source)
XLA Modules:
  0.0 88.1 jit_solution(3274743598130782785)
XLA Ops:
  0.6 0.0 copy-start.8
  1.3 0.0 copy-start
  1.3 1.2 %copy-done = f32[120,2048]{1,0:T(8,128)S(1)} copy-done((f32[120,2048]{1,0:T(8,128)S(1)}, f32[120,2048]{1,0:T(8,128)}, u32[]{:S(2)}) %copy-start) | copy-done | bytes 983064
  2.5 0.0 copy-start.7
  2.5 0.7 copy-done.7
  3.2 0.0 copy-start.2
  3.2 0.0 copy-start.5
  3.2 0.0 copy-start.6
  3.2 0.4 first_rows.1
  3.7 0.0 copy-start.3
  3.7 0.0 copy-start.4
  3.7 15.9 %exchange_first.1 = (f32[11264,128]{1,0:T(8,128)S(1)}, bf16[256,128,128]{2,1,0:T(8,128)(2,1)}) custom-call(f32[2048,128]{1,0:T(8,128)S(1)} %get-tuple-element.20.refs_0_.first_ref, bf16[256,256]{1,0:T(8,128)(2,1)S(1)} %get-tuple-element.21.refs_1_.refs_2_, s32[3072]{0:T(1024)S(1)} %bitcast.25, bf16[120,120,256]{2,1,0:T(8,128)(2,1)} %bitcast.32), custom_call_target="tpu_custom_call" | custom-call | bytes 42000000 | tf_op jit(solution)/shard_map/exchange_first/pallas_call | solution.py:434
  19.6 0.0 copy-done.8
  19.6 0.0 copy-done.2
  19.6 0.0 copy-done.5
  19.6 0.0 copy-done.6
  19.7 1.3 %prepare.1 = (s32[16,128]{1,0:T(8,128)S(1)}, s32[8,128]{1,0:T(8,128)S(1)}, s32[64,128]{1,0:T(8,128)S(1)}, bf16[128,256]{1,0:T(8,128)(2,1)S(1)}, bf16[128,256]{1,0:T(8,128)(2,1)S(1)}, /*index=5*/f32[3,64,128]{2,1,0:T(8,128)S(1)}) custom-call(f32[11264,128]{1,0:T(8,128)S(1)} %get-tuple-element.23._.table_ref, s32[16,128]{1,0:T(8,128)S(1)} %bitcast.31, ...), custom_call_target="tpu_custom_call" | custom-call | bytes 9000000 | tf_op jit(solution)/shard_map/prepare/pallas_call | solution.py:196
  21.0 0.0 copy-done.3
  21.0 0.0 copy-done.4
  21.0 17.0 %image.2.refs_0_ = f32[6144,128]{1,0:T(8,128)S(1)} custom-call(s32[1]{0:T(128)S(6)} %copy.12.count_ref, s32[8192]{0:T(1024)S(1)} %bitcast.19, s32[2048]{0:T(1024)S(1)} %bitcast.21, s32[1024]{0:T(1024)S(1)} %bitcast.28, f32[11264,128]{1,0:T(8,128)S(1)} %get-tuple-element.23._.table_ref, bf16[128,256]{1,0:T(8,128)(2,1)S(1)} %get-tuple-element.27.lift_hi_ref, ...), custom_call_target="tpu_custom_call" | custom-call | bytes 60000000 | tf_op jit(solution)/shard_map/image/pallas_call | solution.py:608
  38.0 12.3 %exchange.1 = (f32[11264,128]{1,0:T(8,128)S(1)}, f32[2048,128]{1,0:T(8,128)S(1)}) custom-call(f32[6144,128]{1,0:T(8,128)S(1)} %image.2.refs_0_, s32[2048]{0:T(1024)S(1)} %bitcast.22, bf16[256,256]{1,0:T(8,128)(2,1)S(1)} %get-tuple-element.21.refs_1_.refs_2_, s32[3072]{0:T(1024)S(1)} %bitcast.26), custom_call_target="tpu_custom_call" | custom-call | bytes 42000000 | tf_op jit(solution)/shard_map/exchange/pallas_call | solution.py:434
  50.3 17.0 %image.3.solved_ref = f32[6144,128]{1,0:T(8,128)S(1)} custom-call(s32[1]{0:T(128)S(6)} %copy.12.count_ref, s32[8192]{0:T(1024)S(1)} %bitcast.20, s32[2048]{0:T(1024)S(1)} %bitcast.23, s32[1024]{0:T(1024)S(1)} %bitcast.29, f32[11264,128]{1,0:T(8,128)S(1)} %get-tuple-element.32.table_ref, bf16[128,256]{1,0:T(8,128)(2,1)S(1)} %get-tuple-element.27.lift_hi_ref, ...), custom_call_target="tpu_custom_call" | custom-call | bytes 60000000 | tf_op jit(solution)/shard_map/image/pallas_call | solution.py:608
  67.3 0.0 copy-start.1
  67.3 18.1 %total.1 = (f32[8,128]{1,0:T(8,128)S(1)}, f32[120,2048]{1,0:T(8,128)S(1)}, f32[120,2048]{1,0:T(8,128)S(1)}) custom-call(f32[2048,128]{1,0:T(8,128)S(1)} %get-tuple-element.20.refs_0_.first_ref, f32[2048,128]{1,0:T(8,128)S(1)} %get-tuple-element.31.second_ref, f32[6144,128]{1,0:T(8,128)S(1)} %image.3.solved_ref, s32[2048]{0:T(1024)S(1)} %bitcast.24), custom_call_target="tpu_custom_call" | custom-call | bytes 36000000 | tf_op jit(solution)/shard_map/total/pallas_call | solution.py:730
  85.4 0.0 copy-done.1
  85.4 2.5 %finish.1 = (f32[3,120,2048]{2,1,0:T(8,128)}, f32[2,3]{1,0:T(2,128)}) custom-call(s32[1]{0:T(128)S(6)} %copy.12.count_ref, f32[8,128]{1,0:T(8,128)S(1)} %get-tuple-element.33.total_ref, f32[120,2048]{1,0:T(8,128)S(1)} %copy-done.1, f32[120,2048]{1,0:T(8,128)S(1)} %get-tuple-element.34.second_ref, f32[120,2048]{1,0:T(8,128)S(1)} %get-tuple-element.35.third_ref), custom_call_target="tpu_custom_call" | custom-call | tf_op jit(solution)/shard_map/finish/pallas_call | solution.py:809
Async XLA Ops:
  0.6 19.0 %copy-start.8 = (s32[2048]{0:T(1024)S(1)}, s32[2048]{0:T(1024)}, u32[]{:S(2)}) copy-start(s32[2048]{0:T(1024)} %param.12) | copy-start | bytes 24580
  1.3 1.2 %copy-start = (f32[120,2048]{1,0:T(8,128)S(1)}, f32[120,2048]{1,0:T(8,128)}, u32[]{:S(2)}) copy-start(f32[120,2048]{1,0:T(8,128)} %field_ref.3) | copy-start | bytes 2949124
  2.5 0.7 copy-start.7
  3.2 16.4 %copy-start.2 = (s32[8192]{0:T(1024)S(1)}, s32[8192]{0:T(1024)}, u32[]{:S(2)}) copy-start(s32[8192]{0:T(1024)} %param.13) | copy-start | bytes 98308
  3.2 16.4 %copy-start.5 = (f32[3,8192]{1,0:T(4,128)S(1)}, f32[3,8192]{1,0:T(4,128)}, u32[]{:S(2)}) copy-start(f32[3,8192]{1,0:T(4,128)} %normal_ref.1) | copy-start | bytes 294916
  3.2 16.4 %copy-start.6 = (f32[4,20,10]{1,0,2:T(4,128)S(1)}, f32[4,20,10]{1,0,2:T(4,128)}, u32[]{:S(2)}) copy-start(f32[4,20,10]{1,0,2:T(4,128)} %param.18) | copy-start | bytes 9604
  3.7 17.3 %copy-start.3 = (s32[8192]{0:T(1024)S(1)}, s32[8192]{0:T(1024)}, u32[]{:S(2)}) copy-start(s32[8192]{0:T(1024)} %param.14) | copy-start | bytes 98308
  3.7 17.3 %copy-start.4 = (f32[8192]{0:T(1024)S(1)}, f32[8192]{0:T(1024)}, u32[]{:S(2)}) copy-start(f32[8192]{0:T(1024)} %param.16) | copy-start | bytes 98308
  67.3 18.1 %copy-start.1 = (f32[120,2048]{1,0:T(8,128)S(1)}, f32[120,2048]{1,0:T(8,128)}, u32[]{:S(2)}) copy-start(f32[120,2048]{1,0:T(8,128)} %field_ref.3) | copy-start | bytes 2949124

commit v6 on v5

--- a/solution.py
+++ b/solution.py
@@ -215,24 +215,39 @@
     )
 
 
-def write_traces(rows_ref, selector_ref, table_ref, first):
+def trace_block(rows_ref, selector_ref, table_ref, first, index):
     elements = rows_ref.shape[0]
     width = 2 * LANES
     left = lax.broadcasted_iota(I32, (width, LANES), 1) < HALF
-
+    base = pl.multiple_of(index * width, width)
+    high, low = split(rows_ref[pl.ds(base, width), :])
+    traces = dot(jnp.concatenate([high, low], axis=1), selector_ref[...])
+    for pair in range(2):
+        both = traces[:, pair * LANES : (pair + 1) * LANES]
+        swapped = pltpu.roll(both, HALF, 1)
+        even, odd = first + 2 * pair * elements, first + (2 * pair + 1) * elements
+        table_ref[pl.ds(even + base, width), :] = jnp.where(left, both, swapped)
+        table_ref[pl.ds(odd + base, width), :] = jnp.where(left, swapped, both)
+
+
+def write_traces(rows_ref, selector_ref, table_ref, first):
     def block(index, carry):
-        base = pl.multiple_of(index * width, width)
-        high, low = split(rows_ref[pl.ds(base, width), :])
-        traces = dot(jnp.concatenate([high, low], axis=1), selector_ref[...])
-        for pair in range(2):
-            both = traces[:, pair * LANES : (pair + 1) * LANES]
-            swapped = pltpu.roll(both, HALF, 1)
-            even, odd = first + 2 * pair * elements, first + (2 * pair + 1) * elements
-            table_ref[pl.ds(even + base, width), :] = jnp.where(left, both, swapped)
-            table_ref[pl.ds(odd + base, width), :] = jnp.where(left, swapped, both)
+        trace_block(rows_ref, selector_ref, table_ref, first, index)
         return carry
 
-    lax.fori_loop(0, elements // width, block, 0, unroll=4)
+    lax.fori_loop(0, rows_ref.shape[0] // (2 * LANES), block, 0, unroll=4)
+
+
+def staggered(count, before, after):
+    before(0)
+
+    def body(index, carry):
+        after(index - 1)
+        before(index)
+        return carry
+
+    lax.fori_loop(1, count, body, 0)
+    after(count - 1)
 
 
 def gather_pairs(table_ref, index_ref, out_ref, first_a, first_b, offset, count, unroll):
@@ -250,7 +265,7 @@
 
 
 def element_order(solved_ref, pos_ref, rows_ref):
-    unroll = 32
+    unroll = 64
 
     def fetch(index, carry):
         base = pl.multiple_of(index * unroll, unroll)
@@ -517,17 +532,21 @@
     chunks = blocks // 8
 
     index_copy.wait()
-    gather_pairs(table_ref, index_ref, picked_ref, 0, 2 * elements, 0, 2 * elements, 64)
-
-    def transpose(index, carry):
-        for step in range(4):
-            block = index * 4 + step
-            rows = pl.ds(pl.multiple_of(block * LANES, LANES), LANES)
-            target = pl.multiple_of(block * NODE_PITCH, 8)
-            node_ref[pl.ds(target, LANES), :] = picked_ref[rows, :].T
-        return carry
-
-    lax.fori_loop(0, 2 * blocks // 4, transpose, 0)
+    left = lax.broadcasted_iota(I32, (1, LANES), 1) < HALF
+
+    def gather(index):
+        base = pl.multiple_of(index * LANES, LANES)
+        for step in range(LANES):
+            row_a = table_ref[pl.ds(index_ref[base + step], 1), :]
+            row_b = table_ref[pl.ds(index_ref[2 * elements + base + step], 1), :]
+            picked_ref[pl.ds(base + step, 1), :] = jnp.where(left, row_a, row_b)
+
+    def transpose(index):
+        rows = pl.ds(pl.multiple_of(index * LANES, LANES), LANES)
+        target = pl.multiple_of(index * NODE_PITCH, 8)
+        node_ref[pl.ds(target, LANES), :] = picked_ref[rows, :].T
+
+    staggered(2 * blocks, gather, transpose)
 
     for block in range(blocks):
         for side in range(4):
@@ -573,9 +592,9 @@
         coupled_ref[pl.ds(base, 2 * LANES), :] = coupled.T
         return carry
 
-    lax.fori_loop(0, blocks // 2, lift, 0, unroll=4)
-
-    unroll = 16
+    lax.fori_loop(0, blocks // 2, lift, 0, unroll=8)
+
+    unroll = 64
     pos_copy.wait()
     tile_copy.wait()
 
@@ -586,16 +605,20 @@
         return carry
 
     lax.fori_loop(0, elements // unroll, place, 0)
-
     class_copy.wait()
 
     def solve(index, carry):
-        for step in range(GROUP):
+        for step in range(0, GROUP, 2):
             tile = index * GROUP + step
-            base = pl.multiple_of(tile * TILE, TILE)
-            high, low = split(sorted_ref[pl.ds(base, TILE), :])
-            result = dot(jnp.concatenate([high, low], axis=0), class_ref[tile_ref[tile]])
-            solved_ref[pl.ds(base, TILE), :] = result[:TILE] + result[TILE:]
+            base = pl.multiple_of(tile * TILE, 2 * TILE)
+            high, low = split(sorted_ref[pl.ds(base, 2 * TILE), :])
+            pair = jnp.concatenate(
+                [class_ref[tile_ref[tile]], class_ref[tile_ref[tile + 1]]], axis=1
+            )
+            result = dot(jnp.concatenate([high, low], axis=0), pair)
+            result = result[: 2 * TILE] + result[2 * TILE :]
+            solved_ref[pl.ds(base, TILE), :] = result[:TILE, :LANES]
+            solved_ref[pl.ds(base + TILE, TILE), :] = result[TILE:, LANES:]
         return carry
 
     lax.fori_loop(0, (tile_ref[4 * LANES] + (GROUP - 1)) // GROUP, solve, 0)
@@ -649,9 +672,12 @@
 
     zero = jnp.zeros((8, LANES), F32)
     sums = lax.fori_loop(0, elements // LANES, block, (zero,) * 6)
+    lane = lax.broadcasted_iota(I32, (1, LANES), 1)
+    row = jnp.zeros((1, LANES), F32)
     for index in range(6):
-        gram_ref[index : index + 1, :] = jnp.sum(sums[index], axis=0, keepdims=True)
-    gram_ref[6:, :] = jnp.zeros((2, LANES), F32)
+        value = jnp.sum(jnp.sum(sums[index], axis=0, keepdims=True), axis=1, keepdims=True)
+        row = jnp.where(lane == index, value, row)
+    gram_ref[...] = row
 
 
 def total_kernel(grid_rows, grid_columns, first_ref, second_ref, solved_ref, pos_any,
@@ -726,7 +752,7 @@
 
 def total_over_devices(first, second, solved, pos):
     grid_rows, grid_columns = lax.axis_size("prow"), lax.axis_size("pcol")
-    part = (8, LANES)
+    part = (1, LANES)
     return pl.pallas_call(
         functools.partial(total_kernel, grid_rows, grid_columns),
         out_shape=(
@@ -761,8 +787,8 @@
     basis_ref, sems,
 ):
     width = field_ref.shape[1]
-    gram = jnp.sum(total_ref[...], axis=1, keepdims=True) * weight
-    ff, ft, tt, fu, tu, uu = (gram[index : index + 1, :] for index in range(6))
+    gram = total_ref[...] * weight
+    ff, ft, tt, fu, tu, uu = (gram[:, index : index + 1] for index in range(6))
     beta = jnp.sqrt(ff + EPSILON)
     square = beta * beta
     h00 = (ff + ft) / square

time: 88.3 us -> 82.9 us (0.939)
  Pallas kernels: 84.6 us -> 79 us
    pallas_call x2, Pallas kernels: 34 us -> 28 us  [image(): pl.pallas_call(image_kernel, out_shape=jax.ShapeDtypeStruct((slots, LANES...]
where the time goes in v6:
time: 82.9 us; the launch traced here: 82.6 us
  Pallas kernels  79 us (95%)
  local copies, waits for them, and re-layouts  1.94 us (2%)
  between operations  1.6 us (2%)
    pallas_call x2, Pallas kernels, exchange(): pl.pallas_call(functools.partial(exchange_kernel, lax.axis_size('prow'),...  28.1 us
    pallas_call x2, Pallas kernels, image(): pl.pallas_call(image_kernel, out_shape=jax.ShapeDtypeStruct((slots, LANES...  28 us
    pallas_call x1, Pallas kernels, total_over_devices(): pl.pallas_call(functools.partial(total_kernel, grid_rows, grid_columns),...  18.2 us
    pallas_call x1, Pallas kernels, finish(): pl.pallas_call(functools.partial(finish_kernel, weight), out_shape=(jax.S...  3.04 us
    unnamed x18, local copies, waits for them, and re-layouts  1.94 us

profile of v6, /device:TPU:1, one launch (start us, length us, event | category | flops | bytes accessed | tf_op | source)
XLA Modules:
  0.0 82.6 jit_solution(12407787738264265191)
XLA Ops:
  0.6 0.0 copy-start.8
  1.3 0.0 copy-start
  1.3 1.2 %copy-done = f32[120,2048]{1,0:T(8,128)S(1)} copy-done((f32[120,2048]{1,0:T(8,128)S(1)}, f32[120,2048]{1,0:T(8,128)}, u32[]{:S(2)}) %copy-start) | copy-done | bytes 983064
  2.5 0.0 copy-start.7
  2.5 0.7 copy-done.7
  3.2 0.0 copy-start.2
  3.2 0.0 copy-start.5
  3.2 0.0 copy-start.6
  3.2 0.4 first_rows.1
  3.7 0.0 copy-start.3
  3.7 0.0 copy-start.4
  3.7 15.9 %exchange_first.1 = (f32[11264,128]{1,0:T(8,128)S(1)}, bf16[256,128,128]{2,1,0:T(8,128)(2,1)}) custom-call(f32[2048,128]{1,0:T(8,128)S(1)} %get-tuple-element.20.refs_0_.first_ref, bf16[256,256]{1,0:T(8,128)(2,1)S(1)} %get-tuple-element.21.refs_1_.refs_2_, s32[3072]{0:T(1024)S(1)} %bitcast.25, bf16[120,120,256]{2,1,0:T(8,128)(2,1)} %bitcast.32), custom_call_target="tpu_custom_call" | custom-call | bytes 42000000 | tf_op jit(solution)/shard_map/exchange_first/pallas_call | solution.py:449
  19.6 0.0 copy-done.8
  19.6 0.0 copy-done.2
  19.6 0.0 copy-done.5
  19.6 0.0 copy-done.6
  19.7 1.3 %prepare.1 = (s32[16,128]{1,0:T(8,128)S(1)}, s32[8,128]{1,0:T(8,128)S(1)}, s32[64,128]{1,0:T(8,128)S(1)}, bf16[128,256]{1,0:T(8,128)(2,1)S(1)}, bf16[128,256]{1,0:T(8,128)(2,1)S(1)}, /*index=5*/f32[3,64,128]{2,1,0:T(8,128)S(1)}) custom-call(f32[11264,128]{1,0:T(8,128)S(1)} %get-tuple-element.23._.table_ref, s32[16,128]{1,0:T(8,128)S(1)} %bitcast.31, ...), custom_call_target="tpu_custom_call" | custom-call | bytes 9000000 | tf_op jit(solution)/shard_map/prepare/pallas_call | solution.py:196
  21.0 0.0 copy-done.3
  21.0 0.0 copy-done.4
  21.0 14.0 %image.2.refs_0_ = f32[6144,128]{1,0:T(8,128)S(1)} custom-call(s32[1]{0:T(128)S(6)} %copy.12.count_ref, s32[8192]{0:T(1024)S(1)} %bitcast.19, s32[2048]{0:T(1024)S(1)} %bitcast.21, s32[1024]{0:T(1024)S(1)} %bitcast.28, f32[11264,128]{1,0:T(8,128)S(1)} %get-tuple-element.23._.table_ref, bf16[128,256]{1,0:T(8,128)(2,1)S(1)} %get-tuple-element.27.lift_hi_ref, ...), custom_call_target="tpu_custom_call" | custom-call | bytes 60000000 | tf_op jit(solution)/shard_map/image/pallas_call | solution.py:631
  35.0 12.1 %exchange.1 = (f32[11264,128]{1,0:T(8,128)S(1)}, f32[2048,128]{1,0:T(8,128)S(1)}) custom-call(f32[6144,128]{1,0:T(8,128)S(1)} %image.2.refs_0_, s32[2048]{0:T(1024)S(1)} %bitcast.22, bf16[256,256]{1,0:T(8,128)(2,1)S(1)} %get-tuple-element.21.refs_1_.refs_2_, s32[3072]{0:T(1024)S(1)} %bitcast.26), custom_call_target="tpu_custom_call" | custom-call | bytes 42000000 | tf_op jit(solution)/shard_map/exchange/pallas_call | solution.py:449
  47.2 14.0 %image.3.solved_ref = f32[6144,128]{1,0:T(8,128)S(1)} custom-call(s32[1]{0:T(128)S(6)} %copy.12.count_ref, s32[8192]{0:T(1024)S(1)} %bitcast.20, s32[2048]{0:T(1024)S(1)} %bitcast.23, s32[1024]{0:T(1024)S(1)} %bitcast.29, f32[11264,128]{1,0:T(8,128)S(1)} %get-tuple-element.32.table_ref, bf16[128,256]{1,0:T(8,128)(2,1)S(1)} %get-tuple-element.27.lift_hi_ref, ...), custom_call_target="tpu_custom_call" | custom-call | bytes 60000000 | tf_op jit(solution)/shard_map/image/pallas_call | solution.py:631
  61.2 0.0 copy-start.1
  61.2 18.2 %total.1 = (f32[1,128]{1,0:T(1,128)S(1)}, f32[120,2048]{1,0:T(8,128)S(1)}, f32[120,2048]{1,0:T(8,128)S(1)}) custom-call(f32[2048,128]{1,0:T(8,128)S(1)} %get-tuple-element.20.refs_0_.first_ref, f32[2048,128]{1,0:T(8,128)S(1)} %get-tuple-element.31.second_ref, f32[6144,128]{1,0:T(8,128)S(1)} %image.3.solved_ref, s32[2048]{0:T(1024)S(1)} %bitcast.24), custom_call_target="tpu_custom_call" | custom-call | bytes 36000000 | tf_op jit(solution)/shard_map/total/pallas_call | solution.py:756
  79.4 0.0 copy-done.1
  79.4 3.0 %finish.1 = (f32[3,120,2048]{2,1,0:T(8,128)}, f32[2,3]{1,0:T(2,128)}) custom-call(s32[1]{0:T(128)S(6)} %copy.12.count_ref, f32[1,128]{1,0:T(1,128)S(1)} %get-tuple-element.33.total_ref, f32[120,2048]{1,0:T(8,128)S(1)} %copy-done.1, f32[120,2048]{1,0:T(8,128)S(1)} %get-tuple-element.34.second_ref, f32[120,2048]{1,0:T(8,128)S(1)} %get-tuple-element.35.third_ref), custom_call_target="tpu_custom_call" | custom-call | tf_op jit(solution)/shard_map/finish/pallas_call | solution.py:835
Async XLA Ops:
  0.6 19.0 %copy-start.8 = (s32[2048]{0:T(1024)S(1)}, s32[2048]{0:T(1024)}, u32[]{:S(2)}) copy-start(s32[2048]{0:T(1024)} %param.12) | copy-start | bytes 24580
  1.3 1.2 %copy-start = (f32[120,2048]{1,0:T(8,128)S(1)}, f32[120,2048]{1,0:T(8,128)}, u32[]{:S(2)}) copy-start(f32[120,2048]{1,0:T(8,128)} %field_ref.3) | copy-start | bytes 2949124
  2.5 0.7 copy-start.7
  3.2 16.4 %copy-start.2 = (s32[8192]{0:T(1024)S(1)}, s32[8192]{0:T(1024)}, u32[]{:S(2)}) copy-start(s32[8192]{0:T(1024)} %param.13) | copy-start | bytes 98308
  3.2 16.4 %copy-start.5 = (f32[3,8192]{1,0:T(4,128)S(1)}, f32[3,8192]{1,0:T(4,128)}, u32[]{:S(2)}) copy-start(f32[3,8192]{1,0:T(4,128)} %normal_ref.1) | copy-start | bytes 294916
  3.2 16.4 %copy-start.6 = (f32[4,20,10]{1,0,2:T(4,128)S(1)}, f32[4,20,10]{1,0,2:T(4,128)}, u32[]{:S(2)}) copy-start(f32[4,20,10]{1,0,2:T(4,128)} %param.18) | copy-start | bytes 9604
  3.7 17.3 %copy-start.3 = (s32[8192]{0:T(1024)S(1)}, s32[8192]{0:T(1024)}, u32[]{:S(2)}) copy-start(s32[8192]{0:T(1024)} %param.14) | copy-start | bytes 98308
  3.7 17.3 %copy-start.4 = (f32[8192]{0:T(1024)S(1)}, f32[8192]{0:T(1024)}, u32[]{:S(2)}) copy-start(f32[8192]{0:T(1024)} %param.16) | copy-start | bytes 98308
  61.2 18.2 %copy-start.1 = (f32[120,2048]{1,0:T(8,128)S(1)}, f32[120,2048]{1,0:T(8,128)}, u32[]{:S(2)}) copy-start(f32[120,2048]{1,0:T(8,128)} %field_ref.3) | copy-start | bytes 2949124

commit v7 on v6

--- a/solution.py
+++ b/solution.py
@@ -265,7 +265,7 @@
 
 
 def element_order(solved_ref, pos_ref, rows_ref):
-    unroll = 64
+    unroll = 256
 
     def fetch(index, carry):
         base = pl.multiple_of(index * unroll, unroll)
@@ -594,17 +594,10 @@
 
     lax.fori_loop(0, blocks // 2, lift, 0, unroll=8)
 
-    unroll = 64
     pos_copy.wait()
     tile_copy.wait()
-
-    def place(index, carry):
-        base = pl.multiple_of(index * unroll, unroll)
-        for step in range(unroll):
-            sorted_ref[pl.ds(pos_ref[base + step], 1), :] = coupled_ref[pl.ds(base + step, 1), :]
-        return carry
-
-    lax.fori_loop(0, elements // unroll, place, 0)
+    for row in range(elements):
+        sorted_ref[pl.ds(pos_ref[row], 1), :] = coupled_ref[row : row + 1, :]
     class_copy.wait()
 
     def solve(index, carry):
@@ -789,20 +782,21 @@
     width = field_ref.shape[1]
     gram = total_ref[...] * weight
     ff, ft, tt, fu, tu, uu = (gram[:, index : index + 1] for index in range(6))
-    beta = jnp.sqrt(ff + EPSILON)
-    square = beta * beta
-    h00 = (ff + ft) / square
-    p = (EPSILON - ft) / square
-    h10 = jnp.sqrt((tt + 2 * p * ft + p * p * ff) / square + EPSILON)
-    k1 = 1.0 / (beta * h10)
-    h01 = k1 / beta * (fu + (1 + p) * ft + p * ff)
-    h11 = k1 * k1 * (tu + (1 + p) * tt + p * ft + p * fu + p * (1 + p) * ft + p * p * ff)
+    square = ff + EPSILON
+    inverse = 1.0 / square
+    p = (EPSILON - ft) * inverse
+    h10_square = jnp.maximum(tt + 2 * p * ft + p * p * ff, 0.0) * inverse + EPSILON
+    k1_square = inverse / h10_square
+    h11 = k1_square * (tu + (1 + p) * tt + p * ft + p * fu + p * (1 + p) * ft + p * p * ff)
+    along = (fu + (1 + p) * ft + p * ff) * inverse
     q = 1 + p - h11
-    w = p * (1 - h11) - h01 * h10
-    h21 = jnp.sqrt(
-        k1 * k1 * (uu + 2 * q * tu + 2 * w * fu + q * q * tt + 2 * q * w * ft + w * w * ff)
-        + EPSILON
-    )
+    w = p * (1 - h11) - along
+    rest = uu + 2 * q * tu + 2 * w * fu + q * q * tt + 2 * q * w * ft + w * w * ff
+    h21_square = k1_square * jnp.maximum(rest, 0.0) + EPSILON
+    k0 = 1.0 / jnp.sqrt(square)
+    k1 = jnp.sqrt(k1_square)
+    h10, h21 = jnp.sqrt(h10_square), jnp.sqrt(h21_square)
+    h00, h01 = (ff + ft) * inverse, along / h10
     k2 = k1 / h21
 
     alive = live_lanes(count_ref[0], 0, width)
@@ -811,7 +805,7 @@
         rows = pl.ds(first, SLAB)
         f = field_ref[rows, :] * alive
         t, u = second_ref[rows, :], third_ref[rows, :]
-        basis_ref[0, rows, :] = f * (1.0 / beta)
+        basis_ref[0, rows, :] = f * k0
         basis_ref[1, rows, :] = t * k1 + f * (p * k1)
         basis_ref[2, rows, :] = u * k2 + t * (q * k2) + f * (w * k2)
         at = (slice(None), rows, slice(None))

time: 82.9 us -> 81.5 us (0.983)
  Pallas kernels: 79 us -> 77.6 us
where the time goes in v7:
time: 81.5 us; the launch traced here: 81.2 us
  Pallas kernels  77.6 us (95%)
  local copies, waits for them, and re-layouts  1.94 us (2%)
  between operations  1.6 us (2%)
    pallas_call x2, Pallas kernels, exchange(): pl.pallas_call(functools.partial(exchange_kernel, lax.axis_size('prow'),...  27.7 us
    pallas_call x2, Pallas kernels, image(): pl.pallas_call(image_kernel, out_shape=jax.ShapeDtypeStruct((slots, LANES...  27.3 us
    pallas_call x1, Pallas kernels, total_over_devices(): pl.pallas_call(functools.partial(total_kernel, grid_rows, grid_columns),...  17.8 us
    pallas_call x1, Pallas kernels, finish(): pl.pallas_call(functools.partial(finish_kernel, weight), out_shape=(jax.S...  3.16 us
    unnamed x18, local copies, waits for them, and re-layouts  1.94 us

profile of v7, /device:TPU:1, one launch (start us, length us, event | category | flops | bytes accessed | tf_op | source)
XLA Modules:
  0.0 81.2 jit_solution(281279322705385596)
XLA Ops:
  0.6 0.0 copy-start.8
  1.3 0.0 copy-start
  1.3 1.2 %copy-done = f32[120,2048]{1,0:T(8,128)S(1)} copy-done((f32[120,2048]{1,0:T(8,128)S(1)}, f32[120,2048]{1,0:T(8,128)}, u32[]{:S(2)}) %copy-start) | copy-done | bytes 983064
  2.5 0.0 copy-start.7
  2.5 0.7 copy-done.7
  3.2 0.0 copy-start.2
  3.2 0.0 copy-start.5
  3.2 0.0 copy-start.6
  3.2 0.4 first_rows.1
  3.7 0.0 copy-start.3
  3.7 0.0 copy-start.4
  3.7 15.9 %exchange_first.1 = (f32[11264,128]{1,0:T(8,128)S(1)}, bf16[256,128,128]{2,1,0:T(8,128)(2,1)}) custom-call(f32[2048,128]{1,0:T(8,128)S(1)} %get-tuple-element.20.refs_0_.first_ref, bf16[256,256]{1,0:T(8,128)(2,1)S(1)} %get-tuple-element.21.refs_1_.refs_2_, s32[3072]{0:T(1024)S(1)} %bitcast.25, bf16[120,120,256]{2,1,0:T(8,128)(2,1)} %bitcast.32), custom_call_target="tpu_custom_call" | custom-call | bytes 42000000 | tf_op jit(solution)/shard_map/exchange_first/pallas_call | solution.py:449
  19.6 0.0 copy-done.8
  19.6 0.0 copy-done.2
  19.6 0.0 copy-done.5
  19.6 0.0 copy-done.6
  19.7 1.3 %prepare.1 = (s32[16,128]{1,0:T(8,128)S(1)}, s32[8,128]{1,0:T(8,128)S(1)}, s32[64,128]{1,0:T(8,128)S(1)}, bf16[128,256]{1,0:T(8,128)(2,1)S(1)}, bf16[128,256]{1,0:T(8,128)(2,1)S(1)}, /*index=5*/f32[3,64,128]{2,1,0:T(8,128)S(1)}) custom-call(f32[11264,128]{1,0:T(8,128)S(1)} %get-tuple-element.23._.table_ref, s32[16,128]{1,0:T(8,128)S(1)} %bitcast.31, ...), custom_call_target="tpu_custom_call" | custom-call | bytes 9000000 | tf_op jit(solution)/shard_map/prepare/pallas_call | solution.py:196
  21.0 0.0 copy-done.3
  21.0 0.0 copy-done.4
  21.0 13.6 %image.2.refs_0_ = f32[6144,128]{1,0:T(8,128)S(1)} custom-call(s32[1]{0:T(128)S(6)} %copy.12.count_ref, s32[8192]{0:T(1024)S(1)} %bitcast.19, s32[2048]{0:T(1024)S(1)} %bitcast.21, s32[1024]{0:T(1024)S(1)} %bitcast.28, f32[11264,128]{1,0:T(8,128)S(1)} %get-tuple-element.23._.table_ref, bf16[128,256]{1,0:T(8,128)(2,1)S(1)} %get-tuple-element.27.lift_hi_ref, ...), custom_call_target="tpu_custom_call" | custom-call | bytes 60000000 | tf_op jit(solution)/shard_map/image/pallas_call | solution.py:624
  34.6 11.7 %exchange.1 = (f32[11264,128]{1,0:T(8,128)S(1)}, f32[2048,128]{1,0:T(8,128)S(1)}) custom-call(f32[6144,128]{1,0:T(8,128)S(1)} %image.2.refs_0_, s32[2048]{0:T(1024)S(1)} %bitcast.22, bf16[256,256]{1,0:T(8,128)(2,1)S(1)} %get-tuple-element.21.refs_1_.refs_2_, s32[3072]{0:T(1024)S(1)} %bitcast.26), custom_call_target="tpu_custom_call" | custom-call | bytes 42000000 | tf_op jit(solution)/shard_map/exchange/pallas_call | solution.py:449
  46.4 13.6 %image.3.solved_ref = f32[6144,128]{1,0:T(8,128)S(1)} custom-call(s32[1]{0:T(128)S(6)} %copy.12.count_ref, s32[8192]{0:T(1024)S(1)} %bitcast.20, s32[2048]{0:T(1024)S(1)} %bitcast.23, s32[1024]{0:T(1024)S(1)} %bitcast.29, f32[11264,128]{1,0:T(8,128)S(1)} %get-tuple-element.32.table_ref, bf16[128,256]{1,0:T(8,128)(2,1)S(1)} %get-tuple-element.27.lift_hi_ref, ...), custom_call_target="tpu_custom_call" | custom-call | bytes 60000000 | tf_op jit(solution)/shard_map/image/pallas_call | solution.py:624
  60.0 0.0 copy-start.1
  60.0 17.8 %total.1 = (f32[1,128]{1,0:T(1,128)S(1)}, f32[120,2048]{1,0:T(8,128)S(1)}, f32[120,2048]{1,0:T(8,128)S(1)}) custom-call(f32[2048,128]{1,0:T(8,128)S(1)} %get-tuple-element.20.refs_0_.first_ref, f32[2048,128]{1,0:T(8,128)S(1)} %get-tuple-element.31.second_ref, f32[6144,128]{1,0:T(8,128)S(1)} %image.3.solved_ref, s32[2048]{0:T(1024)S(1)} %bitcast.24), custom_call_target="tpu_custom_call" | custom-call | bytes 36000000 | tf_op jit(solution)/shard_map/total/pallas_call | solution.py:749
  77.8 0.0 copy-done.1
  77.8 3.2 %finish.1 = (f32[3,120,2048]{2,1,0:T(8,128)}, f32[2,3]{1,0:T(2,128)}) custom-call(s32[1]{0:T(128)S(6)} %copy.12.count_ref, f32[1,128]{1,0:T(1,128)S(1)} %get-tuple-element.33.total_ref, f32[120,2048]{1,0:T(8,128)S(1)} %copy-done.1, f32[120,2048]{1,0:T(8,128)S(1)} %get-tuple-element.34.second_ref, f32[120,2048]{1,0:T(8,128)S(1)} %get-tuple-element.35.third_ref), custom_call_target="tpu_custom_call" | custom-call | tf_op jit(solution)/shard_map/finish/pallas_call | solution.py:829
Async XLA Ops:
  0.6 19.0 %copy-start.8 = (s32[2048]{0:T(1024)S(1)}, s32[2048]{0:T(1024)}, u32[]{:S(2)}) copy-start(s32[2048]{0:T(1024)} %param.12) | copy-start | bytes 24580
  1.3 1.2 %copy-start = (f32[120,2048]{1,0:T(8,128)S(1)}, f32[120,2048]{1,0:T(8,128)}, u32[]{:S(2)}) copy-start(f32[120,2048]{1,0:T(8,128)} %field_ref.3) | copy-start | bytes 2949124
  2.5 0.7 copy-start.7
  3.2 16.4 %copy-start.2 = (s32[8192]{0:T(1024)S(1)}, s32[8192]{0:T(1024)}, u32[]{:S(2)}) copy-start(s32[8192]{0:T(1024)} %param.13) | copy-start | bytes 98308
  3.2 16.4 %copy-start.5 = (f32[3,8192]{1,0:T(4,128)S(1)}, f32[3,8192]{1,0:T(4,128)}, u32[]{:S(2)}) copy-start(f32[3,8192]{1,0:T(4,128)} %normal_ref.1) | copy-start | bytes 294916
  3.2 16.4 %copy-start.6 = (f32[4,20,10]{1,0,2:T(4,128)S(1)}, f32[4,20,10]{1,0,2:T(4,128)}, u32[]{:S(2)}) copy-start(f32[4,20,10]{1,0,2:T(4,128)} %param.18) | copy-start | bytes 9604
  3.7 17.3 %copy-start.3 = (s32[8192]{0:T(1024)S(1)}, s32[8192]{0:T(1024)}, u32[]{:S(2)}) copy-start(s32[8192]{0:T(1024)} %param.14) | copy-start | bytes 98308
  3.7 17.3 %copy-start.4 = (f32[8192]{0:T(1024)S(1)}, f32[8192]{0:T(1024)}, u32[]{:S(2)}) copy-start(f32[8192]{0:T(1024)} %param.16) | copy-start | bytes 98308
  60.0 17.8 %copy-start.1 = (f32[120,2048]{1,0:T(8,128)S(1)}, f32[120,2048]{1,0:T(8,128)}, u32[]{:S(2)}) copy-start(f32[120,2048]{1,0:T(8,128)} %field_ref.3) | copy-start | bytes 2949124

commit v8 on v7

--- a/solution.py
+++ b/solution.py
@@ -276,6 +276,29 @@
     lax.fori_loop(0, rows_ref.shape[0] // unroll, fetch, 0)
 
 
+def inner_partials(refs, pairs_of, lanes, turned):
+    elements = refs[0].shape[0]
+    source, target = turned
+
+    def block(index, sums):
+        rows = pl.ds(pl.multiple_of(index * LANES, LANES), LANES)
+        values = [ref[rows, :] for ref in refs]
+        target[:, rows] = values[source].T[:UNK]
+        return tuple(
+            total + jnp.sum(pair.reshape(LANES // 8, 8, LANES), axis=0)
+            for total, pair in zip(sums, pairs_of(*values))
+        )
+
+    zero = jnp.zeros((8, LANES), F32)
+    sums = lax.fori_loop(0, elements // LANES, block, (zero,) * len(lanes))
+    lane = lax.broadcasted_iota(I32, (1, LANES), 1)
+    row = jnp.zeros((1, LANES), F32)
+    for index, value in zip(lanes, sums):
+        value = jnp.sum(jnp.sum(value, axis=0, keepdims=True), axis=1, keepdims=True)
+        row = jnp.where(lane == index, value, row)
+    return row
+
+
 def class_major(native_ref, turned_ref, stage_ref, part_ref, class_hbm, sems):
     for half in range(2):
         for row in range(CHUNK):
@@ -323,8 +346,8 @@
         native_copy = pltpu.make_async_copy(native_hbm, native_ref, native_sem)
         native_copy.start()
     else:
-        (solved_ref, pos_any, selector_ref, list_any, table_ref, rows_ref,
-         list_ref, outgoing_ref, received_ref, local_sem, send_sem, recv_sem,
+        (solved_ref, first_ref, pos_any, selector_ref, list_any,
+         table_ref, rows_ref, columns_ref, part_ref, list_ref, outgoing_ref, received_ref, local_sem, send_sem, recv_sem,
          pos_ref, pos_sem) = refs
         pos_copy = pltpu.make_async_copy(pos_any, pos_ref, pos_sem)
         pos_copy.start()
@@ -394,6 +417,10 @@
     if with_classes:
         native_copy.wait()
         stores = class_major(native_ref, turned_ref, stage_ref, part_ref, class_hbm, part_sems)
+    else:
+        part_ref[...] = inner_partials(
+            (first_ref, rows_ref), lambda f, t: (f * f, f * t, t * t), (0, 1, 2), (1, columns_ref)
+        )
 
     left = lax.broadcasted_iota(I32, (slots, LANES), 1) < HALF
     for index in (1, 6, 3, 4, 0, 2, 5, 7):
@@ -416,7 +443,7 @@
             store.wait()
 
 
-def exchange(rows, selector, lists, native=None, pos=None):
+def exchange(rows, selector, lists, native=None, first=None, pos=None):
     slots = lists.shape[0] // 16
     with_classes = native is not None
     elements = rows.shape[0] if with_classes else pos.shape[0]
@@ -442,9 +469,13 @@
             pltpu.SemaphoreType.DMA((2,)),
         ]
     else:
-        operands = [rows, pos, selector, lists]
-        in_specs, out_specs = [VMEM, ANY, VMEM, ANY], (VMEM, VMEM)
-        out_shape.append(jax.ShapeDtypeStruct((elements, LANES), F32))
+        operands = [rows, first, pos, selector, lists]
+        in_specs, out_specs = [VMEM, VMEM, ANY, VMEM, ANY], (VMEM,) * 4
+        out_shape += [
+            jax.ShapeDtypeStruct((elements, LANES), F32),
+            jax.ShapeDtypeStruct((UNK, elements), F32),
+            jax.ShapeDtypeStruct((1, LANES), F32),
+        ]
         scratch += [pltpu.SMEM(pos.shape, I32), pltpu.SemaphoreType.DMA(())]
     return pl.pallas_call(
         functools.partial(
@@ -649,32 +680,8 @@
     )
 
 
-def gram_partials(first_ref, second_ref, third_ref, second_out, third_out, gram_ref):
-    elements = first_ref.shape[0]
-
-    def block(index, sums):
-        rows = pl.ds(pl.multiple_of(index * LANES, LANES), LANES)
-        f, t, u = first_ref[rows, :], second_ref[rows, :], third_ref[rows, :]
-        second_out[:, rows] = t.T[:UNK]
-        third_out[:, rows] = u.T[:UNK]
-        pairs = (f * f, f * t, t * t, f * u, t * u, u * u)
-        return tuple(
-            total + jnp.sum(pair.reshape(LANES // 8, 8, LANES), axis=0)
-            for total, pair in zip(sums, pairs)
-        )
-
-    zero = jnp.zeros((8, LANES), F32)
-    sums = lax.fori_loop(0, elements // LANES, block, (zero,) * 6)
-    lane = lax.broadcasted_iota(I32, (1, LANES), 1)
-    row = jnp.zeros((1, LANES), F32)
-    for index in range(6):
-        value = jnp.sum(jnp.sum(sums[index], axis=0, keepdims=True), axis=1, keepdims=True)
-        row = jnp.where(lane == index, value, row)
-    gram_ref[...] = row
-
-
-def total_kernel(grid_rows, grid_columns, first_ref, second_ref, solved_ref, pos_any,
-                 total_ref, second_out, third_out, third_ref, pos_ref, pos_sem, part_ref, over_rows, over_columns, send_row, recv_row, send_column, recv_column):
+def total_kernel(grid_rows, grid_columns, first_ref, second_ref, solved_ref, known_ref, pos_any,
+                 total_ref, columns_ref, third_ref, pos_ref, pos_sem, part_ref, over_rows, over_columns, send_row, recv_row, send_column, recv_column):
     row, column = lax.axis_index("prow"), lax.axis_index("pcol")
     pos_copy = pltpu.make_async_copy(pos_any, pos_ref, pos_sem)
     pos_copy.start()
@@ -696,7 +703,10 @@
         )
     pos_copy.wait()
     element_order(solved_ref, pos_ref, third_ref)
-    gram_partials(first_ref, second_ref, third_ref, second_out, third_out, part_ref)
+    part_ref[...] = known_ref[...] + inner_partials(
+        (first_ref, second_ref, third_ref), lambda f, t, u: (f * u, t * u, u * u), (3, 4, 5),
+        (2, columns_ref),
+    )
     pl.semaphore_wait(barrier, grid_rows + grid_columns - 2)
 
     def row_copy(step):
@@ -743,7 +753,7 @@
     wait_all(over_columns, grid_columns - 1, send_column)
 
 
-def total_over_devices(first, second, solved, pos):
+def total_over_devices(first, second, solved, known, pos):
     grid_rows, grid_columns = lax.axis_size("prow"), lax.axis_size("pcol")
     part = (1, LANES)
     return pl.pallas_call(
@@ -751,10 +761,9 @@
         out_shape=(
             jax.ShapeDtypeStruct(part, F32),
             jax.ShapeDtypeStruct((UNK, first.shape[0]), F32),
-            jax.ShapeDtypeStruct((UNK, first.shape[0]), F32),
         ),
-        in_specs=[VMEM] * 3 + [ANY],
-        out_specs=(VMEM,) * 3,
+        in_specs=[VMEM] * 4 + [ANY],
+        out_specs=(VMEM,) * 2,
         scratch_shapes=[
             pltpu.VMEM(first.shape, F32),
             pltpu.SMEM(pos.shape, I32),
@@ -772,7 +781,7 @@
         ),
         cost_estimate=cost(12),
         name="total",
-    )(first, second, solved, pos)
+    )(first, second, solved, known, pos)
 
 
 def finish_kernel(
@@ -781,7 +790,10 @@
 ):
     width = field_ref.shape[1]
     gram = total_ref[...] * weight
-    ff, ft, tt, fu, tu, uu = (gram[:, index : index + 1] for index in range(6))
+    lane = lax.broadcasted_iota(I32, gram.shape, 1)
+    ff, ft, tt, fu, tu, uu = (
+        jnp.sum(jnp.where(lane == index, gram, 0.0), axis=1, keepdims=True) for index in range(6)
+    )
     square = ff + EPSILON
     inverse = 1.0 / square
     p = (EPSILON - ft) * inverse
@@ -874,9 +886,11 @@
         )
 
     solved = operator_image(first_table)
-    second_table, second = exchange(solved, selector, lists, pos=pos)
+    second_table, second, second_columns, known = exchange(
+        solved, selector, lists, first=first, pos=pos
+    )
     solved = operator_image(second_table)
-    total, second_columns, third_columns = total_over_devices(first, second, solved, pos)
+    total, third_columns = total_over_devices(first, second, solved, known, pos)
     basis, hess = finish(weight, part_count, total, right_side, second_columns, third_columns)
     return (basis, hess.T)
 

time: 81.5 us -> 80.6 us (0.989)
  Pallas kernels: 77.6 us -> 76.5 us
where the time goes in v8:
time: 80.6 us; the launch traced here: 80.1 us
  Pallas kernels  76.5 us (95%)
  local copies, waits for them, and re-layouts  1.94 us (2%)
  between operations  1.6 us (2%)
    pallas_call x2, Pallas kernels, exchange(): pl.pallas_call(functools.partial(exchange_kernel, lax.axis_size('prow'),...  28 us
    pallas_call x2, Pallas kernels, image(): pl.pallas_call(image_kernel, out_shape=jax.ShapeDtypeStruct((slots, LANES...  26.7 us
    pallas_call x1, Pallas kernels, total_over_devices(): pl.pallas_call(functools.partial(total_kernel, grid_rows, grid_columns),...  17.7 us
    pallas_call x1, Pallas kernels, finish(): pl.pallas_call(functools.partial(finish_kernel, weight), out_shape=(jax.S...  2.43 us
    unnamed x18, local copies, waits for them, and re-layouts  1.94 us

profile of v8, /device:TPU:1, one launch (start us, length us, event | category | flops | bytes accessed | tf_op | source)
XLA Modules:
  0.0 80.1 jit_solution(13554995946224186263)
XLA Ops:
  0.6 0.0 copy-start.8
  1.3 0.0 copy-start
  1.3 1.2 %copy-done = f32[120,2048]{1,0:T(8,128)S(1)} copy-done((f32[120,2048]{1,0:T(8,128)S(1)}, f32[120,2048]{1,0:T(8,128)}, u32[]{:S(2)}) %copy-start) | copy-done | bytes 983064
  2.5 0.0 copy-start.7
  2.5 0.7 copy-done.7
  3.2 0.0 copy-start.2
  3.2 0.0 copy-start.5
  3.2 0.0 copy-start.6
  3.2 0.4 first_rows.1
  3.7 0.0 copy-start.3
  3.7 0.0 copy-start.4
  3.7 15.9 %exchange_first.1 = (f32[11264,128]{1,0:T(8,128)S(1)}, bf16[256,128,128]{2,1,0:T(8,128)(2,1)}) custom-call(f32[2048,128]{1,0:T(8,128)S(1)} %get-tuple-element.21.refs_0_.refs_1_.first_ref, bf16[256,256]{1,0:T(8,128)(2,1)S(1)} %get-tuple-element.22.refs_1_.refs_3_, s32[3072]{0:T(1024)S(1)} %bitcast.25, bf16[120,120,256]{2,1,0:T(8,128)(2,1)} %bitcast.32), custom_call_target="tpu_custom_call" | custom-call | bytes 42000000 | tf_op jit(solution)/shard_map/exchange_first/pallas_call | solution.py:480
  19.6 0.0 copy-done.8
  19.6 0.0 copy-done.2
  19.6 0.0 copy-done.5
  19.6 0.0 copy-done.6
  19.7 1.3 %prepare.1 = (s32[16,128]{1,0:T(8,128)S(1)}, s32[8,128]{1,0:T(8,128)S(1)}, s32[64,128]{1,0:T(8,128)S(1)}, bf16[128,256]{1,0:T(8,128)(2,1)S(1)}, bf16[128,256]{1,0:T(8,128)(2,1)S(1)}, /*index=5*/f32[3,64,128]{2,1,0:T(8,128)S(1)}) custom-call(f32[11264,128]{1,0:T(8,128)S(1)} %get-tuple-element.24._.table_ref, s32[16,128]{1,0:T(8,128)S(1)} %bitcast.31, ...), custom_call_target="tpu_custom_call" | custom-call | bytes 9000000 | tf_op jit(solution)/shard_map/prepare/pallas_call | solution.py:196
  21.0 0.0 copy-done.3
  21.0 0.0 copy-done.4
  21.0 13.3 %image.2.refs_0_ = f32[6144,128]{1,0:T(8,128)S(1)} custom-call(s32[1]{0:T(128)S(6)} %copy.12.count_ref, s32[8192]{0:T(1024)S(1)} %bitcast.19, s32[2048]{0:T(1024)S(1)} %bitcast.21, s32[1024]{0:T(1024)S(1)} %bitcast.28, f32[11264,128]{1,0:T(8,128)S(1)} %get-tuple-element.24._.table_ref, bf16[128,256]{1,0:T(8,128)(2,1)S(1)} %get-tuple-element.28.lift_hi_ref, ...), custom_call_target="tpu_custom_call" | custom-call | bytes 60000000 | tf_op jit(solution)/shard_map/image/pallas_call | solution.py:655
  34.3 12.1 %exchange.1 = (f32[11264,128]{1,0:T(8,128)S(1)}, f32[2048,128]{1,0:T(8,128)S(1)}, f32[120,2048]{1,0:T(8,128)S(1)}, f32[1,128]{1,0:T(1,128)S(1)}) custom-call(f32[6144,128]{1,0:T(8,128)S(1)} %image.2.refs_0_, f32[2048,128]{1,0:T(8,128)S(1)} %get-tuple-element.21.refs_0_.refs_1_.first_ref, s32[2048]{0:T(1024)S(1)} %bitcast.22, ...), custom_call_target="tpu_custom_call" | custom-call | bytes 42000000 | tf_op jit(solution)/shard_map/exchange/pallas_call | solution.py:480
  46.4 13.3 %image.3.solved_ref = f32[6144,128]{1,0:T(8,128)S(1)} custom-call(s32[1]{0:T(128)S(6)} %copy.12.count_ref, s32[8192]{0:T(1024)S(1)} %bitcast.20, s32[2048]{0:T(1024)S(1)} %bitcast.23, s32[1024]{0:T(1024)S(1)} %bitcast.29, f32[11264,128]{1,0:T(8,128)S(1)} %get-tuple-element.33.table_ref, bf16[128,256]{1,0:T(8,128)(2,1)S(1)} %get-tuple-element.28.lift_hi_ref, ...), custom_call_target="tpu_custom_call" | custom-call | bytes 60000000 | tf_op jit(solution)/shard_map/image/pallas_call | solution.py:655
  59.8 0.0 copy-start.1
  59.8 17.7 %total.1 = (f32[1,128]{1,0:T(1,128)S(1)}, f32[120,2048]{1,0:T(8,128)S(1)}) custom-call(f32[2048,128]{1,0:T(8,128)S(1)} %get-tuple-element.21.refs_0_.refs_1_.first_ref, f32[2048,128]{1,0:T(8,128)S(1)} %get-tuple-element.32.second_ref, f32[6144,128]{1,0:T(8,128)S(1)} %image.3.solved_ref, f32[1,128]{1,0:T(1,128)S(1)} %get-tuple-element.34.known_ref, ...), custom_call_target="tpu_custom_call" | custom-call | bytes 36000000 | tf_op jit(solution)/shard_map/total/pallas_call | solution.py:759
  77.5 0.0 copy-done.1
  77.5 2.4 %finish.1 = (f32[3,120,2048]{2,1,0:T(8,128)}, f32[2,3]{1,0:T(2,128)}) custom-call(s32[1]{0:T(128)S(6)} %copy.12.count_ref, f32[1,128]{1,0:T(1,128)S(1)} %get-tuple-element.35.total_ref, f32[120,2048]{1,0:T(8,128)S(1)} %copy-done.1, f32[120,2048]{1,0:T(8,128)S(1)} %get-tuple-element.36.second_ref, f32[120,2048]{1,0:T(8,128)S(1)} %get-tuple-element.37.third_ref), custom_call_target="tpu_custom_call" | custom-call | tf_op jit(solution)/shard_map/finish/pallas_call | solution.py:841
Async XLA Ops:
  0.6 19.0 %copy-start.8 = (s32[2048]{0:T(1024)S(1)}, s32[2048]{0:T(1024)}, u32[]{:S(2)}) copy-start(s32[2048]{0:T(1024)} %param.12) | copy-start | bytes 24580
  1.3 1.2 %copy-start = (f32[120,2048]{1,0:T(8,128)S(1)}, f32[120,2048]{1,0:T(8,128)}, u32[]{:S(2)}) copy-start(f32[120,2048]{1,0:T(8,128)} %field_ref.3) | copy-start | bytes 2949124
  2.5 0.7 copy-start.7
  3.2 16.4 %copy-start.2 = (s32[8192]{0:T(1024)S(1)}, s32[8192]{0:T(1024)}, u32[]{:S(2)}) copy-start(s32[8192]{0:T(1024)} %param.13) | copy-start | bytes 98308
  3.2 16.4 %copy-start.5 = (f32[3,8192]{1,0:T(4,128)S(1)}, f32[3,8192]{1,0:T(4,128)}, u32[]{:S(2)}) copy-start(f32[3,8192]{1,0:T(4,128)} %normal_ref.1) | copy-start | bytes 294916
  3.2 16.4 %copy-start.6 = (f32[4,20,10]{1,0,2:T(4,128)S(1)}, f32[4,20,10]{1,0,2:T(4,128)}, u32[]{:S(2)}) copy-start(f32[4,20,10]{1,0,2:T(4,128)} %param.18) | copy-start | bytes 9604
  3.7 17.3 %copy-start.3 = (s32[8192]{0:T(1024)S(1)}, s32[8192]{0:T(1024)}, u32[]{:S(2)}) copy-start(s32[8192]{0:T(1024)} %param.14) | copy-start | bytes 98308
  3.7 17.3 %copy-start.4 = (f32[8192]{0:T(1024)S(1)}, f32[8192]{0:T(1024)}, u32[]{:S(2)}) copy-start(f32[8192]{0:T(1024)} %param.16) | copy-start | bytes 98308
  59.8 17.7 %copy-start.1 = (f32[120,2048]{1,0:T(8,128)S(1)}, f32[120,2048]{1,0:T(8,128)}, u32[]{:S(2)}) copy-start(f32[120,2048]{1,0:T(8,128)} %field_ref.3) | copy-start | bytes 2949124
